TPU v7x, 32 devices: a whole 2x2x4 slice. The times are simulated.
32 devices in a mesh: groups: 2 (over y), patch: 8 (over z, x), uly: 2 (over core).
Axes of the slice: x: 2, y: 2, z: 4, core: 2. Of those that a mesh axis runs over, the one named last changes fastest.
Arguments:
- fresh_qkv: bfloat16 [1280, 3, 2560], P(('groups', 'patch', 'uly')), parts along dimension 0, may hold values from -40 to 40
- stale_kv: bfloat16 [1280, 2, 2560], P(('groups', 'patch'), None, 'uly'), parts along dimension 0, may hold values from -40 to 40
- q_gain: float32 [2560], replicated, may hold values from 0.5 to 1.5
- k_gain: float32 [2560], replicated, may hold values from 2 to 4
Outputs:
- attended: bfloat16 [1280, 2560], P(('groups', 'patch', 'uly')), parts along dimension 0
There are 2 independent parts, one for each index of `groups`. A program takes and returns all parts, laid end to end along the dimension named above; an argument that names none is the same for every part. Nothing has to cross between parts.
All inputs are finite; a program needn't handle non-finite values.
Results may differ from a plain program's by a relative error of at most 0.0074.
Values may be sent and summed in bfloat16 or wider, within the bound.
No kernel may reach another device: no remote copies, remote signals or barrier semaphores. Data moves between devices by JAX's collectives and lax.ppermute only.
A program may use at most 128 MiB of HBM per device.

v0:
```python
import math

import jax
import jax.numpy as jnp
from jax import lax
from jax.sharding import PartitionSpec as P

HD = 128


EPSILON = 1e-06
NEGATIVE = -1e30


def normalise(features, gain, mean_square):
    return (features * lax.rsqrt(mean_square + EPSILON)[:, None] * gain).astype(jnp.bfloat16)


def accumulate(running, query_heads, key_heads, value_heads, usable):
    best, weight_sum, summed = running
    scores = jnp.einsum("qhd,khd->hqk", query_heads, key_heads, preferred_element_type=jnp.float32)
    scores = jnp.where(usable[None, None, :], scores * (1.0 / math.sqrt(HD)), NEGATIVE)
    new_best = jnp.maximum(best, jnp.max(scores, axis=-1))
    weights = jnp.where(usable[None, None, :], jnp.exp(scores - new_best[..., None]), 0.0)
    shrink = jnp.exp(best - new_best)
    product = jnp.einsum(
        "hqk,khd->hqd",
        weights.astype(jnp.bfloat16),
        value_heads,
        preferred_element_type=jnp.float32,
    )
    return (new_best, jnp.sum(weights, axis=-1), product)


def shards(fresh_qkv, stale_kv, q_gain, k_gain):
    head_width = stale_kv.shape[2]
    heads_dev = head_width // HD
    as_float = fresh_qkv[:, :2].astype(jnp.float32)
    query_rows = normalise(
        as_float[:, 0], q_gain, jnp.mean(as_float[:, 0] * as_float[:, 0], axis=-1)
    )
    key_rows = normalise(as_float[:, 1], k_gain, jnp.mean(as_float[:, 1] * as_float[:, 1], axis=-1))
    packed = jnp.stack([query_rows, key_rows, fresh_qkv[:, 2]], axis=1)
    head_major = lax.all_to_all(packed, "uly", split_axis=2, concat_axis=0, tiled=True)
    queries = head_major[:, 0]
    fresh_keys = head_major[:, 1]
    patch_rows = head_major.shape[0]
    fresh_values = head_major[:, 2]
    query_heads = queries.reshape(patch_rows, heads_dev, HD)
    own_first = lax.axis_index("patch") * patch_rows
    stale_all = lax.all_gather(stale_kv, "patch", axis=0, tiled=True)
    all_keys = lax.dynamic_update_slice_in_dim(stale_all[:, 0], fresh_keys, own_first, 0)
    all_values = lax.dynamic_update_slice_in_dim(stale_all[:, 1], fresh_values, own_first, 0)
    total_rows = all_keys.shape[0]
    starting = (
        jnp.full((heads_dev, patch_rows), NEGATIVE, jnp.float32),
        jnp.zeros((heads_dev, patch_rows), jnp.float32),
        jnp.zeros((heads_dev, patch_rows, HD), jnp.float32),
    )
    running = accumulate(
        starting,
        query_heads,
        all_keys.reshape(total_rows, heads_dev, HD),
        all_values.reshape(total_rows, heads_dev, HD),
        jnp.ones((total_rows,), jnp.bool_),
    )
    attended = running[2] / running[1][..., None]
    outgoing = attended.transpose(1, 0, 2).reshape(patch_rows, head_width).astype(jnp.bfloat16)
    return lax.all_to_all(outgoing, "uly", split_axis=0, concat_axis=1, tiled=True)


def solution(mesh):
    in_specs = (
        P(("groups", "patch", "uly"), None, None),
        P(("groups", "patch"), None, "uly"),
        P(),
        P(),
    )
    out_specs = P(("groups", "patch", "uly"), None)
    return jax.shard_map(shards, mesh=mesh, in_specs=in_specs, out_specs=out_specs, check_vma=False)
```

profile of v0, /device:TPU:0, one launch (start us, length us, event | category | flops | bytes accessed | tf_op | source)
XLA Modules:
  0.0 99.5 jit_solution(14843701146552754155)
XLA Ops:
  6.5 0.0 copy-start.5
  6.5 0.0 copy-start.4
  6.5 0.0 all-gather.2.cloned.1.call-start
  6.5 1.8 %copy.38 = bf16[80,2,1280]{2,0,1:T(8,128)(2,1)} copy(bf16[80,2,1280]{2,1,0:T(2,128)(2,1)} %param.5) | data formatting | bytes 819200 | tf_op args[1]
  8.4 0.0 slice-start
  8.4 0.0 all-gather.2.cloned.1.call-update
  8.4 1.1 %slice_convert_fusion = f32[40,2,2560]{2,0,1:T(8,128)S(1)} fusion(bf16[40,3,2560]{2,0,1:T(8,128)(2,1)} %param.4), kind=kLoop, calls=%fused_computation.16 | loop fusion | flops 204800 | bytes 1228800 | tf_op jit(solution)/shard_map/convert_element_type | solution.py:38
  9.5 0.2 multiply_reduce_fusion.2
  9.7 0.0 copy-done.5
  9.7 0.0 copy-done.4
  9.7 0.1 multiply_convert_fusion.1
  9.8 0.0 slice-done
  9.9 0.1 pad_maximum_fusion
  9.9 1.6 %copy.36 = bf16[40,3,2560]{0,1,2:T(4,128)(2,1)S(1)} copy(bf16[40,3,2560]{2,0,1:T(8,128)(2,1)S(1)} %pad_maximum_fusion) | data formatting | bytes 1228800 | tf_op jit(solution)/shard_map/stack | solution.py:43
  11.5 3.6 %reshape.54 = bf16[2,2,76800]{2,1,0:T(2,128)(2,1)} reshape(bf16[2560,3,40]{2,1,0:T(4,128)(2,1)S(1)} %bitcast.34) | data formatting | bytes 1228800
  15.2 3.5 %all-to-all-start = ((bf16[2,2,76800]{2,1,0:T(2,128)(2,1)}), bf16[2,2,76800]{2,1,0:T(2,128)(2,1)S(1)}, u32[]{:S(2)}, u32[]{:S(2)}) async-start(bf16[2,2,76800]{2,1,0:T(2,128)(2,1)} %reshape.54), calls=%async_computation | async-start | bytes 1228800 | tf_op jit(solution)/shard_map/all_to_all | solution.py:44
  18.7 1.8 %all-to-all-done = bf16[2,2,76800]{2,1,0:T(2,128)(2,1)S(1)} async-done(((bf16[2,2,76800]{2,1,0:T(2,128)(2,1)}), bf16[2,2,76800]{2,1,0:T(2,128)(2,1)S(1)}, u32[]{:S(2)}, u32[]{:S(2)}) %all-to-all-start) | async-done | bytes 614432 | tf_op jit(solution)/shard_map/all_to_all | solution.py:44
  20.5 3.3 %reshape.55 = bf16[2560,3,40]{2,1,0:T(4,128)(2,1)S(1)} reshape(bf16[2,2,76800]{2,1,0:T(2,128)(2,1)S(1)} %all-to-all-done) | data formatting | bytes 1228800
  23.8 1.4 %copy.37 = bf16[40,3,2,1280]{3,0,2,1:T(8,128)(2,1)S(1)} copy(bf16[40,3,2,1280]{0,1,3,2:T(4,128)(2,1)S(1)} %bitcast.35) | data formatting | bytes 1228800 | tf_op jit(solution)/shard_map/all_to_all | solution.py:44
  25.2 0.0 copy-start.1
  25.2 0.1 reshape_squeeze.3
  25.3 0.6 copy-done.1
  26.0 48.3 %all-gather.2.cloned.1.call-done = bf16[640,2,1280]{2,0,1:T(8,128)(2,1)} async-done(((bf16[80,2,1280]{2,0,1:T(8,128)(2,1)}), bf16[640,2,1280]{2,0,1:T(8,128)(2,1)}) %all-gather.2.cloned.1.call-update) | async-done | bytes 3276816 | tf_op jit(solution)/shard_map/all_gather | solution.py:51
  74.3 0.0 copy-start.2
  74.3 2.2 %slice_bitcast_fusion.1 = (bf16[640,1280]{1,0:T(8,128)(2,1)S(1)}, bf16[640,1280]{1,0:T(8,128)(2,1)S(1)}) fusion(bf16[640,2,1280]{2,0,1:T(8,128)(2,1)} %all-gather.2.cloned.1.call-done), kind=kLoop, calls=%fused_computation.5 | loop fusion | bytes 6553600 | tf_op jit(solution)/shard_map/squeeze | solution.py:52
  76.5 0.0 copy-done.2
  76.5 0.0 copy-start
  76.5 1.2 %copy-done = bf16[640,1280]{1,0:T(8,128)(2,1)} copy-done((bf16[640,1280]{1,0:T(8,128)(2,1)}, bf16[640,1280]{1,0:T(8,128)(2,1)S(1)}, u32[]{:S(2)}) %copy-start) | copy-done | bytes 1638424
  77.7 2.2 %copy.39 = bf16[640,1280]{0,1:T(8,128)(2,1)} copy(bf16[640,1280]{1,0:T(8,128)(2,1)S(1)} %get-tuple-element.11) | data formatting | bytes 3276800 | tf_op jit(solution)/shard_map/dynamic_update_slice | solution.py:52
  79.9 2.0 %multiply_reduce_fusion = (f32[10,80]{1,0:T(8,128)S(1)}, f32[10,80,640]{2,1,0:T(8,128)S(1)}) fusion(bf16[640,10,128]{0,2,1:T(8,128)(2,1)} %bitcast.36, bf16[80,10,128]{2,1,0:T(8,128)(2,1)S(1)} %reshape_squeeze.3), kind=kOutput, calls=%fused_computation.1 | convolution fusion | flops 132095200 | bytes 3894400 | tf_op jit(solution)/shard_map/qhd,khd->hqk/dot_general | solution.py:21
  81.9 3.6 %copy.42 = bf16[640,1280]{0,1:T(8,128)(2,1)} copy(bf16[640,1280]{1,0:T(8,128)(2,1)} %copy-done) | data formatting | bytes 3276800 | tf_op jit(solution)/shard_map/dynamic_update_slice | solution.py:53
  85.5 0.0 copy-start.3
  85.5 0.6 fusion
  86.1 0.8 copy-done.3
  86.9 0.9 fusion.3
  87.8 0.1 copy.44
  87.9 0.1 convert_element_type.26
  88.1 3.9 %all_to_all.34 = bf16[2,40,1280]{2,1,0:T(8,128)(2,1)S(1)} all-to-all(bf16[2,40,1280]{2,1,0:T(8,128)(2,1)S(1)} %convert_element_type.26), channel_id=1, replica_groups=mesh['groups'=2,'patch'=8,'uly'=2] {'uly'}, dimensions={0} | all-to-all | bytes 409600 | tf_op jit(solution)/shard_map/all_to_all | solution.py:69
  91.9 0.7 copy.48
  (4 shorter events, 0.1 us)
Async XLA Ops:
  6.5 3.2 %copy-start.5 = (f32[2560]{0:T(1024)S(1)}, f32[2560]{0:T(1024)}, u32[]{:S(2)}) copy-start(f32[2560]{0:T(1024)} %param.7) | copy-start | bytes 30724
  6.5 3.2 %copy-start.4 = (f32[2560]{0:T(1024)S(1)}, f32[2560]{0:T(1024)}, u32[]{:S(2)}) copy-start(f32[2560]{0:T(1024)} %param.6) | copy-start | bytes 30724
  6.5 67.7 %all-gather.2.cloned.1.call-start = ((), (), s32[]{:S(2)}) async-start(), calls=%async_computation.2 | async-start | bytes 3686400 | tf_op jit(solution)/shard_map/all_gather | solution.py:51
  8.4 1.5 %slice-start = ((bf16[40,3,2560]{2,0,1:T(8,128)(2,1)}), bf16[40,1,2560]{2,0,1:T(8,128)(2,1)S(1)}, s32[]{:S(2)}) async-start(bf16[40,3,2560]{2,0,1:T(8,128)(2,1)} %param.4), calls=%async_computation.3 | async-start | bytes 409600 | tf_op jit(solution)/shard_map/slice | solution.py:43
  15.2 5.3 %all-to-all-start = ((bf16[2,2,76800]{2,1,0:T(2,128)(2,1)}), bf16[2,2,76800]{2,1,0:T(2,128)(2,1)S(1)}, u32[]{:S(2)}, u32[]{:S(2)}) async-start(bf16[2,2,76800]{2,1,0:T(2,128)(2,1)} %reshape.54), calls=%async_computation | async-start | bytes 1228800 | tf_op jit(solution)/shard_map/all_to_all | solution.py:44
  25.2 0.8 copy-start.1
  74.3 2.2 %copy-start.2 = (bf16[40,3,2,1280]{3,0,2,1:T(8,128)(2,1)S(1)}, bf16[40,3,2,1280]{3,0,2,1:T(8,128)(2,1)}, u32[]{:S(2)}) copy-start(bf16[40,3,2,1280]{3,0,2,1:T(8,128)(2,1)} %copy-done.1) | copy-start | bytes 1843204
  76.5 1.2 %copy-start = (bf16[640,1280]{1,0:T(8,128)(2,1)}, bf16[640,1280]{1,0:T(8,128)(2,1)S(1)}, u32[]{:S(2)}) copy-start(bf16[640,1280]{1,0:T(8,128)(2,1)S(1)} %get-tuple-element.12) | copy-start | bytes 4915204
  85.5 1.4 %copy-start.3 = (bf16[640,1280]{0,1:T(8,128)(2,1)S(1)}, bf16[640,1280]{0,1:T(8,128)(2,1)}, u32[]{:S(2)}) copy-start(bf16[640,1280]{0,1:T(8,128)(2,1)} %copy.42) | copy-start | bytes 4915204
Sparse Core Ops, SparseCore 0:
  9.6 64.6 all-gather.1
where the time goes:
time: 99.8 us; the launch traced here: 99.5 us
  waiting for transfers between devices  50.1 us (50%)
  local copies, waits for them, and re-layouts  23.4 us (23%)
  between operations  13.6 us (14%)
  blocking collectives  3.87 us (4%)
  starting transfers between devices  3.51 us (4%)
  matrix products  2.89 us (3%)
  other arithmetic  2.11 us (2%)
    all_gather x1, waiting for transfers between devices, shards(): stale_all = lax.all_gather(stale_kv, 'patch', axis=0, tiled=True)  48.3 us
    unnamed x15, local copies, waits for them, and re-layouts  11.4 us
    all_to_all x1, blocking collectives, shards(): lax.all_to_all(outgoing, 'uly', split_axis=0, concat_axis=1, tiled=True)  3.87 us
    dynamic_update_slice x1, local copies, waits for them, and re-layouts, shards(): lax.dynamic_update_slice_in_dim(stale_all[:, 1], fresh_values, own_first, 0)  3.56 us
    all_to_all x1, starting transfers between devices, shards(): lax.all_to_all(packed, 'uly', split_axis=2, concat_axis=0, tiled=True)  3.5 us
    dynamic_update_slice x2, local copies, waits for them, and re-layouts, shards(): lax.dynamic_update_slice_in_dim(stale_all[:, 0], fresh_keys, own_first, 0)  2.28 us
    squeeze x1, local copies, waits for them, and re-layouts, shards(): stale_all[:, 0]  2.2 us
    dot_general x1, matrix products, accumulate(): jnp.einsum('qhd,khd->hqk', query_heads, key_heads, preferred_element_type...  2 us
  transfers between devices with their start and end apart: 2, of which 2 were waited for; matrix products, arithmetic and copies ran while one was open for 12% of the time, Pallas kernels for 0%

commit v1 on v0

v1 whole, which is shorter than its diff:
```python
import functools
import math

import jax
import jax.numpy as jnp
from jax import lax
from jax.experimental import pallas as pl
from jax.experimental.pallas import tpu as pltpu
from jax.sharding import PartitionSpec as P

HD = 128
EPSILON = 1e-06
SCALE = math.log2(math.e) / math.sqrt(HD)
VMEM = pl.BlockSpec(memory_space=pltpu.VMEM)
F32 = jnp.float32
BF16 = jnp.bfloat16


def call(body, outs, *args, flops=0, aliases=None):
    size = sum(a.size * a.dtype.itemsize for a in args) + sum(
        math.prod(s) * jnp.dtype(t).itemsize for s, t in outs
    )
    return pl.pallas_call(
        body,
        out_shape=[jax.ShapeDtypeStruct(s, t) for s, t in outs],
        in_specs=[VMEM] * len(args),
        out_specs=[VMEM] * len(outs),
        input_output_aliases=aliases or {},
        compiler_params=pltpu.CompilerParams(vmem_limit_bytes=32 << 20),
        cost_estimate=pl.CostEstimate(flops=flops, bytes_accessed=size, transcendentals=0),
    )(*args)


def split_kernel(x_ref, a_ref, b_ref):
    half = a_ref.shape[-1]
    for part in range(2):
        a_ref[part] = x_ref[:, part, :half]
        b_ref[part] = x_ref[:, part, half:]


def prep_kernel(x_ref, qg_ref, kg_ref, keep_ref, send_ref):
    width = keep_ref.shape[-1]
    first = lax.axis_index("uly") == 0

    def put(part, rows):
        low, high = rows[:, :width], rows[:, width:]

        @pl.when(first)
        def _():
            keep_ref[part] = low
            send_ref[part] = high

        @pl.when(jnp.logical_not(first))
        def _():
            keep_ref[part] = high
            send_ref[part] = low

    for part, gain in ((0, qg_ref), (1, kg_ref)):
        rows = x_ref[part].astype(F32)
        inverse = lax.rsqrt(jnp.mean(rows * rows, axis=-1, keepdims=True) + EPSILON)
        put(part, (rows * inverse * gain[...]).astype(BF16))
    put(2, x_ref[2])


def head_scores(query, key):
    return lax.dot_general(query, key, (((1,), (1,)), ((), ())), preferred_element_type=F32)


def both(one, two):
    return jnp.concatenate([one.astype(F32), two.astype(F32)], axis=0).astype(BF16)


def own_kernel(keep_ref, recv_ref, *outs):
    heads = outs[0].shape[-1] // HD
    for side in range(2):
        q_ref, acc_ref, ml_ref = outs[3 * side : 3 * side + 3]
        for head in range(heads):
            src = pl.ds((side * heads + head) * HD, HD)
            dst = pl.ds(head * HD, HD)
            query = both(keep_ref[0, :, src], recv_ref[0, :, src])
            key = both(keep_ref[1, :, src], recv_ref[1, :, src])
            value = both(keep_ref[2, :, src], recv_ref[2, :, src])
            q_ref[:, dst] = query
            scores = head_scores(query, key)
            best = jnp.max(scores, axis=-1, keepdims=True)
            weights = jnp.exp2((scores - best) * SCALE)
            ml_ref[0, :, head : head + 1] = best
            ml_ref[1, :, head : head + 1] = jnp.sum(weights, axis=-1, keepdims=True)
            acc_ref[:, dst] = jnp.dot(weights.astype(BF16), value, preferred_element_type=F32)


def head_update(head, q_ref, kv_refs, acc_ref, ml_ref):
    at = pl.ds(head * HD, HD)
    keys = [kv[0, :, at] for kv in kv_refs]
    values = [kv[1, :, at] for kv in kv_refs]
    key = keys[0] if len(keys) == 1 else jnp.concatenate(keys, axis=0)
    value = values[0] if len(values) == 1 else jnp.concatenate(values, axis=0)
    scores = head_scores(q_ref[:, at], key)
    old = ml_ref[0, :, head : head + 1]
    best = jnp.maximum(old, jnp.max(scores, axis=-1, keepdims=True))
    weights = jnp.exp2((scores - best) * SCALE)
    shrink = jnp.exp2((old - best) * SCALE)
    total = ml_ref[1, :, head : head + 1] * shrink + jnp.sum(weights, axis=-1, keepdims=True)
    acc = acc_ref[:, at] * shrink + jnp.dot(weights.astype(BF16), value, preferred_element_type=F32)
    return best, total, acc


def update_kernel(blocks, q_ref, *refs):
    kv_refs, (acc_ref, ml_ref, acc_out, ml_out) = refs[:blocks], refs[blocks:]
    for head in range(q_ref.shape[-1] // HD):
        best, total, acc = head_update(head, q_ref, kv_refs, acc_ref, ml_ref)
        ml_out[0, :, head : head + 1] = best
        ml_out[1, :, head : head + 1] = total
        acc_out[:, head * HD : (head + 1) * HD] = acc


def last_kernel(*refs):
    mine_ref, send_ref = refs[-2:]
    rows = mine_ref.shape[0]
    count = (len(refs) - 2) // 2
    for side in range(2):
        q_ref, acc_ref, ml_ref, *kv_refs = refs[side * count : (side + 1) * count]
        heads = q_ref.shape[-1] // HD
        for head in range(heads):
            _, total, acc = head_update(head, q_ref, kv_refs, acc_ref, ml_ref)
            out = acc / total
            at = pl.ds((side * heads + head) * HD, HD)
            mine_ref[:, at] = out[:rows].astype(BF16)
            send_ref[:, at] = out[rows:].astype(BF16)


def join_kernel(mine_ref, recv_ref, out_ref):
    width = mine_ref.shape[-1]
    first = lax.axis_index("uly") == 0

    @pl.when(first)
    def _():
        out_ref[:, :width] = mine_ref[...]
        out_ref[:, width:] = recv_ref[...]

    @pl.when(jnp.logical_not(first))
    def _():
        out_ref[:, :width] = recv_ref[...]
        out_ref[:, width:] = mine_ref[...]


def shards(n, fresh_qkv, stale_kv, q_gain, k_gain):
    rows, _, features = fresh_qkv.shape
    patch_rows, _, width = stale_kv.shape
    half = width // 2
    around = list(range(0, n, 2)) + list(range(1, n, 2))[::-1]
    right = [(around[i], around[(i + 1) % n]) for i in range(n)]
    left = [(b, a) for a, b in right]
    swap = [(0, 1), (1, 0)]
    far, near = n // 2, (n - 1) // 2

    sides = call(split_kernel, [((2, patch_rows, half), BF16)] * 2, stale_kv)
    forward, backward = list(sides), list(sides)
    arrived = [[], []]
    for hop in range(max(far, near)):
        for side in range(2):
            got = []
            if hop < (far if side == 0 else near):
                forward[side] = lax.ppermute(forward[side], "patch", right)
                got.append(forward[side])
            if hop < (near if side == 0 else far):
                backward[side] = lax.ppermute(backward[side], "patch", left)
                got.append(backward[side])
            arrived[side].append(got)

    keep, send = call(
        prep_kernel,
        [((3, rows, width), BF16)] * 2,
        fresh_qkv.transpose(1, 0, 2),
        q_gain.reshape(1, features),
        k_gain.reshape(1, features),
    )
    recv = lax.ppermute(send, "uly", swap)
    state = [((patch_rows, half), BF16), ((patch_rows, half), F32), ((2, patch_rows, HD), F32)]
    own = call(own_kernel, state * 2, keep, recv, flops=4 * patch_rows * patch_rows * width)
    states = [own[:3], own[3:]]
    hops = len(arrived[0])
    for hop in range(hops - 1):
        for side in range(2):
            blocks = arrived[side][hop]
            query, acc, ml = states[side]
            k = len(blocks)
            acc, ml = call(
                functools.partial(update_kernel, k),
                state[1:],
                query,
                *blocks,
                acc,
                ml,
                flops=4 * k * patch_rows * patch_rows * half,
                aliases={k + 1: 0, k + 2: 1},
            )
            states[side] = [query, acc, ml]
    mine, outgoing = call(
        last_kernel,
        [((rows, width), BF16)] * 2,
        *states[0],
        *arrived[0][-1],
        *states[1],
        *arrived[1][-1],
        flops=4 * patch_rows * patch_rows * width,
    )
    incoming = lax.ppermute(outgoing, "uly", swap)
    (out,) = call(join_kernel, [((rows, features), BF16)], mine, incoming)
    return out


def solution(mesh):
    in_specs = (
        P(("groups", "patch", "uly"), None, None),
        P(("groups", "patch"), None, "uly"),
        P(),
        P(),
    )
    out_specs = P(("groups", "patch", "uly"), None)
    body = functools.partial(shards, mesh.shape["patch"])
    return jax.shard_map(body, mesh=mesh, in_specs=in_specs, out_specs=out_specs, check_vma=False)
```

time: 99.8 us -> 47 us (0.47)
  waiting for transfers between devices: 50.1 us -> 13 us
  local copies, waits for them, and re-layouts: 23.4 us -> 2.1 us
  Pallas kernels: 0 us -> 16.1 us
  between operations: 13.6 us -> 0.16 us
  starting transfers between devices: 3.51 us -> 15.5 us
  blocking collectives: 3.87 us -> 0 us
  matrix products: 2.89 us -> 0 us
  other arithmetic: 2.11 us -> 0 us
    all_gather x1 -> x0, waiting for transfers between devices: 48.3 us -> none  [shards(): stale_all = lax.all_gather(stale_kv, 'patch', axis=0, tiled=True)]
    pallas_call x0 -> x11, Pallas kernels: none -> 16.1 us  [call(): pl.pallas_call(body, out_shape=[jax.ShapeDtypeStruct(s, t) for s, t in ou...]
    ppermute x0 -> x16, starting transfers between devices: none -> 15.5 us  [the longest x7 12.8 us: shards(): backward[side] = lax.ppermute(backward[side], 'patch', left)]
    ppermute x0 -> x16, waiting for transfers between devices: none -> 13 us  [the longest x7 7.51 us: shards(): forward[side] = lax.ppermute(forward[side], 'patch', right)]
    unnamed x15 -> x8, local copies, waits for them, and re-layouts: 11.4 us -> 2.08 us
    dynamic_update_slice x3 -> x0, local copies, waits for them, and re-layouts: 5.83 us -> none  [the longest x1 3.56 us: shards(): lax.dynamic_update_slice_in_dim(stale_all[:, 1], fresh_values, own_first, 0)]
    all_to_all x1 -> x0, blocking collectives: 3.87 us -> none  [shards(): lax.all_to_all(outgoing, 'uly', split_axis=0, concat_axis=1, tiled=True)]
    all_to_all x1 -> x0, starting transfers between devices: 3.5 us -> none  [shards(): lax.all_to_all(packed, 'uly', split_axis=2, concat_axis=0, tiled=True)]
  transfers between devices with their start and end apart: 2 -> 16, of which waited for: 2 -> 6; matrix products, arithmetic and copies ran while one was open for 12% -> 0% of each run, Pallas kernels for 0% -> 26%
where the time goes in v1:
time: 47 us; the launch traced here: 46.8 us
  Pallas kernels  16.1 us (34%)
  starting transfers between devices  15.5 us (33%)
  waiting for transfers between devices  13 us (28%)
  local copies, waits for them, and re-layouts  2.1 us (4%)
    pallas_call x11, Pallas kernels, call(): pl.pallas_call(body, out_shape=[jax.ShapeDtypeStruct(s, t) for s, t in ou...  16.1 us
    ppermute x7, starting transfers between devices, shards(): backward[side] = lax.ppermute(backward[side], 'patch', left)  12.8 us
    ppermute x7, waiting for transfers between devices, shards(): forward[side] = lax.ppermute(forward[side], 'patch', right)  7.51 us
    ppermute x7, waiting for transfers between devices, shards(): backward[side] = lax.ppermute(backward[side], 'patch', left)  4.17 us
    ppermute x7, starting transfers between devices, shards(): forward[side] = lax.ppermute(forward[side], 'patch', right)  2.56 us
    unnamed x8, local copies, waits for them, and re-layouts  2.08 us
    ppermute x1, waiting for transfers between devices, shards(): incoming = lax.ppermute(outgoing, 'uly', swap)  1.29 us
  transfers between devices with their start and end apart: 16, of which 6 were waited for; matrix products, arithmetic and copies ran while one was open for 0% of the time, Pallas kernels for 26%

profile of v1, /device:TPU:0, one launch (start us, length us, event | category | flops | bytes accessed | tf_op | source)
XLA Modules:
  0.0 46.8 jit_solution(17237942556275440430)
XLA Ops:
  0.0 0.0 copy-start.1
  0.0 1.0 %copy-done.1 = bf16[80,2,1280]{2,1,0:T(2,128)(2,1)S(1)} copy-done((bf16[80,2,1280]{2,1,0:T(2,128)(2,1)S(1)}, bf16[80,2,1280]{2,1,0:T(2,128)(2,1)}, u32[]{:S(2)}) %copy-start.1) | copy-done | bytes 409624
  1.0 0.0 copy-start.2
  1.0 1.0 %shard_map.48 = (bf16[2,80,640]{2,1,0:T(8,128)(2,1)S(1)}, bf16[2,80,640]{2,1,0:T(8,128)(2,1)S(1)}) custom-call(bf16[80,2,1280]{2,1,0:T(2,128)(2,1)S(1)} %copy-done.1), custom_call_target="tpu_custom_call" | custom-call | bytes 819200 | tf_op jit(solution)/shard_map/pallas_call | solution.py:23
  2.0 0.0 copy-start.3
  2.0 3.0 %collective-permute-start.11 = (bf16[2,80,640]{2,1,0:T(8,128)(2,1)S(1)}, bf16[2,80,640]{2,1,0:T(8,128)(2,1)S(1)}, u32[]{:S(2)}, u32[]{:S(2)}) collective-permute-start(bf16[2,80,640]{2,1,0:T(8,128)(2,1)S(1)} %get-tuple-element.42), channel_id=1, source_target_pairs={{4,0},{8,4},{12,8},{14,12},{10,14},{6,10},{2,6},{0,2},{5,1},{9,5},... | collective-permute-start | bytes 614408 | tf_op jit(solution)/shard_map/ppermute | solution.py:167
  5.0 0.2 collective-permute-start.1
  5.1 2.0 %collective-permute-start.8 = (bf16[2,80,640]{2,1,0:T(8,128)(2,1)S(1)}, bf16[2,80,640]{2,1,0:T(8,128)(2,1)S(1)}, u32[]{:S(2)}, u32[]{:S(2)}) collective-permute-start(bf16[2,80,640]{2,1,0:T(8,128)(2,1)S(1)} %get-tuple-element.42), channel_id=1, source_target_pairs={{0,4},{4,8},{8,12},{12,14},{14,10},{10,6},{6,2},{2,0},{1,5},{5,9},... | collective-permute-start | bytes 614408 | tf_op jit(solution)/shard_map/ppermute | solution.py:164
  7.1 0.1 collective-permute-start.4
  7.2 3.8 %collective-permute-done.11.refs_1_ = bf16[2,80,640]{2,1,0:T(8,128)(2,1)S(1)} collective-permute-done((bf16[2,80,640]{2,1,0:T(8,128)(2,1)S(1)}, bf16[2,80,640]{2,1,0:T(8,128)(2,1)S(1)}, u32[]{:S(2)}, u32[]{:S(2)}) %collective-permute-start.11) | collective-permute-done | bytes 204832 | tf_op jit(solution)/shard_map/ppermute | solution.py:167
  11.0 2.0 %collective-permute-start.12 = (bf16[2,80,640]{2,1,0:T(8,128)(2,1)S(1)}, bf16[2,80,640]{2,1,0:T(8,128)(2,1)S(1)}, u32[]{:S(2)}, u32[]{:S(2)}) collective-permute-start(bf16[2,80,640]{2,1,0:T(8,128)(2,1)S(1)} %collective-permute-done.11.refs_1_), channel_id=1, source_target_pairs={{4,0},{8,4},{12,8},{14,12},{10,14},{6,10},{2,6},{0,2},{5,1},{9,5},... | collective-permute-start | bytes 614408 | tf_op jit(solution)/shard_map/ppermute | solution.py:167
  13.0 0.0 collective-permute-done.1.refs_0_
  13.0 0.1 collective-permute-start.2
  13.1 4.3 %collective-permute-done.8.refs_0_ = bf16[2,80,640]{2,1,0:T(8,128)(2,1)S(1)} collective-permute-done((bf16[2,80,640]{2,1,0:T(8,128)(2,1)S(1)}, bf16[2,80,640]{2,1,0:T(8,128)(2,1)S(1)}, u32[]{:S(2)}, u32[]{:S(2)}) %collective-permute-start.8) | collective-permute-done | bytes 204832 | tf_op jit(solution)/shard_map/ppermute | solution.py:164
  17.4 0.1 collective-permute-start.9
  17.5 0.0 collective-permute-done.4.refs_1_
  17.5 1.9 %collective-permute-start.5 = (bf16[2,80,640]{2,1,0:T(8,128)(2,1)S(1)}, bf16[2,80,640]{2,1,0:T(8,128)(2,1)S(1)}, u32[]{:S(2)}, u32[]{:S(2)}) collective-permute-start(bf16[2,80,640]{2,1,0:T(8,128)(2,1)S(1)} %collective-permute-done.4.refs_1_), channel_id=1, source_target_pairs={{4,0},{8,4},{12,8},{14,12},{10,14},{6,10},{2,6},{0,2},{5,1},{9,5},... | collective-permute-start | bytes 614408 | tf_op jit(solution)/shard_map/ppermute | solution.py:167
  19.4 0.3 collective-permute-done.12.refs_1_
  19.8 2.0 %collective-permute-start.13 = (bf16[2,80,640]{2,1,0:T(8,128)(2,1)S(1)}, bf16[2,80,640]{2,1,0:T(8,128)(2,1)S(1)}, u32[]{:S(2)}, u32[]{:S(2)}) collective-permute-start(bf16[2,80,640]{2,1,0:T(8,128)(2,1)S(1)} %collective-permute-done.12.refs_1_), channel_id=1, source_target_pairs={{4,0},{8,4},{12,8},{14,12},{10,14},{6,10},{2,6},{0,2},{5,1},{9,5},... | collective-permute-start | bytes 614408 | tf_op jit(solution)/shard_map/ppermute | solution.py:167
  21.7 0.0 collective-permute-done.2.refs_0_
  21.8 0.1 collective-permute-start.3
  21.9 0.0 copy-done.2
  21.9 0.0 copy-done.3
  21.9 0.0 copy-start
  21.9 1.1 %copy-done = bf16[40,3,2560]{2,0,1:T(8,128)(2,1)S(1)} copy-done((bf16[40,3,2560]{2,0,1:T(8,128)(2,1)S(1)}, bf16[40,3,2560]{2,0,1:T(8,128)(2,1)}, u32[]{:S(2)}) %copy-start) | copy-done | bytes 614424
  23.0 0.3 shard_map.46
  23.4 0.1 collective-permute-start
  23.4 2.7 %collective-permute-done.9.refs_0_ = bf16[2,80,640]{2,1,0:T(8,128)(2,1)S(1)} collective-permute-done((bf16[2,80,640]{2,1,0:T(8,128)(2,1)S(1)}, bf16[2,80,640]{2,1,0:T(8,128)(2,1)S(1)}, u32[]{:S(2)}, u32[]{:S(2)}) %collective-permute-start.9) | collective-permute-done | bytes 204832 | tf_op jit(solution)/shard_map/ppermute | solution.py:164
  26.2 0.1 collective-permute-start.10
  26.3 0.0 collective-permute-done.5.refs_1_
  26.3 1.9 %collective-permute-start.6 = (bf16[2,80,640]{2,1,0:T(8,128)(2,1)S(1)}, bf16[2,80,640]{2,1,0:T(8,128)(2,1)S(1)}, u32[]{:S(2)}, u32[]{:S(2)}) collective-permute-start(bf16[2,80,640]{2,1,0:T(8,128)(2,1)S(1)} %collective-permute-done.5.refs_1_), channel_id=1, source_target_pairs={{4,0},{8,4},{12,8},{14,12},{10,14},{6,10},{2,6},{0,2},{5,1},{9,5},... | collective-permute-start | bytes 614408 | tf_op jit(solution)/shard_map/ppermute | solution.py:167
  28.2 0.0 collective-permute-done.13.refs_1_
  28.2 1.9 %collective-permute-start.14 = (bf16[2,80,640]{2,1,0:T(8,128)(2,1)S(1)}, bf16[2,80,640]{2,1,0:T(8,128)(2,1)S(1)}, u32[]{:S(2)}, u32[]{:S(2)}) collective-permute-start(bf16[2,80,640]{2,1,0:T(8,128)(2,1)S(1)} %collective-permute-done.13.refs_1_), channel_id=1, source_target_pairs={{4,0},{8,4},{12,8},{14,12},{10,14},{6,10},{2,6},{0,2},{5,1},{9,5},... | collective-permute-start | bytes 614408 | tf_op jit(solution)/shard_map/ppermute | solution.py:167
  30.1 0.4 collective-permute-done.3.refs_0_
  30.6 0.0 collective-permute-start.7
  30.6 0.0 collective-permute-done.recv_ref
  30.6 0.7 %shard_map.47 = (bf16[80,640]{1,0:T(8,128)(2,1)S(1)}, f32[80,640]{1,0:T(8,128)S(1)}, f32[2,80,128]{2,1,0:T(8,128)S(1)}, bf16[80,640]{1,0:T(8,128)(2,1)S(1)}, f32...) custom-call(bf16[3,40,1280]{2,1,0:T(8,128)(2,1)S(1)} %get-tuple-element.29.keep_ref, ...), custom_call_target="tpu_custom_call" | custom-call | flops 32768000 | bytes 1392640 | tf_op jit(solution)/shard_map/pallas_call | solution.py:23
  31.3 1.9 %shard_map.52 = (f32[80,640]{1,0:T(8,128)S(1)}, f32[2,80,128]{2,1,0:T(8,128)S(1)}) custom-call(bf16[80,640]{1,0:T(8,128)(2,1)S(1)} %get-tuple-element.41.q_ref.refs_4_, bf16[2,80,640]{2,1,0:T(8,128)(2,1)S(1)} %collective-permute-done.8.refs_0_, ...), custom_call_target="tpu_custom_call", output_to_operand_aliasing={{0}: (3, {}), {1}: (4, {})} | custom-call | flops 32768000 | bytes 1085440 | tf_op jit(solution)/shard_map/pallas_call | solution.py:23
  33.2 1.8 %shard_map.49 = (f32[80,640]{1,0:T(8,128)S(1)}, f32[2,80,128]{2,1,0:T(8,128)S(1)}) custom-call(bf16[80,640]{1,0:T(8,128)(2,1)S(1)} %get-tuple-element.31.q_ref.refs_0_, bf16[2,80,640]{2,1,0:T(8,128)(2,1)S(1)} %collective-permute-done.1.refs_0_, bf16[2,80,640]{2,1,0:T(8,128)(2,1)S(1)} %collective-permute-done.4.refs_1_, ...), custom_call_target="tpu_custom_call", output_to_operand_aliasing={{0}: (3, {}), {1}: (4, {})} | custom-call | flops 32768000 | bytes 1085440 | tf_op jit(solution)/shard_map/pallas_call | solution.py:23
  35.0 1.8 %shard_map.53 = (f32[80,640]{1,0:T(8,128)S(1)}, f32[2,80,128]{2,1,0:T(8,128)S(1)}) custom-call(bf16[80,640]{1,0:T(8,128)(2,1)S(1)} %get-tuple-element.41.q_ref.refs_4_, bf16[2,80,640]{2,1,0:T(8,128)(2,1)S(1)} %collective-permute-done.9.refs_0_, ...), custom_call_target="tpu_custom_call", output_to_operand_aliasing={{0}: (3, {}), {1}: (4, {})} | custom-call | flops 32768000 | bytes 1085440 | tf_op jit(solution)/shard_map/pallas_call | solution.py:23
  36.9 1.8 %shard_map.50 = (f32[80,640]{1,0:T(8,128)S(1)}, f32[2,80,128]{2,1,0:T(8,128)S(1)}) custom-call(bf16[80,640]{1,0:T(8,128)(2,1)S(1)} %get-tuple-element.31.q_ref.refs_0_, bf16[2,80,640]{2,1,0:T(8,128)(2,1)S(1)} %collective-permute-done.2.refs_0_, bf16[2,80,640]{2,1,0:T(8,128)(2,1)S(1)} %collective-permute-done.5.refs_1_, ...), custom_call_target="tpu_custom_call", output_to_operand_aliasing={{0}: (3, {}), {1}: (4, {})} | custom-call | flops 32768000 | bytes 1085440 | tf_op jit(solution)/shard_map/pallas_call | solution.py:23
  38.7 0.0 collective-permute-done.10.refs_0_
  38.7 1.8 %shard_map.54 = (f32[80,640]{1,0:T(8,128)S(1)}, f32[2,80,128]{2,1,0:T(8,128)S(1)}) custom-call(bf16[80,640]{1,0:T(8,128)(2,1)S(1)} %get-tuple-element.41.q_ref.refs_4_, bf16[2,80,640]{2,1,0:T(8,128)(2,1)S(1)} %collective-permute-done.10.refs_0_, ...), custom_call_target="tpu_custom_call", output_to_operand_aliasing={{0}: (3, {}), {1}: (4, {})} | custom-call | flops 32768000 | bytes 1085440 | tf_op jit(solution)/shard_map/pallas_call | solution.py:23
  40.6 0.0 collective-permute-done.6.refs_1_
  40.6 1.8 %shard_map.51 = (f32[80,640]{1,0:T(8,128)S(1)}, f32[2,80,128]{2,1,0:T(8,128)S(1)}) custom-call(bf16[80,640]{1,0:T(8,128)(2,1)S(1)} %get-tuple-element.31.q_ref.refs_0_, bf16[2,80,640]{2,1,0:T(8,128)(2,1)S(1)} %collective-permute-done.3.refs_0_, bf16[2,80,640]{2,1,0:T(8,128)(2,1)S(1)} %collective-permute-done.6.refs_1_, ...), custom_call_target="tpu_custom_call", output_to_operand_aliasing={{0}: (3, {}), {1}: (4, {})} | custom-call | flops 32768000 | bytes 1085440 | tf_op jit(solution)/shard_map/pallas_call | solution.py:23
  42.5 0.0 collective-permute-done.14.refs_7_
  42.5 0.0 collective-permute-done.7.refs_3_
  42.5 2.2 %shard_map.55 = (bf16[40,1280]{1,0:T(8,128)(2,1)S(1)}, bf16[40,1280]{1,0:T(8,128)(2,1)S(1)}) custom-call(bf16[80,640]{1,0:T(8,128)(2,1)S(1)} %get-tuple-element.31.q_ref.refs_0_, f32[80,640]{1,0:T(8,128)S(1)} %get-tuple-element.39.refs_1_, f32[2,80,128]{2,1,0:T(8,128)S(1)} %get-tuple-element.40.refs_2_, ...), custom_call_target="tpu_custom_call" | custom-call | flops 32768000 | bytes 1392640 | tf_op jit(solution)/shard_map/pallas_call | solution.py:23
  44.7 0.1 collective-permute-start.15
  44.8 1.3 %collective-permute-done.15.recv_ref = bf16[40,1280]{1,0:T(8,128)(2,1)S(1)} collective-permute-done((bf16[40,1280]{1,0:T(8,128)(2,1)S(1)}, bf16[40,1280]{1,0:T(8,128)(2,1)S(1)}, u32[]{:S(2)}, u32[]{:S(2)}) %collective-permute-start.15) | collective-permute-done | bytes 102432 | tf_op jit(solution)/shard_map/ppermute | solution.py:208
  46.1 0.7 %shard_map.56 = bf16[40,2560]{1,0:T(8,128)(2,1)} custom-call(bf16[40,1280]{1,0:T(8,128)(2,1)S(1)} %get-tuple-element.51.mine_ref, bf16[40,1280]{1,0:T(8,128)(2,1)S(1)} %collective-permute-done.15.recv_ref), custom_call_target="tpu_custom_call" | custom-call | bytes 409600 | tf_op jit(solution)/shard_map/pallas_call | solution.py:23
  (2 shorter events, 0.0 us)
Async XLA Ops:
  0.0 1.0 %copy-start.1 = (bf16[80,2,1280]{2,1,0:T(2,128)(2,1)S(1)}, bf16[80,2,1280]{2,1,0:T(2,128)(2,1)}, u32[]{:S(2)}) copy-start(bf16[80,2,1280]{2,1,0:T(2,128)(2,1)} %x_ref.1) | copy-start | bytes 1228804
  1.0 20.9 %copy-start.2 = (f32[2560]{0:T(1024)S(1)}, f32[2560]{0:T(1024)}, u32[]{:S(2)}) copy-start(f32[2560]{0:T(1024)} %param.6) | copy-start | bytes 30724
  2.0 19.9 %copy-start.3 = (f32[2560]{0:T(1024)S(1)}, f32[2560]{0:T(1024)}, u32[]{:S(2)}) copy-start(f32[2560]{0:T(1024)} %param.7) | copy-start | bytes 30724
  2.0 9.0 %collective-permute-start.11 = (bf16[2,80,640]{2,1,0:T(8,128)(2,1)S(1)}, bf16[2,80,640]{2,1,0:T(8,128)(2,1)S(1)}, u32[]{:S(2)}, u32[]{:S(2)}) collective-permute-start(bf16[2,80,640]{2,1,0:T(8,128)(2,1)S(1)} %get-tuple-element.42), channel_id=1, source_target_pairs={{4,0},{8,4},{12,8},{14,12},{10,14},{6,10},{2,6},{0,2},{5,1},{9,5},... | collective-permute-start | bytes 614408 | tf_op jit(solution)/shard_map/ppermute | solution.py:167
  5.0 8.0 %collective-permute-start.1 = (bf16[2,80,640]{2,1,0:T(8,128)(2,1)S(1)}, bf16[2,80,640]{2,1,0:T(8,128)(2,1)S(1)}, u32[]{:S(2)}, u32[]{:S(2)}) collective-permute-start(bf16[2,80,640]{2,1,0:T(8,128)(2,1)S(1)} %get-tuple-element.32), channel_id=1, source_target_pairs={{0,4},{4,8},{8,12},{12,14},{14,10},{10,6},{6,2},{2,0},{1,5},{5,9},... | collective-permute-start | bytes 614408 | tf_op jit(solution)/shard_map/ppermute | solution.py:164
  5.1 12.2 %collective-permute-start.8 = (bf16[2,80,640]{2,1,0:T(8,128)(2,1)S(1)}, bf16[2,80,640]{2,1,0:T(8,128)(2,1)S(1)}, u32[]{:S(2)}, u32[]{:S(2)}) collective-permute-start(bf16[2,80,640]{2,1,0:T(8,128)(2,1)S(1)} %get-tuple-element.42), channel_id=1, source_target_pairs={{0,4},{4,8},{8,12},{12,14},{14,10},{10,6},{6,2},{2,0},{1,5},{5,9},... | collective-permute-start | bytes 614408 | tf_op jit(solution)/shard_map/ppermute | solution.py:164
  7.1 10.4 %collective-permute-start.4 = (bf16[2,80,640]{2,1,0:T(8,128)(2,1)S(1)}, bf16[2,80,640]{2,1,0:T(8,128)(2,1)S(1)}, u32[]{:S(2)}, u32[]{:S(2)}) collective-permute-start(bf16[2,80,640]{2,1,0:T(8,128)(2,1)S(1)} %get-tuple-element.32), channel_id=1, source_target_pairs={{4,0},{8,4},{12,8},{14,12},{10,14},{6,10},{2,6},{0,2},{5,1},{9,5},... | collective-permute-start | bytes 614408 | tf_op jit(solution)/shard_map/ppermute | solution.py:167
  11.0 8.8 %collective-permute-start.12 = (bf16[2,80,640]{2,1,0:T(8,128)(2,1)S(1)}, bf16[2,80,640]{2,1,0:T(8,128)(2,1)S(1)}, u32[]{:S(2)}, u32[]{:S(2)}) collective-permute-start(bf16[2,80,640]{2,1,0:T(8,128)(2,1)S(1)} %collective-permute-done.11.refs_1_), channel_id=1, source_target_pairs={{4,0},{8,4},{12,8},{14,12},{10,14},{6,10},{2,6},{0,2},{5,1},{9,5},... | collective-permute-start | bytes 614408 | tf_op jit(solution)/shard_map/ppermute | solution.py:167
  13.0 8.8 %collective-permute-start.2 = (bf16[2,80,640]{2,1,0:T(8,128)(2,1)S(1)}, bf16[2,80,640]{2,1,0:T(8,128)(2,1)S(1)}, u32[]{:S(2)}, u32[]{:S(2)}) collective-permute-start(bf16[2,80,640]{2,1,0:T(8,128)(2,1)S(1)} %collective-permute-done.1.refs_0_), channel_id=1, source_target_pairs={{0,4},{4,8},{8,12},{12,14},{14,10},{10,6},{6,2},{2,0},{1,5},{5,9},... | collective-permute-start | bytes 614408 | tf_op jit(solution)/shard_map/ppermute | solution.py:164
  17.4 8.8 %collective-permute-start.9 = (bf16[2,80,640]{2,1,0:T(8,128)(2,1)S(1)}, bf16[2,80,640]{2,1,0:T(8,128)(2,1)S(1)}, u32[]{:S(2)}, u32[]{:S(2)}) collective-permute-start(bf16[2,80,640]{2,1,0:T(8,128)(2,1)S(1)} %collective-permute-done.8.refs_0_), channel_id=1, source_target_pairs={{0,4},{4,8},{8,12},{12,14},{14,10},{10,6},{6,2},{2,0},{1,5},{5,9},... | collective-permute-start | bytes 614408 | tf_op jit(solution)/shard_map/ppermute | solution.py:164
  17.5 8.8 %collective-permute-start.5 = (bf16[2,80,640]{2,1,0:T(8,128)(2,1)S(1)}, bf16[2,80,640]{2,1,0:T(8,128)(2,1)S(1)}, u32[]{:S(2)}, u32[]{:S(2)}) collective-permute-start(bf16[2,80,640]{2,1,0:T(8,128)(2,1)S(1)} %collective-permute-done.4.refs_1_), channel_id=1, source_target_pairs={{4,0},{8,4},{12,8},{14,12},{10,14},{6,10},{2,6},{0,2},{5,1},{9,5},... | collective-permute-start | bytes 614408 | tf_op jit(solution)/shard_map/ppermute | solution.py:167
  19.8 8.4 %collective-permute-start.13 = (bf16[2,80,640]{2,1,0:T(8,128)(2,1)S(1)}, bf16[2,80,640]{2,1,0:T(8,128)(2,1)S(1)}, u32[]{:S(2)}, u32[]{:S(2)}) collective-permute-start(bf16[2,80,640]{2,1,0:T(8,128)(2,1)S(1)} %collective-permute-done.12.refs_1_), channel_id=1, source_target_pairs={{4,0},{8,4},{12,8},{14,12},{10,14},{6,10},{2,6},{0,2},{5,1},{9,5},... | collective-permute-start | bytes 614408 | tf_op jit(solution)/shard_map/ppermute | solution.py:167
  21.8 8.8 %collective-permute-start.3 = (bf16[2,80,640]{2,1,0:T(8,128)(2,1)S(1)}, bf16[2,80,640]{2,1,0:T(8,128)(2,1)S(1)}, u32[]{:S(2)}, u32[]{:S(2)}) collective-permute-start(bf16[2,80,640]{2,1,0:T(8,128)(2,1)S(1)} %collective-permute-done.2.refs_0_), channel_id=1, source_target_pairs={{0,4},{4,8},{8,12},{12,14},{14,10},{10,6},{6,2},{2,0},{1,5},{5,9},... | collective-permute-start | bytes 614408 | tf_op jit(solution)/shard_map/ppermute | solution.py:164
  21.9 1.1 %copy-start = (bf16[40,3,2560]{2,0,1:T(8,128)(2,1)S(1)}, bf16[40,3,2560]{2,0,1:T(8,128)(2,1)}, u32[]{:S(2)}) copy-start(bf16[40,3,2560]{2,0,1:T(8,128)(2,1)} %param.4) | copy-start | bytes 1843204
  23.4 7.2 %collective-permute-start = (bf16[3,40,1280]{2,1,0:T(8,128)(2,1)S(1)}, bf16[3,40,1280]{2,1,0:T(8,128)(2,1)S(1)}, u32[]{:S(2)}, u32[]{:S(2)}) collective-permute-start(bf16[3,40,1280]{2,1,0:T(8,128)(2,1)S(1)} %get-tuple-element.30), channel_id=1, source_target_pairs={{0,1},{1,0},{2,3},{3,2},{4,5},{5,4},{6,7},{7,6},{8,9},{9,8},{10,11... | collective-permute-start | bytes 921608 | tf_op jit(solution)/shard_map/ppermute | solution.py:178
  26.2 12.6 %collective-permute-start.10 = (bf16[2,80,640]{2,1,0:T(8,128)(2,1)S(1)}, bf16[2,80,640]{2,1,0:T(8,128)(2,1)S(1)}, u32[]{:S(2)}, u32[]{:S(2)}) collective-permute-start(bf16[2,80,640]{2,1,0:T(8,128)(2,1)S(1)} %collective-permute-done.9.refs_0_), channel_id=1, source_target_pairs={{0,4},{4,8},{8,12},{12,14},{14,10},{10,6},{6,2},{2,0},{1,5},{5,9},... | collective-permute-start | bytes 614408 | tf_op jit(solution)/shard_map/ppermute | solution.py:164
  26.3 14.3 %collective-permute-start.6 = (bf16[2,80,640]{2,1,0:T(8,128)(2,1)S(1)}, bf16[2,80,640]{2,1,0:T(8,128)(2,1)S(1)}, u32[]{:S(2)}, u32[]{:S(2)}) collective-permute-start(bf16[2,80,640]{2,1,0:T(8,128)(2,1)S(1)} %collective-permute-done.5.refs_1_), channel_id=1, source_target_pairs={{4,0},{8,4},{12,8},{14,12},{10,14},{6,10},{2,6},{0,2},{5,1},{9,5},... | collective-permute-start | bytes 614408 | tf_op jit(solution)/shard_map/ppermute | solution.py:167
  28.2 14.3 %collective-permute-start.14 = (bf16[2,80,640]{2,1,0:T(8,128)(2,1)S(1)}, bf16[2,80,640]{2,1,0:T(8,128)(2,1)S(1)}, u32[]{:S(2)}, u32[]{:S(2)}) collective-permute-start(bf16[2,80,640]{2,1,0:T(8,128)(2,1)S(1)} %collective-permute-done.13.refs_1_), channel_id=1, source_target_pairs={{4,0},{8,4},{12,8},{14,12},{10,14},{6,10},{2,6},{0,2},{5,1},{9,5},... | collective-permute-start | bytes 614408 | tf_op jit(solution)/shard_map/ppermute | solution.py:167
  30.6 11.9 %collective-permute-start.7 = (bf16[2,80,640]{2,1,0:T(8,128)(2,1)S(1)}, bf16[2,80,640]{2,1,0:T(8,128)(2,1)S(1)}, u32[]{:S(2)}, u32[]{:S(2)}) collective-permute-start(bf16[2,80,640]{2,1,0:T(8,128)(2,1)S(1)} %collective-permute-done.3.refs_0_), channel_id=1, source_target_pairs={{0,4},{4,8},{8,12},{12,14},{14,10},{10,6},{6,2},{2,0},{1,5},{5,9},... | collective-permute-start | bytes 614408 | tf_op jit(solution)/shard_map/ppermute | solution.py:164
  44.7 1.4 %collective-permute-start.15 = (bf16[40,1280]{1,0:T(8,128)(2,1)S(1)}, bf16[40,1280]{1,0:T(8,128)(2,1)S(1)}, u32[]{:S(2)}, u32[]{:S(2)}) collective-permute-start(bf16[40,1280]{1,0:T(8,128)(2,1)S(1)} %get-tuple-element.52), channel_id=1, source_target_pairs={{0,1},{1,0},{2,3},{3,2},{4,5},{5,4},{6,7},{7,6},{8,9},{9,8},{10,11... | collective-permute-start | bytes 307208 | tf_op jit(solution)/shard_map/ppermute | solution.py:208

commit v2 on v1

v2 whole, which is shorter than its diff:
```python
import functools
import math

import jax
import jax.numpy as jnp
from jax import lax
from jax.experimental import pallas as pl
from jax.experimental.pallas import tpu as pltpu
from jax.sharding import PartitionSpec as P

HD = 128
EPSILON = 1e-06
SCALE = math.log2(math.e) / math.sqrt(HD)
VMEM = pl.BlockSpec(memory_space=pltpu.VMEM)
ANY = pl.BlockSpec(memory_space=pl.ANY)
F32 = jnp.float32
BF16 = jnp.bfloat16
WORK = 24
OWN = 1
GRANT = 32 << 20


def call(name, body, outs, *args, flops=0, ins=None, to=None, aliases=None, scratch=(), grant=32 << 20):
    size = sum(a.size * a.dtype.itemsize for a in args) + sum(
        math.prod(s) * jnp.dtype(t).itemsize for s, t in outs
    )
    return pl.pallas_call(
        body,
        name=name,
        out_shape=[jax.ShapeDtypeStruct(s, t) for s, t in outs],
        in_specs=ins or [VMEM] * len(args),
        out_specs=to or [VMEM] * len(outs),
        scratch_shapes=scratch,
        input_output_aliases=aliases or {},
        compiler_params=pltpu.CompilerParams(vmem_limit_bytes=grant),
        cost_estimate=pl.CostEstimate(flops=flops, bytes_accessed=size, transcendentals=0),
    )(*args)


def split_kernel(side, x_hbm, out_ref, buf, sem):
    half = out_ref.shape[-1]
    copy = pltpu.make_async_copy(x_hbm.at[:, :, pl.ds(side * half, half)], buf, sem)
    copy.start()
    copy.wait()
    for part in range(2):
        out_ref[part] = buf[:, part]


def prep_kernel(x_hbm, qg_ref, kg_ref, _, __, keep_ref, send_ref, buf, sem):
    width = keep_ref.shape[-1]
    first = lax.axis_index("uly") == 0
    copies = [pltpu.make_async_copy(x_hbm.at[i], buf.at[i], sem.at[i]) for i in range(3)]
    for copy in copies:
        copy.start()

    def put(part, rows):
        low, high = rows[:, :width], rows[:, width:]

        @pl.when(first)
        def _():
            keep_ref[part] = low
            send_ref[part] = high

        @pl.when(jnp.logical_not(first))
        def _():
            keep_ref[part] = high
            send_ref[part] = low

    for part, gain in ((0, qg_ref), (1, kg_ref)):
        copies[part].wait()
        rows = buf[part].astype(F32)
        inverse = lax.rsqrt(jnp.mean(rows * rows, axis=-1, keepdims=True) + EPSILON)
        put(part, (rows * inverse * gain[...]).astype(BF16))
    copies[2].wait()
    put(2, buf[2])


def scores_of(query, key):
    return lax.dot_general(query, key, (((1,), (1,)), ((), ())), preferred_element_type=F32)


def both(one, two):
    return jnp.concatenate([one.astype(F32), two.astype(F32)], axis=0).astype(BF16)


def own_kernel(keep_ref, recv_ref, *outs):
    heads = outs[0].shape[-1] // HD
    for side in range(2):
        q_ref, acc_ref, best_ref, total_ref = outs[4 * side : 4 * side + 4]
        for head in range(heads):
            src = pl.ds((side * heads + head) * HD, HD)
            dst = pl.ds(head * HD, HD)
            query = both(keep_ref[0, :, src], recv_ref[0, :, src])
            key = both(keep_ref[1, :, src], recv_ref[1, :, src])
            value = both(keep_ref[2, :, src], recv_ref[2, :, src])
            scores = scores_of(query, key)
            best = jnp.max(scores, axis=-1, keepdims=True)
            weights = jnp.exp2((scores - best) * SCALE)
            total = jnp.sum(weights, axis=-1, keepdims=True)
            acc = jnp.dot(weights.astype(BF16), value, preferred_element_type=F32)
            q_ref[:, dst] = query
            best_ref[:, dst] = jnp.broadcast_to(best, acc.shape)
            total_ref[:, dst] = jnp.broadcast_to(total, acc.shape)
            acc_ref[:, dst] = acc


def step(query, keys, values, acc, old, total):
    scores = [scores_of(query, key) for key in keys]
    top = jnp.max(functools.reduce(jnp.maximum, scores), axis=-1, keepdims=True)
    best = jnp.maximum(old, jnp.broadcast_to(top, old.shape))
    shrink = jnp.exp2((old - best) * SCALE)
    weights = [jnp.exp2((s - best[:, : s.shape[-1]]) * SCALE) for s in scores]
    total = total * shrink + jnp.sum(functools.reduce(jnp.add, weights), axis=-1, keepdims=True)
    acc = acc * shrink
    for w, value in zip(weights, values):
        acc = acc + jnp.dot(w.astype(BF16), value, preferred_element_type=F32)
    return acc, best, total


def update_kernel(blocks, q_ref, *refs):
    kv_refs, state, outs = refs[:blocks], refs[blocks : blocks + 3], refs[blocks + 3 :]
    for head in range(q_ref.shape[-1] // HD):
        at = pl.ds(head * HD, HD)
        old = [ref[:, at] for ref in state]
        keys = [kv[0, :, at] for kv in kv_refs]
        values = [kv[1, :, at] for kv in kv_refs]
        new = step(q_ref[:, at], keys, values, *old)
        for ref, value in zip(outs, new):
            ref[:, at] = value


def finish(begin, q_ref, sides, put):
    rows = q_ref.shape[1]
    for side, (acc_ref, best_ref, total_ref, *kv_refs) in enumerate(sides):
        heads = acc_ref.shape[-1] // HD
        for head in range(heads):
            at = pl.ds(head * HD, HD)
            to = pl.ds((side * heads + head) * HD, HD)
            old = [ref[begin : begin + rows, at] for ref in (acc_ref, best_ref, total_ref)]
            keys = [kv[0, :, at] for kv in kv_refs]
            values = [kv[1, :, at] for kv in kv_refs]
            acc, _, total = step(q_ref[0, :, to], keys, values, *old)
            put(to, (acc / total).astype(BF16))


def send_kernel(begin, cut, q_ref, *refs):
    out_ref = refs[-1]

    def put(to, value):
        out_ref[:, to] = value

    finish(begin, q_ref, (refs[:cut], refs[cut:-1]), put)


def mine_kernel(begin, cut, q_ref, *refs):
    out_hbm, buf, sem = refs[-3:]

    def put(to, value):
        buf[:, to] = value

    finish(begin, q_ref, (refs[:cut], refs[cut:-3]), put)
    width = buf.shape[-1]
    at = pl.ds(pl.multiple_of(lax.axis_index("uly") * width, HD), width)
    copy = pltpu.make_async_copy(buf, out_hbm.at[:, at], sem)
    copy.start()
    copy.wait()


def join_kernel(recv_ref, _, out_hbm, sem):
    width = recv_ref.shape[-1]
    at = pl.ds(pl.multiple_of((1 - lax.axis_index("uly")) * width, HD), width)
    copy = pltpu.make_async_copy(recv_ref, out_hbm.at[:, at], sem)
    copy.start()
    copy.wait()


def shards(n, fresh_qkv, stale_kv, q_gain, k_gain):
    rows, _, features = fresh_qkv.shape
    patch_rows, _, width = stale_kv.shape
    half = width // 2
    around = list(range(0, n, 2)) + list(range(1, n, 2))[::-1]
    right = [(around[i], around[(i + 1) % n]) for i in range(n)]
    left = [(b, a) for a, b in right]
    swap = [(0, 1), (1, 0)]
    far, near = n // 2, (n - 1) // 2

    dma = pltpu.SemaphoreType.DMA
    sides = [
        call(
            f"split{side}",
            functools.partial(split_kernel, side),
            [((2, patch_rows, half), BF16)],
            stale_kv,
            ins=[ANY],
            scratch=[pltpu.VMEM((patch_rows, 2, half), BF16), dma],
            grant=GRANT,
        )[0]
        for side in range(2)
    ]
    forward, backward = list(sides), list(sides)
    arrived = [[], []]
    for hop in range(max(far, near)):
        for side in range(2):
            got = []
            if hop < (far if side == 0 else near):
                forward[side] = lax.ppermute(forward[side], "patch", right)
                got.append(forward[side])
            if hop < (near if side == 0 else far):
                backward[side] = lax.ppermute(backward[side], "patch", left)
                got.append(backward[side])
            arrived[side].append(got)

    keep, send = call(
        "prep",
        prep_kernel,
        [((3, rows, width), BF16)] * 2,
        fresh_qkv.transpose(1, 0, 2),
        q_gain.reshape(1, features),
        k_gain.reshape(1, features),
        *sides,
        ins=[ANY, VMEM, VMEM, ANY, ANY],
        scratch=[pltpu.VMEM((3, rows, features), BF16), dma((3,))],
        grant=GRANT,
        flops=patch_rows * patch_rows * width // 8,
    )
    recv = lax.ppermute(send, "uly", swap)
    state = [((patch_rows, half), F32)] * 3
    work = WORK * 4 * patch_rows * patch_rows * half
    own = call("own", own_kernel, ([((patch_rows, half), BF16)] + state) * 2, keep, recv, flops=OWN * work)
    queries = [own[0], own[4]]
    states = [own[1:4], own[5:8]]
    for hop in range(len(arrived[0]) - 1):
        for side in range(2):
            blocks = arrived[side][hop]
            body = functools.partial(update_kernel, len(blocks))
            states[side] = call(
                f"update{hop}{side}", body, state, queries[side], *blocks, *states[side], flops=len(blocks) * work
            )
    last = [*states[0], *arrived[0][-1], *states[1], *arrived[1][-1]]
    cut = len(states[0]) + len(arrived[0][-1])
    (outgoing,) = call(
        "send", functools.partial(send_kernel, rows, cut), [((rows, width), BF16)], recv, *last, flops=work
    )
    incoming = lax.ppermute(outgoing, "uly", swap)
    result = [((rows, features), BF16)]
    (out,) = call(
        "mine",
        functools.partial(mine_kernel, 0, cut),
        result,
        keep,
        *last,
        to=[ANY],
        scratch=[pltpu.VMEM((rows, width), BF16), dma],
        flops=work,
    )
    (out,) = call("join", join_kernel, result, incoming, out, ins=[VMEM, ANY], to=[ANY], aliases={1: 0}, scratch=[dma])
    return out


def solution(mesh):
    in_specs = (
        P(("groups", "patch", "uly"), None, None),
        P(("groups", "patch"), None, "uly"),
        P(),
        P(),
    )
    out_specs = P(("groups", "patch", "uly"), None)
    body = functools.partial(shards, mesh.shape["patch"])
    return jax.shard_map(body, mesh=mesh, in_specs=in_specs, out_specs=out_specs, check_vma=False)
```

time: 47 us -> 44 us (0.936)
  Pallas kernels: 16.1 us -> 12 us
  waiting for transfers between devices: 13 us -> 14.8 us
  local copies, waits for them, and re-layouts: 2.1 us -> 1.56 us
    ppermute x7, waiting for transfers between devices: 7.51 us -> 11.9 us  [shards(): forward[side] = lax.ppermute(forward[side], 'patch', right)]
    pallas_call x11 -> x13, Pallas kernels: 16.1 us -> 12 us  [call(): pl.pallas_call(body, name=name, out_shape=[jax.ShapeDtypeStruct(s, t) for...]
    ppermute x7, waiting for transfers between devices: 4.17 us -> 2.88 us  [shards(): backward[side] = lax.ppermute(backward[side], 'patch', left)]
    ppermute x1, waiting for transfers between devices: 1.29 us -> 0.01 us  [shards(): incoming = lax.ppermute(outgoing, 'uly', swap)]
    ppermute x7, starting transfers between devices: 12.8 us -> 11.7 us  [shards(): backward[side] = lax.ppermute(backward[side], 'patch', left)]
    ppermute x7, starting transfers between devices: 2.56 us -> 3.37 us  [shards(): forward[side] = lax.ppermute(forward[side], 'patch', right)]
    unnamed x8, local copies, waits for them, and re-layouts: 2.08 us -> 1.55 us
  transfers between devices with their start and end apart: 16 -> 16, of which waited for: 6 -> 9; matrix products, arithmetic and copies ran while one was open for 0% -> 0% of each run, Pallas kernels for 26% -> 20%
where the time goes in v2:
time: 44 us; the launch traced here: 43.7 us
  starting transfers between devices  15.2 us (35%)
  waiting for transfers between devices  14.8 us (34%)
  Pallas kernels  12 us (27%)
  local copies, waits for them, and re-layouts  1.56 us (4%)
    pallas_call x13, Pallas kernels, call(): pl.pallas_call(body, name=name, out_shape=[jax.ShapeDtypeStruct(s, t) for...  12 us
    ppermute x7, waiting for transfers between devices, shards(): forward[side] = lax.ppermute(forward[side], 'patch', right)  11.9 us
    ppermute x7, starting transfers between devices, shards(): backward[side] = lax.ppermute(backward[side], 'patch', left)  11.7 us
    ppermute x7, starting transfers between devices, shards(): forward[side] = lax.ppermute(forward[side], 'patch', right)  3.37 us
    ppermute x7, waiting for transfers between devices, shards(): backward[side] = lax.ppermute(backward[side], 'patch', left)  2.88 us
    unnamed x8, local copies, waits for them, and re-layouts  1.55 us
  transfers between devices with their start and end apart: 16, of which 9 were waited for; matrix products, arithmetic and copies ran while one was open for 0% of the time, Pallas kernels for 20%

profile of v2, /device:TPU:0, one launch (start us, length us, event | category | flops | bytes accessed | tf_op | source)
XLA Modules:
  0.0 43.7 jit_solution(1520037072853002652)
XLA Ops:
  0.0 0.0 copy-start
  0.0 1.0 %copy-done = bf16[80,2,1280]{2,1,0:T(2,128)(2,1)S(1)} copy-done((bf16[80,2,1280]{2,1,0:T(2,128)(2,1)S(1)}, bf16[80,2,1280]{2,1,0:T(2,128)(2,1)}, u32[]{:S(2)}) %copy-start) | copy-done | bytes 409624
  1.0 0.0 copy-start.1
  1.0 0.5 %split1.1.__ = bf16[2,80,640]{2,1,0:T(8,128)(2,1)S(1)} custom-call(bf16[80,2,1280]{2,1,0:T(2,128)(2,1)S(1)} %copy-done), custom_call_target="tpu_custom_call" | custom-call | bytes 614400 | tf_op jit(solution)/shard_map/split1/pallas_call | solution.py:27
  1.6 0.0 copy-start.2
  1.6 3.0 %collective-permute-start.11 = (bf16[2,80,640]{2,1,0:T(8,128)(2,1)S(1)}, bf16[2,80,640]{2,1,0:T(8,128)(2,1)S(1)}, u32[]{:S(2)}, u32[]{:S(2)}) collective-permute-start(bf16[2,80,640]{2,1,0:T(8,128)(2,1)S(1)} %split1.1.__), channel_id=1, source_target_pairs={{4,0},{8,4},{12,8},{14,12},{10,14},{6,10},{2,6},{0,2},{5,1},{9,5},... | collective-permute-start | bytes 614408 | tf_op jit(solution)/shard_map/ppermute | solution.py:209
  4.6 0.5 %split0.1._ = bf16[2,80,640]{2,1,0:T(8,128)(2,1)S(1)} custom-call(bf16[80,2,1280]{2,1,0:T(2,128)(2,1)S(1)} %copy-done), custom_call_target="tpu_custom_call" | custom-call | bytes 614400 | tf_op jit(solution)/shard_map/split0/pallas_call | solution.py:27
  5.1 0.0 copy-start.3
  5.1 0.2 collective-permute-start.1
  5.3 0.0 copy-done.2
  5.3 0.5 %copy-done.3 = f32[2560]{0:T(1024)S(1)} copy-done((f32[2560]{0:T(1024)S(1)}, f32[2560]{0:T(1024)}, u32[]{:S(2)}) %copy-start.3) | copy-done | bytes 10264
  5.8 0.0 copy-done.1
  5.8 1.2 %prep.1 = (bf16[3,40,1280]{2,1,0:T(8,128)(2,1)S(1)}, bf16[3,40,1280]{2,1,0:T(8,128)(2,1)S(1)}) custom-call(bf16[3,40,2560]{2,1,0:T(8,128)(2,1)S(1)} %bitcast.1, f32[1,2560]{1,0:T(1,128)S(1)} %reshape.6.qg_ref, f32[1,2560]{1,0:T(1,128)S(1)} %reshape.7.kg_ref, bf16[2,80,640]{2,1,0:T(8,128)(2,1)S(1)} %split0.1._, bf16[2,80,640]{2,1,0:T(8,128)(2,1)S(1)} %split1.1.__), custom_call_target="tpu_custom_call" | custom-call | flops 1024000 | bytes 1658880 | tf_op jit(solution)/shard_map/prep/pallas_call | solution.py:27
  7.0 0.1 collective-permute-start
  7.1 1.5 %collective-permute-start.8 = (bf16[2,80,640]{2,1,0:T(8,128)(2,1)S(1)}, bf16[2,80,640]{2,1,0:T(8,128)(2,1)S(1)}, u32[]{:S(2)}, u32[]{:S(2)}) collective-permute-start(bf16[2,80,640]{2,1,0:T(8,128)(2,1)S(1)} %split1.1.__), channel_id=1, source_target_pairs={{0,4},{4,8},{8,12},{12,14},{14,10},{10,6},{6,2},{2,0},{1,5},{5,9},... | collective-permute-start | bytes 614408 | tf_op jit(solution)/shard_map/ppermute | solution.py:206
  8.6 0.5 %collective-permute-start.4 = (bf16[2,80,640]{2,1,0:T(8,128)(2,1)S(1)}, bf16[2,80,640]{2,1,0:T(8,128)(2,1)S(1)}, u32[]{:S(2)}, u32[]{:S(2)}) collective-permute-start(bf16[2,80,640]{2,1,0:T(8,128)(2,1)S(1)} %split0.1._), channel_id=1, source_target_pairs={{4,0},{8,4},{12,8},{14,12},{10,14},{6,10},{2,6},{0,2},{5,1},{9,5},... | collective-permute-start | bytes 614408 | tf_op jit(solution)/shard_map/ppermute | solution.py:209
  9.2 0.5 %collective-permute-done.11.refs_1_ = bf16[2,80,640]{2,1,0:T(8,128)(2,1)S(1)} collective-permute-done((bf16[2,80,640]{2,1,0:T(8,128)(2,1)S(1)}, bf16[2,80,640]{2,1,0:T(8,128)(2,1)S(1)}, u32[]{:S(2)}, u32[]{:S(2)}) %collective-permute-start.11) | collective-permute-done | bytes 204832 | tf_op jit(solution)/shard_map/ppermute | solution.py:209
  9.7 1.7 %collective-permute-start.12 = (bf16[2,80,640]{2,1,0:T(8,128)(2,1)S(1)}, bf16[2,80,640]{2,1,0:T(8,128)(2,1)S(1)}, u32[]{:S(2)}, u32[]{:S(2)}) collective-permute-start(bf16[2,80,640]{2,1,0:T(8,128)(2,1)S(1)} %collective-permute-done.11.refs_1_), channel_id=1, source_target_pairs={{4,0},{8,4},{12,8},{14,12},{10,14},{6,10},{2,6},{0,2},{5,1},{9,5},... | collective-permute-start | bytes 614408 | tf_op jit(solution)/shard_map/ppermute | solution.py:209
  11.4 1.8 %collective-permute-done.1.refs_0_ = bf16[2,80,640]{2,1,0:T(8,128)(2,1)S(1)} collective-permute-done((bf16[2,80,640]{2,1,0:T(8,128)(2,1)S(1)}, bf16[2,80,640]{2,1,0:T(8,128)(2,1)S(1)}, u32[]{:S(2)}, u32[]{:S(2)}) %collective-permute-start.1) | collective-permute-done | bytes 204832 | tf_op jit(solution)/shard_map/ppermute | solution.py:206
  13.2 0.0 collective-permute-start.2
  13.2 4.4 %collective-permute-done.8.refs_0_ = bf16[2,80,640]{2,1,0:T(8,128)(2,1)S(1)} collective-permute-done((bf16[2,80,640]{2,1,0:T(8,128)(2,1)S(1)}, bf16[2,80,640]{2,1,0:T(8,128)(2,1)S(1)}, u32[]{:S(2)}, u32[]{:S(2)}) %collective-permute-start.8) | collective-permute-done | bytes 204832 | tf_op jit(solution)/shard_map/ppermute | solution.py:206
  17.6 0.0 collective-permute-start.9
  17.6 0.0 collective-permute-done.4.refs_1_
  17.6 2.0 %collective-permute-start.5 = (bf16[2,80,640]{2,1,0:T(8,128)(2,1)S(1)}, bf16[2,80,640]{2,1,0:T(8,128)(2,1)S(1)}, u32[]{:S(2)}, u32[]{:S(2)}) collective-permute-start(bf16[2,80,640]{2,1,0:T(8,128)(2,1)S(1)} %collective-permute-done.4.refs_1_), channel_id=1, source_target_pairs={{4,0},{8,4},{12,8},{14,12},{10,14},{6,10},{2,6},{0,2},{5,1},{9,5},... | collective-permute-start | bytes 614408 | tf_op jit(solution)/shard_map/ppermute | solution.py:209
  19.6 0.0 collective-permute-done.recv_ref.q_ref
  19.6 0.7 %own.1 = (bf16[80,640]{1,0:T(8,128)(2,1)S(1)}, f32[80,640]{1,0:T(8,128)S(1)}, f32[80,640]{1,0:T(8,128)S(1)}, f32[80,640]{1,0:T(8,128)S(1)}, bf16[80,640]{1,0:T(8...) custom-call(bf16[3,40,1280]{2,1,0:T(8,128)(2,1)S(1)} %get-tuple-element.34.keep_ref.q_ref, ...), custom_call_target="tpu_custom_call" | custom-call | flops 393216000 | bytes 2048000 | tf_op jit(solution)/shard_map/own/pallas_call | solution.py:27
  20.3 0.6 %collective-permute-done.12.refs_1_ = bf16[2,80,640]{2,1,0:T(8,128)(2,1)S(1)} collective-permute-done((bf16[2,80,640]{2,1,0:T(8,128)(2,1)S(1)}, bf16[2,80,640]{2,1,0:T(8,128)(2,1)S(1)}, u32[]{:S(2)}, u32[]{:S(2)}) %collective-permute-start.12) | collective-permute-done | bytes 204832 | tf_op jit(solution)/shard_map/ppermute | solution.py:209
  20.9 1.0 %collective-permute-start.13 = (bf16[2,80,640]{2,1,0:T(8,128)(2,1)S(1)}, bf16[2,80,640]{2,1,0:T(8,128)(2,1)S(1)}, u32[]{:S(2)}, u32[]{:S(2)}) collective-permute-start(bf16[2,80,640]{2,1,0:T(8,128)(2,1)S(1)} %collective-permute-done.12.refs_1_), channel_id=1, source_target_pairs={{4,0},{8,4},{12,8},{14,12},{10,14},{6,10},{2,6},{0,2},{5,1},{9,5},... | collective-permute-start | bytes 614408 | tf_op jit(solution)/shard_map/ppermute | solution.py:209
  22.0 0.0 collective-permute-done.2.refs_0_
  22.0 1.0 %collective-permute-start.3 = (bf16[2,80,640]{2,1,0:T(8,128)(2,1)S(1)}, bf16[2,80,640]{2,1,0:T(8,128)(2,1)S(1)}, u32[]{:S(2)}, u32[]{:S(2)}) collective-permute-start(bf16[2,80,640]{2,1,0:T(8,128)(2,1)S(1)} %collective-permute-done.2.refs_0_), channel_id=1, source_target_pairs={{0,4},{4,8},{8,12},{12,14},{14,10},{10,6},{6,2},{2,0},{1,5},{5,9},... | collective-permute-start | bytes 614408 | tf_op jit(solution)/shard_map/ppermute | solution.py:206
  23.0 0.6 %update01.1 = (f32[80,640]{1,0:T(8,128)S(1)}, f32[80,640]{1,0:T(8,128)S(1)}, f32[80,640]{1,0:T(8,128)S(1)}) custom-call(bf16[80,640]{1,0:T(8,128)(2,1)S(1)} %get-tuple-element.48.q_ref, bf16[2,80,640]{2,1,0:T(8,128)(2,1)S(1)} %collective-permute-done.8.refs_0_, bf16[2,80,640]{2,1,0:T(8,128)(2,1)S(1)} %collective-permute-done.11.refs_1_, ...), custom_call_target="tpu_custom_call" | custom-call | flops 786432000 | bytes 1740800 | tf_op jit(solution)/shard_map/update01/pallas_call | solution.py:27
  23.6 2.8 %collective-permute-done.9.refs_0_ = bf16[2,80,640]{2,1,0:T(8,128)(2,1)S(1)} collective-permute-done((bf16[2,80,640]{2,1,0:T(8,128)(2,1)S(1)}, bf16[2,80,640]{2,1,0:T(8,128)(2,1)S(1)}, u32[]{:S(2)}, u32[]{:S(2)}) %collective-permute-start.9) | collective-permute-done | bytes 204832 | tf_op jit(solution)/shard_map/ppermute | solution.py:206
  26.3 0.0 collective-permute-start.10
  26.3 0.6 %update00.1 = (f32[80,640]{1,0:T(8,128)S(1)}, f32[80,640]{1,0:T(8,128)S(1)}, f32[80,640]{1,0:T(8,128)S(1)}) custom-call(bf16[80,640]{1,0:T(8,128)(2,1)S(1)} %get-tuple-element.35.q_ref, bf16[2,80,640]{2,1,0:T(8,128)(2,1)S(1)} %collective-permute-done.1.refs_0_, bf16[2,80,640]{2,1,0:T(8,128)(2,1)S(1)} %collective-permute-done.4.refs_1_, ...), custom_call_target="tpu_custom_call" | custom-call | flops 786432000 | bytes 1740800 | tf_op jit(solution)/shard_map/update00/pallas_call | solution.py:27
  26.9 0.0 collective-permute-done.5.refs_1_
  26.9 2.1 %collective-permute-start.6 = (bf16[2,80,640]{2,1,0:T(8,128)(2,1)S(1)}, bf16[2,80,640]{2,1,0:T(8,128)(2,1)S(1)}, u32[]{:S(2)}, u32[]{:S(2)}) collective-permute-start(bf16[2,80,640]{2,1,0:T(8,128)(2,1)S(1)} %collective-permute-done.5.refs_1_), channel_id=1, source_target_pairs={{4,0},{8,4},{12,8},{14,12},{10,14},{6,10},{2,6},{0,2},{5,1},{9,5},... | collective-permute-start | bytes 614408 | tf_op jit(solution)/shard_map/ppermute | solution.py:209
  29.0 0.6 %update11.1 = (f32[80,640]{1,0:T(8,128)S(1)}, f32[80,640]{1,0:T(8,128)S(1)}, f32[80,640]{1,0:T(8,128)S(1)}) custom-call(bf16[80,640]{1,0:T(8,128)(2,1)S(1)} %get-tuple-element.48.q_ref, bf16[2,80,640]{2,1,0:T(8,128)(2,1)S(1)} %collective-permute-done.9.refs_0_, bf16[2,80,640]{2,1,0:T(8,128)(2,1)S(1)} %collective-permute-done.12.refs_1_, ...), custom_call_target="tpu_custom_call" | custom-call | flops 786432000 | bytes 1740800 | tf_op jit(solution)/shard_map/update11/pallas_call | solution.py:27
  29.6 0.3 collective-permute-done.13.refs_1_
  29.9 1.4 %collective-permute-start.14 = (bf16[2,80,640]{2,1,0:T(8,128)(2,1)S(1)}, bf16[2,80,640]{2,1,0:T(8,128)(2,1)S(1)}, u32[]{:S(2)}, u32[]{:S(2)}) collective-permute-start(bf16[2,80,640]{2,1,0:T(8,128)(2,1)S(1)} %collective-permute-done.13.refs_1_), channel_id=1, source_target_pairs={{4,0},{8,4},{12,8},{14,12},{10,14},{6,10},{2,6},{0,2},{5,1},{9,5},... | collective-permute-start | bytes 614408 | tf_op jit(solution)/shard_map/ppermute | solution.py:209
  31.2 0.0 collective-permute-done.3.refs_0_
  31.2 0.7 %collective-permute-start.7 = (bf16[2,80,640]{2,1,0:T(8,128)(2,1)S(1)}, bf16[2,80,640]{2,1,0:T(8,128)(2,1)S(1)}, u32[]{:S(2)}, u32[]{:S(2)}) collective-permute-start(bf16[2,80,640]{2,1,0:T(8,128)(2,1)S(1)} %collective-permute-done.3.refs_0_), channel_id=1, source_target_pairs={{0,4},{4,8},{8,12},{12,14},{14,10},{10,6},{6,2},{2,0},{1,5},{5,9},... | collective-permute-start | bytes 614408 | tf_op jit(solution)/shard_map/ppermute | solution.py:206
  31.9 0.6 %update10.1 = (f32[80,640]{1,0:T(8,128)S(1)}, f32[80,640]{1,0:T(8,128)S(1)}, f32[80,640]{1,0:T(8,128)S(1)}) custom-call(bf16[80,640]{1,0:T(8,128)(2,1)S(1)} %get-tuple-element.35.q_ref, bf16[2,80,640]{2,1,0:T(8,128)(2,1)S(1)} %collective-permute-done.2.refs_0_, bf16[2,80,640]{2,1,0:T(8,128)(2,1)S(1)} %collective-permute-done.5.refs_1_, ...), custom_call_target="tpu_custom_call" | custom-call | flops 786432000 | bytes 1740800 | tf_op jit(solution)/shard_map/update10/pallas_call | solution.py:27
  32.5 2.6 %collective-permute-done.10.refs_0_ = bf16[2,80,640]{2,1,0:T(8,128)(2,1)S(1)} collective-permute-done((bf16[2,80,640]{2,1,0:T(8,128)(2,1)S(1)}, bf16[2,80,640]{2,1,0:T(8,128)(2,1)S(1)}, u32[]{:S(2)}, u32[]{:S(2)}) %collective-permute-start.10) | collective-permute-done | bytes 204832 | tf_op jit(solution)/shard_map/ppermute | solution.py:206
  35.1 0.6 %update21.1 = (f32[80,640]{1,0:T(8,128)S(1)}, f32[80,640]{1,0:T(8,128)S(1)}, f32[80,640]{1,0:T(8,128)S(1)}) custom-call(bf16[80,640]{1,0:T(8,128)(2,1)S(1)} %get-tuple-element.48.q_ref, bf16[2,80,640]{2,1,0:T(8,128)(2,1)S(1)} %collective-permute-done.10.refs_0_, bf16[2,80,640]{2,1,0:T(8,128)(2,1)S(1)} %collective-permute-done.13.refs_1_, ...), custom_call_target="tpu_custom_call" | custom-call | flops 786432000 | bytes 1740800 | tf_op jit(solution)/shard_map/update21/pallas_call | solution.py:27
  35.7 0.0 collective-permute-done.6.refs_1_
  35.7 0.6 %update20.1 = (f32[80,640]{1,0:T(8,128)S(1)}, f32[80,640]{1,0:T(8,128)S(1)}, f32[80,640]{1,0:T(8,128)S(1)}) custom-call(bf16[80,640]{1,0:T(8,128)(2,1)S(1)} %get-tuple-element.35.q_ref, bf16[2,80,640]{2,1,0:T(8,128)(2,1)S(1)} %collective-permute-done.3.refs_0_, bf16[2,80,640]{2,1,0:T(8,128)(2,1)S(1)} %collective-permute-done.6.refs_1_, ...), custom_call_target="tpu_custom_call" | custom-call | flops 786432000 | bytes 1740800 | tf_op jit(solution)/shard_map/update20/pallas_call | solution.py:27
  36.3 1.4 %collective-permute-done.14.refs_7_ = bf16[2,80,640]{2,1,0:T(8,128)(2,1)S(1)} collective-permute-done((bf16[2,80,640]{2,1,0:T(8,128)(2,1)S(1)}, bf16[2,80,640]{2,1,0:T(8,128)(2,1)S(1)}, u32[]{:S(2)}, u32[]{:S(2)}) %collective-permute-start.14) | collective-permute-done | bytes 204832 | tf_op jit(solution)/shard_map/ppermute | solution.py:209
  37.7 0.3 collective-permute-done.7.refs_3_
  38.0 2.1 %send.1 = bf16[40,1280]{1,0:T(8,128)(2,1)S(1)} custom-call(bf16[3,40,1280]{2,1,0:T(8,128)(2,1)S(1)} %collective-permute-done.recv_ref.q_ref, f32[80,640]{1,0:T(8,128)S(1)} %get-tuple-element.45.refs_0_, f32[80,640]{1,0:T(8,128)S(1)} %get-tuple-element.46.refs_1_, f32[80,640]{1,0:T(8,128)S(1)} %get-tuple-element.47.refs_2_, ...), custom_call_target="tpu_custom_call" | custom-call | flops 393216000 | bytes 2048000 | tf_op jit(solution)/shard_map/send/pallas_call | solution.py:27
  40.2 0.1 collective-permute-start.15
  40.2 2.8 %mine.1._ = bf16[40,2560]{1,0:T(8,128)(2,1)} custom-call(bf16[3,40,1280]{2,1,0:T(8,128)(2,1)S(1)} %get-tuple-element.34.keep_ref.q_ref, f32[80,640]{1,0:T(8,128)S(1)} %get-tuple-element.45.refs_0_, f32[80,640]{1,0:T(8,128)S(1)} %get-tuple-element.46.refs_1_, f32[80,640]{1,0:T(8,128)S(1)} %get-tuple-element.47.refs_2_, ...), custom_call_target="tpu_custom_call" | custom-call | flops 393216000 | bytes 2150400 | tf_op jit(solution)/shard_map/mine/pallas_call | solution.py:27
  43.0 0.0 collective-permute-done.15.recv_ref
  43.1 0.7 %join.1 = bf16[40,2560]{1,0:T(8,128)(2,1)} custom-call(bf16[40,1280]{1,0:T(8,128)(2,1)S(1)} %collective-permute-done.15.recv_ref, bf16[40,2560]{1,0:T(8,128)(2,1)} %mine.1._), custom_call_target="tpu_custom_call", output_to_operand_aliasing={{}: (1, {})} | custom-call | bytes 512000 | tf_op jit(solution)/shard_map/join/pallas_call | solution.py:27
  (2 shorter events, 0.0 us)
Async XLA Ops:
  0.0 1.0 %copy-start = (bf16[80,2,1280]{2,1,0:T(2,128)(2,1)S(1)}, bf16[80,2,1280]{2,1,0:T(2,128)(2,1)}, u32[]{:S(2)}) copy-start(bf16[80,2,1280]{2,1,0:T(2,128)(2,1)} %x_hbm.3) | copy-start | bytes 1228804
  1.0 4.8 %copy-start.1 = (bf16[40,3,2560]{2,0,1:T(8,128)(2,1)S(1)}, bf16[40,3,2560]{2,0,1:T(8,128)(2,1)}, u32[]{:S(2)}) copy-start(bf16[40,3,2560]{2,0,1:T(8,128)(2,1)} %param.4) | copy-start | bytes 1843204
  1.6 3.7 %copy-start.2 = (f32[2560]{0:T(1024)S(1)}, f32[2560]{0:T(1024)}, u32[]{:S(2)}) copy-start(f32[2560]{0:T(1024)} %param.6) | copy-start | bytes 30724
  1.6 8.2 %collective-permute-start.11 = (bf16[2,80,640]{2,1,0:T(8,128)(2,1)S(1)}, bf16[2,80,640]{2,1,0:T(8,128)(2,1)S(1)}, u32[]{:S(2)}, u32[]{:S(2)}) collective-permute-start(bf16[2,80,640]{2,1,0:T(8,128)(2,1)S(1)} %split1.1.__), channel_id=1, source_target_pairs={{4,0},{8,4},{12,8},{14,12},{10,14},{6,10},{2,6},{0,2},{5,1},{9,5},... | collective-permute-start | bytes 614408 | tf_op jit(solution)/shard_map/ppermute | solution.py:209
  5.1 0.7 %copy-start.3 = (f32[2560]{0:T(1024)S(1)}, f32[2560]{0:T(1024)}, u32[]{:S(2)}) copy-start(f32[2560]{0:T(1024)} %param.7) | copy-start | bytes 30724
  5.1 8.1 %collective-permute-start.1 = (bf16[2,80,640]{2,1,0:T(8,128)(2,1)S(1)}, bf16[2,80,640]{2,1,0:T(8,128)(2,1)S(1)}, u32[]{:S(2)}, u32[]{:S(2)}) collective-permute-start(bf16[2,80,640]{2,1,0:T(8,128)(2,1)S(1)} %split0.1._), channel_id=1, source_target_pairs={{0,4},{4,8},{8,12},{12,14},{14,10},{10,6},{6,2},{2,0},{1,5},{5,9},... | collective-permute-start | bytes 614408 | tf_op jit(solution)/shard_map/ppermute | solution.py:206
  7.0 12.6 %collective-permute-start = (bf16[3,40,1280]{2,1,0:T(8,128)(2,1)S(1)}, bf16[3,40,1280]{2,1,0:T(8,128)(2,1)S(1)}, u32[]{:S(2)}, u32[]{:S(2)}) collective-permute-start(bf16[3,40,1280]{2,1,0:T(8,128)(2,1)S(1)} %get-tuple-element.33), channel_id=1, source_target_pairs={{0,1},{1,0},{2,3},{3,2},{4,5},{5,4},{6,7},{7,6},{8,9},{9,8},{10,11... | collective-permute-start | bytes 921608 | tf_op jit(solution)/shard_map/ppermute | solution.py:226
  7.1 10.5 %collective-permute-start.8 = (bf16[2,80,640]{2,1,0:T(8,128)(2,1)S(1)}, bf16[2,80,640]{2,1,0:T(8,128)(2,1)S(1)}, u32[]{:S(2)}, u32[]{:S(2)}) collective-permute-start(bf16[2,80,640]{2,1,0:T(8,128)(2,1)S(1)} %split1.1.__), channel_id=1, source_target_pairs={{0,4},{4,8},{8,12},{12,14},{14,10},{10,6},{6,2},{2,0},{1,5},{5,9},... | collective-permute-start | bytes 614408 | tf_op jit(solution)/shard_map/ppermute | solution.py:206
  8.6 8.9 %collective-permute-start.4 = (bf16[2,80,640]{2,1,0:T(8,128)(2,1)S(1)}, bf16[2,80,640]{2,1,0:T(8,128)(2,1)S(1)}, u32[]{:S(2)}, u32[]{:S(2)}) collective-permute-start(bf16[2,80,640]{2,1,0:T(8,128)(2,1)S(1)} %split0.1._), channel_id=1, source_target_pairs={{4,0},{8,4},{12,8},{14,12},{10,14},{6,10},{2,6},{0,2},{5,1},{9,5},... | collective-permute-start | bytes 614408 | tf_op jit(solution)/shard_map/ppermute | solution.py:209
  9.7 11.2 %collective-permute-start.12 = (bf16[2,80,640]{2,1,0:T(8,128)(2,1)S(1)}, bf16[2,80,640]{2,1,0:T(8,128)(2,1)S(1)}, u32[]{:S(2)}, u32[]{:S(2)}) collective-permute-start(bf16[2,80,640]{2,1,0:T(8,128)(2,1)S(1)} %collective-permute-done.11.refs_1_), channel_id=1, source_target_pairs={{4,0},{8,4},{12,8},{14,12},{10,14},{6,10},{2,6},{0,2},{5,1},{9,5},... | collective-permute-start | bytes 614408 | tf_op jit(solution)/shard_map/ppermute | solution.py:209
  13.2 8.8 %collective-permute-start.2 = (bf16[2,80,640]{2,1,0:T(8,128)(2,1)S(1)}, bf16[2,80,640]{2,1,0:T(8,128)(2,1)S(1)}, u32[]{:S(2)}, u32[]{:S(2)}) collective-permute-start(bf16[2,80,640]{2,1,0:T(8,128)(2,1)S(1)} %collective-permute-done.1.refs_0_), channel_id=1, source_target_pairs={{0,4},{4,8},{8,12},{12,14},{14,10},{10,6},{6,2},{2,0},{1,5},{5,9},... | collective-permute-start | bytes 614408 | tf_op jit(solution)/shard_map/ppermute | solution.py:206
  17.6 8.8 %collective-permute-start.9 = (bf16[2,80,640]{2,1,0:T(8,128)(2,1)S(1)}, bf16[2,80,640]{2,1,0:T(8,128)(2,1)S(1)}, u32[]{:S(2)}, u32[]{:S(2)}) collective-permute-start(bf16[2,80,640]{2,1,0:T(8,128)(2,1)S(1)} %collective-permute-done.8.refs_0_), channel_id=1, source_target_pairs={{0,4},{4,8},{8,12},{12,14},{14,10},{10,6},{6,2},{2,0},{1,5},{5,9},... | collective-permute-start | bytes 614408 | tf_op jit(solution)/shard_map/ppermute | solution.py:206
  17.6 9.4 %collective-permute-start.5 = (bf16[2,80,640]{2,1,0:T(8,128)(2,1)S(1)}, bf16[2,80,640]{2,1,0:T(8,128)(2,1)S(1)}, u32[]{:S(2)}, u32[]{:S(2)}) collective-permute-start(bf16[2,80,640]{2,1,0:T(8,128)(2,1)S(1)} %collective-permute-done.4.refs_1_), channel_id=1, source_target_pairs={{4,0},{8,4},{12,8},{14,12},{10,14},{6,10},{2,6},{0,2},{5,1},{9,5},... | collective-permute-start | bytes 614408 | tf_op jit(solution)/shard_map/ppermute | solution.py:209
  20.9 8.9 %collective-permute-start.13 = (bf16[2,80,640]{2,1,0:T(8,128)(2,1)S(1)}, bf16[2,80,640]{2,1,0:T(8,128)(2,1)S(1)}, u32[]{:S(2)}, u32[]{:S(2)}) collective-permute-start(bf16[2,80,640]{2,1,0:T(8,128)(2,1)S(1)} %collective-permute-done.12.refs_1_), channel_id=1, source_target_pairs={{4,0},{8,4},{12,8},{14,12},{10,14},{6,10},{2,6},{0,2},{5,1},{9,5},... | collective-permute-start | bytes 614408 | tf_op jit(solution)/shard_map/ppermute | solution.py:209
  22.0 9.2 %collective-permute-start.3 = (bf16[2,80,640]{2,1,0:T(8,128)(2,1)S(1)}, bf16[2,80,640]{2,1,0:T(8,128)(2,1)S(1)}, u32[]{:S(2)}, u32[]{:S(2)}) collective-permute-start(bf16[2,80,640]{2,1,0:T(8,128)(2,1)S(1)} %collective-permute-done.2.refs_0_), channel_id=1, source_target_pairs={{0,4},{4,8},{8,12},{12,14},{14,10},{10,6},{6,2},{2,0},{1,5},{5,9},... | collective-permute-start | bytes 614408 | tf_op jit(solution)/shard_map/ppermute | solution.py:206
  26.3 8.8 %collective-permute-start.10 = (bf16[2,80,640]{2,1,0:T(8,128)(2,1)S(1)}, bf16[2,80,640]{2,1,0:T(8,128)(2,1)S(1)}, u32[]{:S(2)}, u32[]{:S(2)}) collective-permute-start(bf16[2,80,640]{2,1,0:T(8,128)(2,1)S(1)} %collective-permute-done.9.refs_0_), channel_id=1, source_target_pairs={{0,4},{4,8},{8,12},{12,14},{14,10},{10,6},{6,2},{2,0},{1,5},{5,9},... | collective-permute-start | bytes 614408 | tf_op jit(solution)/shard_map/ppermute | solution.py:206
  26.9 8.8 %collective-permute-start.6 = (bf16[2,80,640]{2,1,0:T(8,128)(2,1)S(1)}, bf16[2,80,640]{2,1,0:T(8,128)(2,1)S(1)}, u32[]{:S(2)}, u32[]{:S(2)}) collective-permute-start(bf16[2,80,640]{2,1,0:T(8,128)(2,1)S(1)} %collective-permute-done.5.refs_1_), channel_id=1, source_target_pairs={{4,0},{8,4},{12,8},{14,12},{10,14},{6,10},{2,6},{0,2},{5,1},{9,5},... | collective-permute-start | bytes 614408 | tf_op jit(solution)/shard_map/ppermute | solution.py:209
  29.9 7.9 %collective-permute-start.14 = (bf16[2,80,640]{2,1,0:T(8,128)(2,1)S(1)}, bf16[2,80,640]{2,1,0:T(8,128)(2,1)S(1)}, u32[]{:S(2)}, u32[]{:S(2)}) collective-permute-start(bf16[2,80,640]{2,1,0:T(8,128)(2,1)S(1)} %collective-permute-done.13.refs_1_), channel_id=1, source_target_pairs={{4,0},{8,4},{12,8},{14,12},{10,14},{6,10},{2,6},{0,2},{5,1},{9,5},... | collective-permute-start | bytes 614408 | tf_op jit(solution)/shard_map/ppermute | solution.py:209
  31.2 6.8 %collective-permute-start.7 = (bf16[2,80,640]{2,1,0:T(8,128)(2,1)S(1)}, bf16[2,80,640]{2,1,0:T(8,128)(2,1)S(1)}, u32[]{:S(2)}, u32[]{:S(2)}) collective-permute-start(bf16[2,80,640]{2,1,0:T(8,128)(2,1)S(1)} %collective-permute-done.3.refs_0_), channel_id=1, source_target_pairs={{0,4},{4,8},{8,12},{12,14},{14,10},{10,6},{6,2},{2,0},{1,5},{5,9},... | collective-permute-start | bytes 614408 | tf_op jit(solution)/shard_map/ppermute | solution.py:206
  40.2 2.9 %collective-permute-start.15 = (bf16[40,1280]{1,0:T(8,128)(2,1)S(1)}, bf16[40,1280]{1,0:T(8,128)(2,1)S(1)}, u32[]{:S(2)}, u32[]{:S(2)}) collective-permute-start(bf16[40,1280]{1,0:T(8,128)(2,1)S(1)} %send.1), channel_id=1, source_target_pairs={{0,1},{1,0},{2,3},{3,2},{4,5},{5,4},{6,7},{7,6},{8,9},{9,8},{10,11... | collective-permute-start | bytes 307208 | tf_op jit(solution)/shard_map/ppermute | solution.py:244

commit v3 on v2

--- a/solution.py
+++ b/solution.py
@@ -17,7 +17,8 @@
 BF16 = jnp.bfloat16
 WORK = 24
 OWN = 1
-GRANT = 32 << 20
+GRANT = 56150240
+PIECES = 5
 
 
 def call(name, body, outs, *args, flops=0, ins=None, to=None, aliases=None, scratch=(), grant=32 << 20):
@@ -39,11 +40,19 @@
 
 def split_kernel(side, x_hbm, out_ref, buf, sem):
     half = out_ref.shape[-1]
-    copy = pltpu.make_async_copy(x_hbm.at[:, :, pl.ds(side * half, half)], buf, sem)
-    copy.start()
-    copy.wait()
-    for part in range(2):
-        out_ref[part] = buf[:, part]
+    count = sem.shape[0]
+    rows = buf.shape[0] // count
+    copies = []
+    for i in range(count):
+        at = pl.ds(i * rows, rows)
+        copies.append(
+            pltpu.make_async_copy(x_hbm.at[at, :, pl.ds(side * half, half)], buf.at[at], sem.at[i])
+        )
+        copies[i].start()
+    for i in range(count):
+        copies[i].wait()
+        for part in range(2):
+            out_ref[part, i * rows : (i + 1) * rows] = buf[i * rows : (i + 1) * rows, part]
 
 
 def prep_kernel(x_hbm, qg_ref, kg_ref, _, __, keep_ref, send_ref, buf, sem):
@@ -83,82 +92,85 @@
     return jnp.concatenate([one.astype(F32), two.astype(F32)], axis=0).astype(BF16)
 
 
+def weigh(scores, old):
+    top = jnp.max(functools.reduce(jnp.maximum, scores), axis=-1, keepdims=True)
+    if old is None:
+        weights = [jnp.exp2((s - top) * SCALE) for s in scores]
+        total = jnp.sum(functools.reduce(jnp.add, weights), axis=-1, keepdims=True)
+        shape = (top.shape[0], HD)
+        return weights, None, jnp.broadcast_to(top, shape), jnp.broadcast_to(total, shape)
+    _, best, total = old
+    new = jnp.maximum(best, jnp.broadcast_to(top, best.shape))
+    shrink = jnp.exp2((best - new) * SCALE)
+    weights = [jnp.exp2((s - new[:, : s.shape[-1]]) * SCALE) for s in scores]
+    total = total * shrink + jnp.sum(functools.reduce(jnp.add, weights), axis=-1, keepdims=True)
+    return weights, shrink, new, total
+
+
+def attend(heads):
+    scores = [[scores_of(query, key) for key in keys] for query, keys, _, _ in heads]
+    weighed = [weigh(s, old) for s, (_, _, _, old) in zip(scores, heads)]
+    for (_, _, values, old), (weights, shrink, best, total) in zip(heads, weighed):
+        products = [
+            jnp.dot(w.astype(BF16), value, preferred_element_type=F32)
+            for w, value in zip(weights, values)
+        ]
+        acc = functools.reduce(jnp.add, products)
+        yield (acc if old is None else old[0] * shrink + acc), best, total
+
+
 def own_kernel(keep_ref, recv_ref, *outs):
-    heads = outs[0].shape[-1] // HD
-    for side in range(2):
-        q_ref, acc_ref, best_ref, total_ref = outs[4 * side : 4 * side + 4]
-        for head in range(heads):
-            src = pl.ds((side * heads + head) * HD, HD)
-            dst = pl.ds(head * HD, HD)
-            query = both(keep_ref[0, :, src], recv_ref[0, :, src])
-            key = both(keep_ref[1, :, src], recv_ref[1, :, src])
-            value = both(keep_ref[2, :, src], recv_ref[2, :, src])
-            scores = scores_of(query, key)
-            best = jnp.max(scores, axis=-1, keepdims=True)
-            weights = jnp.exp2((scores - best) * SCALE)
-            total = jnp.sum(weights, axis=-1, keepdims=True)
-            acc = jnp.dot(weights.astype(BF16), value, preferred_element_type=F32)
-            q_ref[:, dst] = query
-            best_ref[:, dst] = jnp.broadcast_to(best, acc.shape)
-            total_ref[:, dst] = jnp.broadcast_to(total, acc.shape)
-            acc_ref[:, dst] = acc
-
-
-def step(query, keys, values, acc, old, total):
-    scores = [scores_of(query, key) for key in keys]
-    top = jnp.max(functools.reduce(jnp.maximum, scores), axis=-1, keepdims=True)
-    best = jnp.maximum(old, jnp.broadcast_to(top, old.shape))
-    shrink = jnp.exp2((old - best) * SCALE)
-    weights = [jnp.exp2((s - best[:, : s.shape[-1]]) * SCALE) for s in scores]
-    total = total * shrink + jnp.sum(functools.reduce(jnp.add, weights), axis=-1, keepdims=True)
-    acc = acc * shrink
-    for w, value in zip(weights, values):
-        acc = acc + jnp.dot(w.astype(BF16), value, preferred_element_type=F32)
-    return acc, best, total
+    count = outs[0].shape[-1] // HD
+    heads = []
+    for head in range(2 * count):
+        at = pl.ds(head * HD, HD)
+        query, key, value = (both(keep_ref[i, :, at], recv_ref[i, :, at]) for i in range(3))
+        heads.append((query, [key], [value], None))
+    for head, new in enumerate(attend(heads)):
+        q_ref, *state = outs[4 * (head // count) : 4 * (head // count) + 4]
+        to = pl.ds(head % count * HD, HD)
+        q_ref[:, to] = heads[head][0]
+        for ref, value in zip(state, new):
+            ref[:, to] = value
 
 
 def update_kernel(blocks, q_ref, *refs):
     kv_refs, state, outs = refs[:blocks], refs[blocks : blocks + 3], refs[blocks + 3 :]
+    heads = []
     for head in range(q_ref.shape[-1] // HD):
         at = pl.ds(head * HD, HD)
-        old = [ref[:, at] for ref in state]
-        keys = [kv[0, :, at] for kv in kv_refs]
-        values = [kv[1, :, at] for kv in kv_refs]
-        new = step(q_ref[:, at], keys, values, *old)
+        keys, values = ([kv[i, :, at] for kv in kv_refs] for i in range(2))
+        heads.append((q_ref[:, at], keys, values, [ref[:, at] for ref in state]))
+    for head, new in enumerate(attend(heads)):
         for ref, value in zip(outs, new):
-            ref[:, at] = value
-
-
-def finish(begin, q_ref, sides, put):
+            ref[:, head * HD : (head + 1) * HD] = value
+
+
+def finish(begin, q_ref, sides, out_ref):
     rows = q_ref.shape[1]
-    for side, (acc_ref, best_ref, total_ref, *kv_refs) in enumerate(sides):
-        heads = acc_ref.shape[-1] // HD
-        for head in range(heads):
+    heads = []
+    for *state, kv_refs in sides:
+        for head in range(state[0].shape[-1] // HD):
             at = pl.ds(head * HD, HD)
-            to = pl.ds((side * heads + head) * HD, HD)
-            old = [ref[begin : begin + rows, at] for ref in (acc_ref, best_ref, total_ref)]
-            keys = [kv[0, :, at] for kv in kv_refs]
-            values = [kv[1, :, at] for kv in kv_refs]
-            acc, _, total = step(q_ref[0, :, to], keys, values, *old)
-            put(to, (acc / total).astype(BF16))
+            query = q_ref[0, :, pl.ds(len(heads) * HD, HD)]
+            keys, values = ([kv[i, :, at] for kv in kv_refs] for i in range(2))
+            old = [ref[begin : begin + rows, at] for ref in state]
+            heads.append((query, keys, values, old))
+    for head, (acc, _, total) in enumerate(attend(heads)):
+        out_ref[:, head * HD : (head + 1) * HD] = (acc / total).astype(BF16)
+
+
+def two_sides(refs, cut):
+    return [(*side[:3], side[3:]) for side in (refs[:cut], refs[cut:])]
 
 
 def send_kernel(begin, cut, q_ref, *refs):
-    out_ref = refs[-1]
-
-    def put(to, value):
-        out_ref[:, to] = value
-
-    finish(begin, q_ref, (refs[:cut], refs[cut:-1]), put)
+    finish(begin, q_ref, two_sides(refs[:-1], cut), refs[-1])
 
 
 def mine_kernel(begin, cut, q_ref, *refs):
     out_hbm, buf, sem = refs[-3:]
-
-    def put(to, value):
-        buf[:, to] = value
-
-    finish(begin, q_ref, (refs[:cut], refs[cut:-3]), put)
+    finish(begin, q_ref, two_sides(refs[:-3], cut), buf)
     width = buf.shape[-1]
     at = pl.ds(pl.multiple_of(lax.axis_index("uly") * width, HD), width)
     copy = pltpu.make_async_copy(buf, out_hbm.at[:, at], sem)
@@ -192,7 +204,7 @@
             [((2, patch_rows, half), BF16)],
             stale_kv,
             ins=[ANY],
-            scratch=[pltpu.VMEM((patch_rows, 2, half), BF16), dma],
+            scratch=[pltpu.VMEM((patch_rows, 2, half), BF16), dma((PIECES,))],
             grant=GRANT,
         )[0]
         for side in range(2)
@@ -220,7 +232,6 @@
         *sides,
         ins=[ANY, VMEM, VMEM, ANY, ANY],
         scratch=[pltpu.VMEM((3, rows, features), BF16), dma((3,))],
-        grant=GRANT,
         flops=patch_rows * patch_rows * width // 8,
     )
     recv = lax.ppermute(send, "uly", swap)

time: 44 us -> 41.3 us (0.939)
  Pallas kernels: 12 us -> 9.55 us
  waiting for transfers between devices: 14.8 us -> 15.9 us
  local copies, waits for them, and re-layouts: 1.56 us -> 0.56 us
    pallas_call x13, Pallas kernels: 12 us -> 9.55 us  [call(): pl.pallas_call(body, name=name, out_shape=[jax.ShapeDtypeStruct(s, t) for...]
    unnamed x8 -> x6, local copies, waits for them, and re-layouts: 1.55 us -> 0.54 us
    ppermute x7, waiting for transfers between devices: 11.9 us -> 12.8 us  [shards(): forward[side] = lax.ppermute(forward[side], 'patch', right)]
    ppermute x7, starting transfers between devices: 11.7 us -> 11.1 us  [shards(): backward[side] = lax.ppermute(backward[side], 'patch', left)]
  transfers between devices with their start and end apart: 16 -> 16, of which waited for: 9 -> 10; matrix products, arithmetic and copies ran while one was open for 0% -> 0% of each run, Pallas kernels for 20% -> 17%
where the time goes in v3:
time: 41.3 us; the launch traced here: 41.1 us
  waiting for transfers between devices  15.9 us (38%)
  starting transfers between devices  14.9 us (36%)
  Pallas kernels  9.55 us (23%)
  local copies, waits for them, and re-layouts  0.56 us (1%)
    ppermute x7, waiting for transfers between devices, shards(): forward[side] = lax.ppermute(forward[side], 'patch', right)  12.8 us
    ppermute x7, starting transfers between devices, shards(): backward[side] = lax.ppermute(backward[side], 'patch', left)  11.1 us
    pallas_call x13, Pallas kernels, call(): pl.pallas_call(body, name=name, out_shape=[jax.ShapeDtypeStruct(s, t) for...  9.55 us
    ppermute x7, starting transfers between devices, shards(): forward[side] = lax.ppermute(forward[side], 'patch', right)  3.66 us
    ppermute x7, waiting for transfers between devices, shards(): backward[side] = lax.ppermute(backward[side], 'patch', left)  3 us
  transfers between devices with their start and end apart: 16, of which 10 were waited for; matrix products, arithmetic and copies ran while one was open for 0% of the time, Pallas kernels for 17%

profile of v3, /device:TPU:0, one launch (start us, length us, event | category | flops | bytes accessed | tf_op | source)
XLA Modules:
  0.0 41.1 jit_solution(1363603138623670138)
XLA Ops:
  0.0 0.0 copy-start
  0.0 1.3 %split1.1.__ = bf16[2,80,640]{2,1,0:T(8,128)(2,1)S(1)} custom-call(bf16[80,2,1280]{2,1,0:T(2,128)(2,1)} %x_hbm.3), custom_call_target="tpu_custom_call" | custom-call | bytes 614400 | tf_op jit(solution)/shard_map/split1/pallas_call | solution.py:28
  1.3 0.0 copy-start.1
  1.4 3.0 %collective-permute-start.11 = (bf16[2,80,640]{2,1,0:T(8,128)(2,1)S(1)}, bf16[2,80,640]{2,1,0:T(8,128)(2,1)S(1)}, u32[]{:S(2)}, u32[]{:S(2)}) collective-permute-start(bf16[2,80,640]{2,1,0:T(8,128)(2,1)S(1)} %split1.1.__), channel_id=1, source_target_pairs={{4,0},{8,4},{12,8},{14,12},{10,14},{6,10},{2,6},{0,2},{5,1},{9,5},... | collective-permute-start | bytes 614408 | tf_op jit(solution)/shard_map/ppermute | solution.py:221
  4.3 1.3 %split0.1._ = bf16[2,80,640]{2,1,0:T(8,128)(2,1)S(1)} custom-call(bf16[80,2,1280]{2,1,0:T(2,128)(2,1)} %x_hbm.3), custom_call_target="tpu_custom_call" | custom-call | bytes 614400 | tf_op jit(solution)/shard_map/split0/pallas_call | solution.py:28
  5.6 0.0 copy-start.2
  5.6 0.2 collective-permute-start.1
  5.8 0.0 copy-done.1
  5.8 0.5 %copy-done.2 = f32[2560]{0:T(1024)S(1)} copy-done((f32[2560]{0:T(1024)S(1)}, f32[2560]{0:T(1024)}, u32[]{:S(2)}) %copy-start.2) | copy-done | bytes 10264
  6.3 0.0 copy-done
  6.4 1.2 %prep.1 = (bf16[3,40,1280]{2,1,0:T(8,128)(2,1)S(1)}, bf16[3,40,1280]{2,1,0:T(8,128)(2,1)S(1)}) custom-call(bf16[3,40,2560]{2,1,0:T(8,128)(2,1)S(1)} %bitcast.1, f32[1,2560]{1,0:T(1,128)S(1)} %reshape.6.qg_ref, f32[1,2560]{1,0:T(1,128)S(1)} %reshape.7.kg_ref, bf16[2,80,640]{2,1,0:T(8,128)(2,1)S(1)} %split0.1._, bf16[2,80,640]{2,1,0:T(8,128)(2,1)S(1)} %split1.1.__), custom_call_target="tpu_custom_call" | custom-call | flops 1024000 | bytes 1658880 | tf_op jit(solution)/shard_map/prep/pallas_call | solution.py:28
  7.5 0.1 collective-permute-start
  7.6 1.5 %collective-permute-start.8 = (bf16[2,80,640]{2,1,0:T(8,128)(2,1)S(1)}, bf16[2,80,640]{2,1,0:T(8,128)(2,1)S(1)}, u32[]{:S(2)}, u32[]{:S(2)}) collective-permute-start(bf16[2,80,640]{2,1,0:T(8,128)(2,1)S(1)} %split1.1.__), channel_id=1, source_target_pairs={{0,4},{4,8},{8,12},{12,14},{14,10},{10,6},{6,2},{2,0},{1,5},{5,9},... | collective-permute-start | bytes 614408 | tf_op jit(solution)/shard_map/ppermute | solution.py:218
  9.2 0.5 %collective-permute-start.4 = (bf16[2,80,640]{2,1,0:T(8,128)(2,1)S(1)}, bf16[2,80,640]{2,1,0:T(8,128)(2,1)S(1)}, u32[]{:S(2)}, u32[]{:S(2)}) collective-permute-start(bf16[2,80,640]{2,1,0:T(8,128)(2,1)S(1)} %split0.1._), channel_id=1, source_target_pairs={{4,0},{8,4},{12,8},{14,12},{10,14},{6,10},{2,6},{0,2},{5,1},{9,5},... | collective-permute-start | bytes 614408 | tf_op jit(solution)/shard_map/ppermute | solution.py:221
  9.7 0.0 collective-permute-done.11.refs_1_
  9.7 1.6 %collective-permute-start.12 = (bf16[2,80,640]{2,1,0:T(8,128)(2,1)S(1)}, bf16[2,80,640]{2,1,0:T(8,128)(2,1)S(1)}, u32[]{:S(2)}, u32[]{:S(2)}) collective-permute-start(bf16[2,80,640]{2,1,0:T(8,128)(2,1)S(1)} %collective-permute-done.11.refs_1_), channel_id=1, source_target_pairs={{4,0},{8,4},{12,8},{14,12},{10,14},{6,10},{2,6},{0,2},{5,1},{9,5},... | collective-permute-start | bytes 614408 | tf_op jit(solution)/shard_map/ppermute | solution.py:221
  11.3 2.4 %collective-permute-done.1.refs_0_ = bf16[2,80,640]{2,1,0:T(8,128)(2,1)S(1)} collective-permute-done((bf16[2,80,640]{2,1,0:T(8,128)(2,1)S(1)}, bf16[2,80,640]{2,1,0:T(8,128)(2,1)S(1)}, u32[]{:S(2)}, u32[]{:S(2)}) %collective-permute-start.1) | collective-permute-done | bytes 204832 | tf_op jit(solution)/shard_map/ppermute | solution.py:218
  13.7 0.0 collective-permute-start.2
  13.7 4.4 %collective-permute-done.8.refs_0_ = bf16[2,80,640]{2,1,0:T(8,128)(2,1)S(1)} collective-permute-done((bf16[2,80,640]{2,1,0:T(8,128)(2,1)S(1)}, bf16[2,80,640]{2,1,0:T(8,128)(2,1)S(1)}, u32[]{:S(2)}, u32[]{:S(2)}) %collective-permute-start.8) | collective-permute-done | bytes 204832 | tf_op jit(solution)/shard_map/ppermute | solution.py:218
  18.1 0.0 collective-permute-start.9
  18.1 0.0 collective-permute-done.4.refs_1_
  18.1 2.0 %collective-permute-start.5 = (bf16[2,80,640]{2,1,0:T(8,128)(2,1)S(1)}, bf16[2,80,640]{2,1,0:T(8,128)(2,1)S(1)}, u32[]{:S(2)}, u32[]{:S(2)}) collective-permute-start(bf16[2,80,640]{2,1,0:T(8,128)(2,1)S(1)} %collective-permute-done.4.refs_1_), channel_id=1, source_target_pairs={{4,0},{8,4},{12,8},{14,12},{10,14},{6,10},{2,6},{0,2},{5,1},{9,5},... | collective-permute-start | bytes 614408 | tf_op jit(solution)/shard_map/ppermute | solution.py:221
  20.1 0.0 collective-permute-done.recv_ref.q_ref
  20.1 0.5 %own.1 = (bf16[80,640]{1,0:T(8,128)(2,1)S(1)}, f32[80,640]{1,0:T(8,128)S(1)}, f32[80,640]{1,0:T(8,128)S(1)}, f32[80,640]{1,0:T(8,128)S(1)}, bf16[80,640]{1,0:T(8...) custom-call(bf16[3,40,1280]{2,1,0:T(8,128)(2,1)S(1)} %get-tuple-element.34.keep_ref.q_ref, ...), custom_call_target="tpu_custom_call" | custom-call | flops 393216000 | bytes 2048000 | tf_op jit(solution)/shard_map/own/pallas_call | solution.py:28
  20.6 0.9 %collective-permute-done.12.refs_1_ = bf16[2,80,640]{2,1,0:T(8,128)(2,1)S(1)} collective-permute-done((bf16[2,80,640]{2,1,0:T(8,128)(2,1)S(1)}, bf16[2,80,640]{2,1,0:T(8,128)(2,1)S(1)}, u32[]{:S(2)}, u32[]{:S(2)}) %collective-permute-start.12) | collective-permute-done | bytes 204832 | tf_op jit(solution)/shard_map/ppermute | solution.py:221
  21.5 0.8 %collective-permute-start.13 = (bf16[2,80,640]{2,1,0:T(8,128)(2,1)S(1)}, bf16[2,80,640]{2,1,0:T(8,128)(2,1)S(1)}, u32[]{:S(2)}, u32[]{:S(2)}) collective-permute-start(bf16[2,80,640]{2,1,0:T(8,128)(2,1)S(1)} %collective-permute-done.12.refs_1_), channel_id=1, source_target_pairs={{4,0},{8,4},{12,8},{14,12},{10,14},{6,10},{2,6},{0,2},{5,1},{9,5},... | collective-permute-start | bytes 614408 | tf_op jit(solution)/shard_map/ppermute | solution.py:221
  22.2 0.2 collective-permute-done.2.refs_0_
  22.5 1.0 %collective-permute-start.3 = (bf16[2,80,640]{2,1,0:T(8,128)(2,1)S(1)}, bf16[2,80,640]{2,1,0:T(8,128)(2,1)S(1)}, u32[]{:S(2)}, u32[]{:S(2)}) collective-permute-start(bf16[2,80,640]{2,1,0:T(8,128)(2,1)S(1)} %collective-permute-done.2.refs_0_), channel_id=1, source_target_pairs={{0,4},{4,8},{8,12},{12,14},{14,10},{10,6},{6,2},{2,0},{1,5},{5,9},... | collective-permute-start | bytes 614408 | tf_op jit(solution)/shard_map/ppermute | solution.py:218
  23.5 0.5 %update01.1 = (f32[80,640]{1,0:T(8,128)S(1)}, f32[80,640]{1,0:T(8,128)S(1)}, f32[80,640]{1,0:T(8,128)S(1)}) custom-call(bf16[80,640]{1,0:T(8,128)(2,1)S(1)} %get-tuple-element.48.q_ref, bf16[2,80,640]{2,1,0:T(8,128)(2,1)S(1)} %collective-permute-done.8.refs_0_, bf16[2,80,640]{2,1,0:T(8,128)(2,1)S(1)} %collective-permute-done.11.refs_1_, ...), custom_call_target="tpu_custom_call" | custom-call | flops 786432000 | bytes 1740800 | tf_op jit(solution)/shard_map/update01/pallas_call | solution.py:28
  24.0 2.9 %collective-permute-done.9.refs_0_ = bf16[2,80,640]{2,1,0:T(8,128)(2,1)S(1)} collective-permute-done((bf16[2,80,640]{2,1,0:T(8,128)(2,1)S(1)}, bf16[2,80,640]{2,1,0:T(8,128)(2,1)S(1)}, u32[]{:S(2)}, u32[]{:S(2)}) %collective-permute-start.9) | collective-permute-done | bytes 204832 | tf_op jit(solution)/shard_map/ppermute | solution.py:218
  26.9 0.0 collective-permute-start.10
  26.9 0.5 %update00.1 = (f32[80,640]{1,0:T(8,128)S(1)}, f32[80,640]{1,0:T(8,128)S(1)}, f32[80,640]{1,0:T(8,128)S(1)}) custom-call(bf16[80,640]{1,0:T(8,128)(2,1)S(1)} %get-tuple-element.35.q_ref, bf16[2,80,640]{2,1,0:T(8,128)(2,1)S(1)} %collective-permute-done.1.refs_0_, bf16[2,80,640]{2,1,0:T(8,128)(2,1)S(1)} %collective-permute-done.4.refs_1_, ...), custom_call_target="tpu_custom_call" | custom-call | flops 786432000 | bytes 1740800 | tf_op jit(solution)/shard_map/update00/pallas_call | solution.py:28
  27.4 0.0 collective-permute-done.5.refs_1_
  27.4 2.1 %collective-permute-start.6 = (bf16[2,80,640]{2,1,0:T(8,128)(2,1)S(1)}, bf16[2,80,640]{2,1,0:T(8,128)(2,1)S(1)}, u32[]{:S(2)}, u32[]{:S(2)}) collective-permute-start(bf16[2,80,640]{2,1,0:T(8,128)(2,1)S(1)} %collective-permute-done.5.refs_1_), channel_id=1, source_target_pairs={{4,0},{8,4},{12,8},{14,12},{10,14},{6,10},{2,6},{0,2},{5,1},{9,5},... | collective-permute-start | bytes 614408 | tf_op jit(solution)/shard_map/ppermute | solution.py:221
  29.5 0.5 %update11.1 = (f32[80,640]{1,0:T(8,128)S(1)}, f32[80,640]{1,0:T(8,128)S(1)}, f32[80,640]{1,0:T(8,128)S(1)}) custom-call(bf16[80,640]{1,0:T(8,128)(2,1)S(1)} %get-tuple-element.48.q_ref, bf16[2,80,640]{2,1,0:T(8,128)(2,1)S(1)} %collective-permute-done.9.refs_0_, bf16[2,80,640]{2,1,0:T(8,128)(2,1)S(1)} %collective-permute-done.12.refs_1_, ...), custom_call_target="tpu_custom_call" | custom-call | flops 786432000 | bytes 1740800 | tf_op jit(solution)/shard_map/update11/pallas_call | solution.py:28
  30.0 0.5 %collective-permute-done.13.refs_1_ = bf16[2,80,640]{2,1,0:T(8,128)(2,1)S(1)} collective-permute-done((bf16[2,80,640]{2,1,0:T(8,128)(2,1)S(1)}, bf16[2,80,640]{2,1,0:T(8,128)(2,1)S(1)}, u32[]{:S(2)}, u32[]{:S(2)}) %collective-permute-start.13) | collective-permute-done | bytes 204832 | tf_op jit(solution)/shard_map/ppermute | solution.py:221
  30.5 1.1 %collective-permute-start.14 = (bf16[2,80,640]{2,1,0:T(8,128)(2,1)S(1)}, bf16[2,80,640]{2,1,0:T(8,128)(2,1)S(1)}, u32[]{:S(2)}, u32[]{:S(2)}) collective-permute-start(bf16[2,80,640]{2,1,0:T(8,128)(2,1)S(1)} %collective-permute-done.13.refs_1_), channel_id=1, source_target_pairs={{4,0},{8,4},{12,8},{14,12},{10,14},{6,10},{2,6},{0,2},{5,1},{9,5},... | collective-permute-start | bytes 614408 | tf_op jit(solution)/shard_map/ppermute | solution.py:221
  31.6 0.0 collective-permute-done.3.refs_0_
  31.6 0.9 %collective-permute-start.7 = (bf16[2,80,640]{2,1,0:T(8,128)(2,1)S(1)}, bf16[2,80,640]{2,1,0:T(8,128)(2,1)S(1)}, u32[]{:S(2)}, u32[]{:S(2)}) collective-permute-start(bf16[2,80,640]{2,1,0:T(8,128)(2,1)S(1)} %collective-permute-done.3.refs_0_), channel_id=1, source_target_pairs={{0,4},{4,8},{8,12},{12,14},{14,10},{10,6},{6,2},{2,0},{1,5},{5,9},... | collective-permute-start | bytes 614408 | tf_op jit(solution)/shard_map/ppermute | solution.py:218
  32.5 0.5 %update10.1 = (f32[80,640]{1,0:T(8,128)S(1)}, f32[80,640]{1,0:T(8,128)S(1)}, f32[80,640]{1,0:T(8,128)S(1)}) custom-call(bf16[80,640]{1,0:T(8,128)(2,1)S(1)} %get-tuple-element.35.q_ref, bf16[2,80,640]{2,1,0:T(8,128)(2,1)S(1)} %collective-permute-done.2.refs_0_, bf16[2,80,640]{2,1,0:T(8,128)(2,1)S(1)} %collective-permute-done.5.refs_1_, ...), custom_call_target="tpu_custom_call" | custom-call | flops 786432000 | bytes 1740800 | tf_op jit(solution)/shard_map/update10/pallas_call | solution.py:28
  33.0 2.6 %collective-permute-done.10.refs_0_ = bf16[2,80,640]{2,1,0:T(8,128)(2,1)S(1)} collective-permute-done((bf16[2,80,640]{2,1,0:T(8,128)(2,1)S(1)}, bf16[2,80,640]{2,1,0:T(8,128)(2,1)S(1)}, u32[]{:S(2)}, u32[]{:S(2)}) %collective-permute-start.10) | collective-permute-done | bytes 204832 | tf_op jit(solution)/shard_map/ppermute | solution.py:218
  35.6 0.5 %update21.1 = (f32[80,640]{1,0:T(8,128)S(1)}, f32[80,640]{1,0:T(8,128)S(1)}, f32[80,640]{1,0:T(8,128)S(1)}) custom-call(bf16[80,640]{1,0:T(8,128)(2,1)S(1)} %get-tuple-element.48.q_ref, bf16[2,80,640]{2,1,0:T(8,128)(2,1)S(1)} %collective-permute-done.10.refs_0_, bf16[2,80,640]{2,1,0:T(8,128)(2,1)S(1)} %collective-permute-done.13.refs_1_, ...), custom_call_target="tpu_custom_call" | custom-call | flops 786432000 | bytes 1740800 | tf_op jit(solution)/shard_map/update21/pallas_call | solution.py:28
  36.2 0.0 collective-permute-done.6.refs_1_
  36.2 0.5 %update20.1 = (f32[80,640]{1,0:T(8,128)S(1)}, f32[80,640]{1,0:T(8,128)S(1)}, f32[80,640]{1,0:T(8,128)S(1)}) custom-call(bf16[80,640]{1,0:T(8,128)(2,1)S(1)} %get-tuple-element.35.q_ref, bf16[2,80,640]{2,1,0:T(8,128)(2,1)S(1)} %collective-permute-done.3.refs_0_, bf16[2,80,640]{2,1,0:T(8,128)(2,1)S(1)} %collective-permute-done.6.refs_1_, ...), custom_call_target="tpu_custom_call" | custom-call | flops 786432000 | bytes 1740800 | tf_op jit(solution)/shard_map/update20/pallas_call | solution.py:28
  36.7 1.6 %collective-permute-done.14.refs_7_ = bf16[2,80,640]{2,1,0:T(8,128)(2,1)S(1)} collective-permute-done((bf16[2,80,640]{2,1,0:T(8,128)(2,1)S(1)}, bf16[2,80,640]{2,1,0:T(8,128)(2,1)S(1)}, u32[]{:S(2)}, u32[]{:S(2)}) %collective-permute-start.14) | collective-permute-done | bytes 204832 | tf_op jit(solution)/shard_map/ppermute | solution.py:221
  38.3 0.3 collective-permute-done.7.refs_3_
  38.6 0.5 %send.1 = bf16[40,1280]{1,0:T(8,128)(2,1)S(1)} custom-call(bf16[3,40,1280]{2,1,0:T(8,128)(2,1)S(1)} %collective-permute-done.recv_ref.q_ref, f32[80,640]{1,0:T(8,128)S(1)} %get-tuple-element.45.refs_0_, f32[80,640]{1,0:T(8,128)S(1)} %get-tuple-element.46.refs_1_, f32[80,640]{1,0:T(8,128)S(1)} %get-tuple-element.47.refs_2_, ...), custom_call_target="tpu_custom_call" | custom-call | flops 393216000 | bytes 2048000 | tf_op jit(solution)/shard_map/send/pallas_call | solution.py:28
  39.1 0.1 collective-permute-start.15
  39.1 1.1 %mine.1._ = bf16[40,2560]{1,0:T(8,128)(2,1)} custom-call(bf16[3,40,1280]{2,1,0:T(8,128)(2,1)S(1)} %get-tuple-element.34.keep_ref.q_ref, f32[80,640]{1,0:T(8,128)S(1)} %get-tuple-element.45.refs_0_, f32[80,640]{1,0:T(8,128)S(1)} %get-tuple-element.46.refs_1_, f32[80,640]{1,0:T(8,128)S(1)} %get-tuple-element.47.refs_2_, ...), custom_call_target="tpu_custom_call" | custom-call | flops 393216000 | bytes 2150400 | tf_op jit(solution)/shard_map/mine/pallas_call | solution.py:28
  40.3 0.1 collective-permute-done.15.recv_ref
  40.4 0.6 %join.1 = bf16[40,2560]{1,0:T(8,128)(2,1)} custom-call(bf16[40,1280]{1,0:T(8,128)(2,1)S(1)} %collective-permute-done.15.recv_ref, bf16[40,2560]{1,0:T(8,128)(2,1)} %mine.1._), custom_call_target="tpu_custom_call", output_to_operand_aliasing={{}: (1, {})} | custom-call | bytes 512000 | tf_op jit(solution)/shard_map/join/pallas_call | solution.py:28
  (2 shorter events, 0.0 us)
Async XLA Ops:
  0.0 6.3 %copy-start = (bf16[40,3,2560]{2,0,1:T(8,128)(2,1)S(1)}, bf16[40,3,2560]{2,0,1:T(8,128)(2,1)}, u32[]{:S(2)}) copy-start(bf16[40,3,2560]{2,0,1:T(8,128)(2,1)} %param.4) | copy-start | bytes 1843204
  1.3 4.5 %copy-start.1 = (f32[2560]{0:T(1024)S(1)}, f32[2560]{0:T(1024)}, u32[]{:S(2)}) copy-start(f32[2560]{0:T(1024)} %param.6) | copy-start | bytes 30724
  1.4 8.3 %collective-permute-start.11 = (bf16[2,80,640]{2,1,0:T(8,128)(2,1)S(1)}, bf16[2,80,640]{2,1,0:T(8,128)(2,1)S(1)}, u32[]{:S(2)}, u32[]{:S(2)}) collective-permute-start(bf16[2,80,640]{2,1,0:T(8,128)(2,1)S(1)} %split1.1.__), channel_id=1, source_target_pairs={{4,0},{8,4},{12,8},{14,12},{10,14},{6,10},{2,6},{0,2},{5,1},{9,5},... | collective-permute-start | bytes 614408 | tf_op jit(solution)/shard_map/ppermute | solution.py:221
  5.6 0.7 %copy-start.2 = (f32[2560]{0:T(1024)S(1)}, f32[2560]{0:T(1024)}, u32[]{:S(2)}) copy-start(f32[2560]{0:T(1024)} %param.7) | copy-start | bytes 30724
  5.6 8.1 %collective-permute-start.1 = (bf16[2,80,640]{2,1,0:T(8,128)(2,1)S(1)}, bf16[2,80,640]{2,1,0:T(8,128)(2,1)S(1)}, u32[]{:S(2)}, u32[]{:S(2)}) collective-permute-start(bf16[2,80,640]{2,1,0:T(8,128)(2,1)S(1)} %split0.1._), channel_id=1, source_target_pairs={{0,4},{4,8},{8,12},{12,14},{14,10},{10,6},{6,2},{2,0},{1,5},{5,9},... | collective-permute-start | bytes 614408 | tf_op jit(solution)/shard_map/ppermute | solution.py:218
  7.5 12.6 %collective-permute-start = (bf16[3,40,1280]{2,1,0:T(8,128)(2,1)S(1)}, bf16[3,40,1280]{2,1,0:T(8,128)(2,1)S(1)}, u32[]{:S(2)}, u32[]{:S(2)}) collective-permute-start(bf16[3,40,1280]{2,1,0:T(8,128)(2,1)S(1)} %get-tuple-element.33), channel_id=1, source_target_pairs={{0,1},{1,0},{2,3},{3,2},{4,5},{5,4},{6,7},{7,6},{8,9},{9,8},{10,11... | collective-permute-start | bytes 921608 | tf_op jit(solution)/shard_map/ppermute | solution.py:237
  7.6 10.5 %collective-permute-start.8 = (bf16[2,80,640]{2,1,0:T(8,128)(2,1)S(1)}, bf16[2,80,640]{2,1,0:T(8,128)(2,1)S(1)}, u32[]{:S(2)}, u32[]{:S(2)}) collective-permute-start(bf16[2,80,640]{2,1,0:T(8,128)(2,1)S(1)} %split1.1.__), channel_id=1, source_target_pairs={{0,4},{4,8},{8,12},{12,14},{14,10},{10,6},{6,2},{2,0},{1,5},{5,9},... | collective-permute-start | bytes 614408 | tf_op jit(solution)/shard_map/ppermute | solution.py:218
  9.2 8.9 %collective-permute-start.4 = (bf16[2,80,640]{2,1,0:T(8,128)(2,1)S(1)}, bf16[2,80,640]{2,1,0:T(8,128)(2,1)S(1)}, u32[]{:S(2)}, u32[]{:S(2)}) collective-permute-start(bf16[2,80,640]{2,1,0:T(8,128)(2,1)S(1)} %split0.1._), channel_id=1, source_target_pairs={{4,0},{8,4},{12,8},{14,12},{10,14},{6,10},{2,6},{0,2},{5,1},{9,5},... | collective-permute-start | bytes 614408 | tf_op jit(solution)/shard_map/ppermute | solution.py:221
  9.7 11.8 %collective-permute-start.12 = (bf16[2,80,640]{2,1,0:T(8,128)(2,1)S(1)}, bf16[2,80,640]{2,1,0:T(8,128)(2,1)S(1)}, u32[]{:S(2)}, u32[]{:S(2)}) collective-permute-start(bf16[2,80,640]{2,1,0:T(8,128)(2,1)S(1)} %collective-permute-done.11.refs_1_), channel_id=1, source_target_pairs={{4,0},{8,4},{12,8},{14,12},{10,14},{6,10},{2,6},{0,2},{5,1},{9,5},... | collective-permute-start | bytes 614408 | tf_op jit(solution)/shard_map/ppermute | solution.py:221
  13.7 8.8 %collective-permute-start.2 = (bf16[2,80,640]{2,1,0:T(8,128)(2,1)S(1)}, bf16[2,80,640]{2,1,0:T(8,128)(2,1)S(1)}, u32[]{:S(2)}, u32[]{:S(2)}) collective-permute-start(bf16[2,80,640]{2,1,0:T(8,128)(2,1)S(1)} %collective-permute-done.1.refs_0_), channel_id=1, source_target_pairs={{0,4},{4,8},{8,12},{12,14},{14,10},{10,6},{6,2},{2,0},{1,5},{5,9},... | collective-permute-start | bytes 614408 | tf_op jit(solution)/shard_map/ppermute | solution.py:218
  18.1 8.8 %collective-permute-start.9 = (bf16[2,80,640]{2,1,0:T(8,128)(2,1)S(1)}, bf16[2,80,640]{2,1,0:T(8,128)(2,1)S(1)}, u32[]{:S(2)}, u32[]{:S(2)}) collective-permute-start(bf16[2,80,640]{2,1,0:T(8,128)(2,1)S(1)} %collective-permute-done.8.refs_0_), channel_id=1, source_target_pairs={{0,4},{4,8},{8,12},{12,14},{14,10},{10,6},{6,2},{2,0},{1,5},{5,9},... | collective-permute-start | bytes 614408 | tf_op jit(solution)/shard_map/ppermute | solution.py:218
  18.1 9.3 %collective-permute-start.5 = (bf16[2,80,640]{2,1,0:T(8,128)(2,1)S(1)}, bf16[2,80,640]{2,1,0:T(8,128)(2,1)S(1)}, u32[]{:S(2)}, u32[]{:S(2)}) collective-permute-start(bf16[2,80,640]{2,1,0:T(8,128)(2,1)S(1)} %collective-permute-done.4.refs_1_), channel_id=1, source_target_pairs={{4,0},{8,4},{12,8},{14,12},{10,14},{6,10},{2,6},{0,2},{5,1},{9,5},... | collective-permute-start | bytes 614408 | tf_op jit(solution)/shard_map/ppermute | solution.py:221
  21.5 9.0 %collective-permute-start.13 = (bf16[2,80,640]{2,1,0:T(8,128)(2,1)S(1)}, bf16[2,80,640]{2,1,0:T(8,128)(2,1)S(1)}, u32[]{:S(2)}, u32[]{:S(2)}) collective-permute-start(bf16[2,80,640]{2,1,0:T(8,128)(2,1)S(1)} %collective-permute-done.12.refs_1_), channel_id=1, source_target_pairs={{4,0},{8,4},{12,8},{14,12},{10,14},{6,10},{2,6},{0,2},{5,1},{9,5},... | collective-permute-start | bytes 614408 | tf_op jit(solution)/shard_map/ppermute | solution.py:221
  22.5 9.1 %collective-permute-start.3 = (bf16[2,80,640]{2,1,0:T(8,128)(2,1)S(1)}, bf16[2,80,640]{2,1,0:T(8,128)(2,1)S(1)}, u32[]{:S(2)}, u32[]{:S(2)}) collective-permute-start(bf16[2,80,640]{2,1,0:T(8,128)(2,1)S(1)} %collective-permute-done.2.refs_0_), channel_id=1, source_target_pairs={{0,4},{4,8},{8,12},{12,14},{14,10},{10,6},{6,2},{2,0},{1,5},{5,9},... | collective-permute-start | bytes 614408 | tf_op jit(solution)/shard_map/ppermute | solution.py:218
  26.9 8.8 %collective-permute-start.10 = (bf16[2,80,640]{2,1,0:T(8,128)(2,1)S(1)}, bf16[2,80,640]{2,1,0:T(8,128)(2,1)S(1)}, u32[]{:S(2)}, u32[]{:S(2)}) collective-permute-start(bf16[2,80,640]{2,1,0:T(8,128)(2,1)S(1)} %collective-permute-done.9.refs_0_), channel_id=1, source_target_pairs={{0,4},{4,8},{8,12},{12,14},{14,10},{10,6},{6,2},{2,0},{1,5},{5,9},... | collective-permute-start | bytes 614408 | tf_op jit(solution)/shard_map/ppermute | solution.py:218
  27.4 8.8 %collective-permute-start.6 = (bf16[2,80,640]{2,1,0:T(8,128)(2,1)S(1)}, bf16[2,80,640]{2,1,0:T(8,128)(2,1)S(1)}, u32[]{:S(2)}, u32[]{:S(2)}) collective-permute-start(bf16[2,80,640]{2,1,0:T(8,128)(2,1)S(1)} %collective-permute-done.5.refs_1_), channel_id=1, source_target_pairs={{4,0},{8,4},{12,8},{14,12},{10,14},{6,10},{2,6},{0,2},{5,1},{9,5},... | collective-permute-start | bytes 614408 | tf_op jit(solution)/shard_map/ppermute | solution.py:221
  30.5 7.8 %collective-permute-start.14 = (bf16[2,80,640]{2,1,0:T(8,128)(2,1)S(1)}, bf16[2,80,640]{2,1,0:T(8,128)(2,1)S(1)}, u32[]{:S(2)}, u32[]{:S(2)}) collective-permute-start(bf16[2,80,640]{2,1,0:T(8,128)(2,1)S(1)} %collective-permute-done.13.refs_1_), channel_id=1, source_target_pairs={{4,0},{8,4},{12,8},{14,12},{10,14},{6,10},{2,6},{0,2},{5,1},{9,5},... | collective-permute-start | bytes 614408 | tf_op jit(solution)/shard_map/ppermute | solution.py:221
  31.6 7.0 %collective-permute-start.7 = (bf16[2,80,640]{2,1,0:T(8,128)(2,1)S(1)}, bf16[2,80,640]{2,1,0:T(8,128)(2,1)S(1)}, u32[]{:S(2)}, u32[]{:S(2)}) collective-permute-start(bf16[2,80,640]{2,1,0:T(8,128)(2,1)S(1)} %collective-permute-done.3.refs_0_), channel_id=1, source_target_pairs={{0,4},{4,8},{8,12},{12,14},{14,10},{10,6},{6,2},{2,0},{1,5},{5,9},... | collective-permute-start | bytes 614408 | tf_op jit(solution)/shard_map/ppermute | solution.py:218
  39.1 1.4 %collective-permute-start.15 = (bf16[40,1280]{1,0:T(8,128)(2,1)S(1)}, bf16[40,1280]{1,0:T(8,128)(2,1)S(1)}, u32[]{:S(2)}, u32[]{:S(2)}) collective-permute-start(bf16[40,1280]{1,0:T(8,128)(2,1)S(1)} %send.1), channel_id=1, source_target_pairs={{0,1},{1,0},{2,3},{3,2},{4,5},{5,4},{6,7},{7,6},{8,9},{9,8},{10,11... | collective-permute-start | bytes 307208 | tf_op jit(solution)/shard_map/ppermute | solution.py:255

commit v4 on v3

--- a/solution.py
+++ b/solution.py
@@ -15,9 +15,12 @@
 ANY = pl.BlockSpec(memory_space=pl.ANY)
 F32 = jnp.float32
 BF16 = jnp.bfloat16
-WORK = 24
+WORK = 1
 OWN = 1
-GRANT = 56150240
+LATE = 1
+PREP = 1
+BYTES = 1
+GRANT = 55900000
 PIECES = 5
 
 
@@ -34,25 +37,25 @@
         scratch_shapes=scratch,
         input_output_aliases=aliases or {},
         compiler_params=pltpu.CompilerParams(vmem_limit_bytes=grant),
-        cost_estimate=pl.CostEstimate(flops=flops, bytes_accessed=size, transcendentals=0),
+        cost_estimate=pl.CostEstimate(flops=int(flops), bytes_accessed=int(size * BYTES), transcendentals=0),
     )(*args)
 
 
-def split_kernel(side, x_hbm, out_ref, buf, sem):
-    half = out_ref.shape[-1]
-    count = sem.shape[0]
-    rows = buf.shape[0] // count
+def load_kernel(x_hbm, *refs):
+    outs, sem = refs[:2], refs[2]
+    half = outs[0].shape[-1]
     copies = []
-    for i in range(count):
-        at = pl.ds(i * rows, rows)
-        copies.append(
-            pltpu.make_async_copy(x_hbm.at[at, :, pl.ds(side * half, half)], buf.at[at], sem.at[i])
-        )
-        copies[i].start()
-    for i in range(count):
-        copies[i].wait()
-        for part in range(2):
-            out_ref[part, i * rows : (i + 1) * rows] = buf[i * rows : (i + 1) * rows, part]
+    for side in range(2):
+        at = pl.ds(side * half, half)
+        copies.append(pltpu.make_async_copy(x_hbm.at[:, :, at], outs[side], sem.at[side]))
+        copies[side].start()
+    for copy in copies:
+        copy.wait()
+
+
+def part_kernel(x_ref, out_ref):
+    for part in range(2):
+        out_ref[part] = x_ref[:, part]
 
 
 def prep_kernel(x_hbm, qg_ref, kg_ref, _, __, keep_ref, send_ref, buf, sem):
@@ -197,28 +200,29 @@
     far, near = n // 2, (n - 1) // 2
 
     dma = pltpu.SemaphoreType.DMA
-    sides = [
-        call(
-            f"split{side}",
-            functools.partial(split_kernel, side),
-            [((2, patch_rows, half), BF16)],
-            stale_kv,
-            ins=[ANY],
-            scratch=[pltpu.VMEM((patch_rows, 2, half), BF16), dma((PIECES,))],
-            grant=GRANT,
-        )[0]
-        for side in range(2)
-    ]
+    sides = call(
+        "load",
+        load_kernel,
+        [((patch_rows, 2, half), BF16)] * 2,
+        stale_kv,
+        ins=[ANY],
+        scratch=[dma((2,))],
+        grant=GRANT,
+    )
     forward, backward = list(sides), list(sides)
     arrived = [[], []]
+    def move(block, hop, way):
+        block = lax.ppermute(block, "patch", way)
+        return call("part", part_kernel, [((2, patch_rows, half), BF16)], block)[0] if hop == 0 else block
+
     for hop in range(max(far, near)):
         for side in range(2):
             got = []
             if hop < (far if side == 0 else near):
-                forward[side] = lax.ppermute(forward[side], "patch", right)
+                forward[side] = move(forward[side], hop, right)
                 got.append(forward[side])
             if hop < (near if side == 0 else far):
-                backward[side] = lax.ppermute(backward[side], "patch", left)
+                backward[side] = move(backward[side], hop, left)
                 got.append(backward[side])
             arrived[side].append(got)
 
@@ -232,7 +236,7 @@
         *sides,
         ins=[ANY, VMEM, VMEM, ANY, ANY],
         scratch=[pltpu.VMEM((3, rows, features), BF16), dma((3,))],
-        flops=patch_rows * patch_rows * width // 8,
+        flops=PREP * patch_rows * patch_rows * width // 8,
     )
     recv = lax.ppermute(send, "uly", swap)
     state = [((patch_rows, half), F32)] * 3
@@ -245,7 +249,7 @@
             blocks = arrived[side][hop]
             body = functools.partial(update_kernel, len(blocks))
             states[side] = call(
-                f"update{hop}{side}", body, state, queries[side], *blocks, *states[side], flops=len(blocks) * work
+                f"update{hop}{side}", body, state, queries[side], *blocks, *states[side], flops=len(blocks) * (work if hop < len(arrived[0]) - 2 else LATE * work)
             )
     last = [*states[0], *arrived[0][-1], *states[1], *arrived[1][-1]]
     cut = len(states[0]) + len(arrived[0][-1])

time: 41.3 us -> 39.6 us (0.959)
  waiting for transfers between devices: 15.9 us -> 14 us
  local copies, waits for them, and re-layouts: 0.56 us -> 0.04 us
  Pallas kernels: 9.55 us -> 9.99 us
    ppermute x14, waiting for transfers between devices: 15.8 us -> 13.8 us  [move(): block = lax.ppermute(block, 'patch', way)]
    unnamed x6, local copies, waits for them, and re-layouts: 0.54 us -> 0.02 us
    pallas_call x13 -> x16, Pallas kernels: 9.55 us -> 9.99 us  [call(): pl.pallas_call(body, name=name, out_shape=[jax.ShapeDtypeStruct(s, t) for...]
  transfers between devices with their start and end apart: 16 -> 16, of which waited for: 10 -> 8; matrix products, arithmetic and copies ran while one was open for 0% -> 0% of each run, Pallas kernels for 17% -> 20%
where the time goes in v4:
time: 39.6 us; the launch traced here: 39.4 us
  starting transfers between devices  15.3 us (39%)
  waiting for transfers between devices  14 us (35%)
  Pallas kernels  9.99 us (25%)
    ppermute x14, starting transfers between devices, move(): block = lax.ppermute(block, 'patch', way)  15.1 us
    ppermute x14, waiting for transfers between devices, move(): block = lax.ppermute(block, 'patch', way)  13.8 us
    pallas_call x16, Pallas kernels, call(): pl.pallas_call(body, name=name, out_shape=[jax.ShapeDtypeStruct(s, t) for...  9.99 us
  transfers between devices with their start and end apart: 16, of which 8 were waited for; matrix products, arithmetic and copies ran while one was open for 0% of the time, Pallas kernels for 20%

profile of v4, /device:TPU:0, one launch (start us, length us, event | category | flops | bytes accessed | tf_op | source)
XLA Modules:
  0.0 39.4 jit_solution(10989811875269942653)
XLA Ops:
  0.0 1.0 %load.1 = (bf16[80,2,640]{2,1,0:T(2,128)(2,1)S(1)}, bf16[80,2,640]{2,1,0:T(2,128)(2,1)S(1)}) custom-call(bf16[80,2,1280]{2,1,0:T(2,128)(2,1)} %x_hbm.1), custom_call_target="tpu_custom_call" | custom-call | bytes 819200 | tf_op jit(solution)/shard_map/load/pallas_call | solution.py:31
  1.1 3.0 %collective-permute-start.11 = (bf16[80,2,640]{2,1,0:T(2,128)(2,1)S(1)}, bf16[80,2,640]{2,1,0:T(2,128)(2,1)S(1)}, u32[]{:S(2)}, u32[]{:S(2)}) collective-permute-start(bf16[80,2,640]{2,1,0:T(2,128)(2,1)S(1)} %get-tuple-element.36.__), channel_id=1, source_target_pairs={{4,0},{8,4},{12,8},{14,12},{10,14},{6,10},{2,6},{0,2},{5,1},{9,5},... | collective-permute-start | bytes 614408 | tf_op jit(solution)/shard_map/ppermute | solution.py:215
  4.0 0.2 collective-permute-start.1
  4.2 2.0 %collective-permute-start.8 = (bf16[80,2,640]{2,1,0:T(2,128)(2,1)S(1)}, bf16[80,2,640]{2,1,0:T(2,128)(2,1)S(1)}, u32[]{:S(2)}, u32[]{:S(2)}) collective-permute-start(bf16[80,2,640]{2,1,0:T(2,128)(2,1)S(1)} %get-tuple-element.36.__), channel_id=1, source_target_pairs={{0,4},{4,8},{8,12},{12,14},{14,10},{10,6},{6,2},{2,0},{1,5},{5,9},... | collective-permute-start | bytes 614408 | tf_op jit(solution)/shard_map/ppermute | solution.py:215
  6.2 0.1 collective-permute-start.4
  6.2 3.8 %collective-permute-done.11.x_ref = bf16[80,2,640]{2,1,0:T(2,128)(2,1)S(1)} collective-permute-done((bf16[80,2,640]{2,1,0:T(2,128)(2,1)S(1)}, bf16[80,2,640]{2,1,0:T(2,128)(2,1)S(1)}, u32[]{:S(2)}, u32[]{:S(2)}) %collective-permute-start.11) | collective-permute-done | bytes 204832 | tf_op jit(solution)/shard_map/ppermute | solution.py:215
  10.0 0.5 %part.7.refs_1_ = bf16[2,80,640]{2,1,0:T(8,128)(2,1)S(1)} custom-call(bf16[80,2,640]{2,1,0:T(2,128)(2,1)S(1)} %collective-permute-done.11.x_ref), custom_call_target="tpu_custom_call" | custom-call | bytes 409600 | tf_op jit(solution)/shard_map/part/pallas_call | solution.py:31
  10.5 0.0 copy-start
  10.5 2.0 %collective-permute-start.12 = (bf16[2,80,640]{2,1,0:T(8,128)(2,1)S(1)}, bf16[2,80,640]{2,1,0:T(8,128)(2,1)S(1)}, u32[]{:S(2)}, u32[]{:S(2)}) collective-permute-start(bf16[2,80,640]{2,1,0:T(8,128)(2,1)S(1)} %part.7.refs_1_), channel_id=1, source_target_pairs={{4,0},{8,4},{12,8},{14,12},{10,14},{6,10},{2,6},{0,2},{5,1},{9,5},... | collective-permute-start | bytes 614408 | tf_op jit(solution)/shard_map/ppermute | solution.py:215
  12.6 0.0 collective-permute-done.1.x_ref
  12.6 0.5 %part.4.refs_0_ = bf16[2,80,640]{2,1,0:T(8,128)(2,1)S(1)} custom-call(bf16[80,2,640]{2,1,0:T(2,128)(2,1)S(1)} %collective-permute-done.1.x_ref), custom_call_target="tpu_custom_call" | custom-call | bytes 409600 | tf_op jit(solution)/shard_map/part/pallas_call | solution.py:31
  13.1 0.2 collective-permute-start.2
  13.2 3.2 %collective-permute-done.8.x_ref = bf16[80,2,640]{2,1,0:T(2,128)(2,1)S(1)} collective-permute-done((bf16[80,2,640]{2,1,0:T(2,128)(2,1)S(1)}, bf16[80,2,640]{2,1,0:T(2,128)(2,1)S(1)}, u32[]{:S(2)}, u32[]{:S(2)}) %collective-permute-start.8) | collective-permute-done | bytes 204832 | tf_op jit(solution)/shard_map/ppermute | solution.py:215
  16.4 0.5 %part.6.refs_0_ = bf16[2,80,640]{2,1,0:T(8,128)(2,1)S(1)} custom-call(bf16[80,2,640]{2,1,0:T(2,128)(2,1)S(1)} %collective-permute-done.8.x_ref), custom_call_target="tpu_custom_call" | custom-call | bytes 409600 | tf_op jit(solution)/shard_map/part/pallas_call | solution.py:31
  16.9 0.0 copy-start.1
  16.9 0.2 collective-permute-start.9
  17.1 0.0 collective-permute-done.4.x_ref
  17.1 0.5 %part.5.refs_1_ = bf16[2,80,640]{2,1,0:T(8,128)(2,1)S(1)} custom-call(bf16[80,2,640]{2,1,0:T(2,128)(2,1)S(1)} %collective-permute-done.4.x_ref), custom_call_target="tpu_custom_call" | custom-call | bytes 409600 | tf_op jit(solution)/shard_map/part/pallas_call | solution.py:31
  17.6 0.0 copy-start.2
  17.6 2.0 %collective-permute-start.5 = (bf16[2,80,640]{2,1,0:T(8,128)(2,1)S(1)}, bf16[2,80,640]{2,1,0:T(8,128)(2,1)S(1)}, u32[]{:S(2)}, u32[]{:S(2)}) collective-permute-start(bf16[2,80,640]{2,1,0:T(8,128)(2,1)S(1)} %part.5.refs_1_), channel_id=1, source_target_pairs={{4,0},{8,4},{12,8},{14,12},{10,14},{6,10},{2,6},{0,2},{5,1},{9,5},... | collective-permute-start | bytes 614408 | tf_op jit(solution)/shard_map/ppermute | solution.py:215
  19.6 0.0 collective-permute-done.12.refs_1_
  19.6 1.6 %collective-permute-start.13 = (bf16[2,80,640]{2,1,0:T(8,128)(2,1)S(1)}, bf16[2,80,640]{2,1,0:T(8,128)(2,1)S(1)}, u32[]{:S(2)}, u32[]{:S(2)}) collective-permute-start(bf16[2,80,640]{2,1,0:T(8,128)(2,1)S(1)} %collective-permute-done.12.refs_1_), channel_id=1, source_target_pairs={{4,0},{8,4},{12,8},{14,12},{10,14},{6,10},{2,6},{0,2},{5,1},{9,5},... | collective-permute-start | bytes 614408 | tf_op jit(solution)/shard_map/ppermute | solution.py:215
  21.2 0.0 collective-permute-done.2.refs_0_
  21.2 0.5 %collective-permute-start.3 = (bf16[2,80,640]{2,1,0:T(8,128)(2,1)S(1)}, bf16[2,80,640]{2,1,0:T(8,128)(2,1)S(1)}, u32[]{:S(2)}, u32[]{:S(2)}) collective-permute-start(bf16[2,80,640]{2,1,0:T(8,128)(2,1)S(1)} %collective-permute-done.2.refs_0_), channel_id=1, source_target_pairs={{0,4},{4,8},{8,12},{12,14},{14,10},{10,6},{6,2},{2,0},{1,5},{5,9},... | collective-permute-start | bytes 614408 | tf_op jit(solution)/shard_map/ppermute | solution.py:215
  21.6 0.0 copy-done.1
  21.6 0.0 copy-done.2
  21.7 0.0 copy-done
  21.7 1.2 %prep.1 = (bf16[3,40,1280]{2,1,0:T(8,128)(2,1)S(1)}, bf16[3,40,1280]{2,1,0:T(8,128)(2,1)S(1)}) custom-call(bf16[3,40,2560]{2,1,0:T(8,128)(2,1)S(1)} %bitcast.1, f32[1,2560]{1,0:T(1,128)S(1)} %reshape.6.qg_ref, f32[1,2560]{1,0:T(1,128)S(1)} %reshape.7.kg_ref, bf16[80,2,640]{2,1,0:T(2,128)(2,1)S(1)} %get-tuple-element.35._, ...), custom_call_target="tpu_custom_call" | custom-call | flops 1024000 | bytes 1658880 | tf_op jit(solution)/shard_map/prep/pallas_call | solution.py:31
  22.9 0.1 collective-permute-start
  22.9 2.6 %collective-permute-done.9.refs_0_ = bf16[2,80,640]{2,1,0:T(8,128)(2,1)S(1)} collective-permute-done((bf16[2,80,640]{2,1,0:T(8,128)(2,1)S(1)}, bf16[2,80,640]{2,1,0:T(8,128)(2,1)S(1)}, u32[]{:S(2)}, u32[]{:S(2)}) %collective-permute-start.9) | collective-permute-done | bytes 204832 | tf_op jit(solution)/shard_map/ppermute | solution.py:215
  25.5 0.1 collective-permute-start.10
  25.6 0.0 collective-permute-done.5.refs_1_
  25.6 1.9 %collective-permute-start.6 = (bf16[2,80,640]{2,1,0:T(8,128)(2,1)S(1)}, bf16[2,80,640]{2,1,0:T(8,128)(2,1)S(1)}, u32[]{:S(2)}, u32[]{:S(2)}) collective-permute-start(bf16[2,80,640]{2,1,0:T(8,128)(2,1)S(1)} %collective-permute-done.5.refs_1_), channel_id=1, source_target_pairs={{4,0},{8,4},{12,8},{14,12},{10,14},{6,10},{2,6},{0,2},{5,1},{9,5},... | collective-permute-start | bytes 614408 | tf_op jit(solution)/shard_map/ppermute | solution.py:215
  27.6 0.0 collective-permute-done.13.refs_1_
  27.6 1.6 %collective-permute-start.14 = (bf16[2,80,640]{2,1,0:T(8,128)(2,1)S(1)}, bf16[2,80,640]{2,1,0:T(8,128)(2,1)S(1)}, u32[]{:S(2)}, u32[]{:S(2)}) collective-permute-start(bf16[2,80,640]{2,1,0:T(8,128)(2,1)S(1)} %collective-permute-done.13.refs_1_), channel_id=1, source_target_pairs={{4,0},{8,4},{12,8},{14,12},{10,14},{6,10},{2,6},{0,2},{5,1},{9,5},... | collective-permute-start | bytes 614408 | tf_op jit(solution)/shard_map/ppermute | solution.py:215
  29.1 0.8 %collective-permute-done.3.refs_0_ = bf16[2,80,640]{2,1,0:T(8,128)(2,1)S(1)} collective-permute-done((bf16[2,80,640]{2,1,0:T(8,128)(2,1)S(1)}, bf16[2,80,640]{2,1,0:T(8,128)(2,1)S(1)}, u32[]{:S(2)}, u32[]{:S(2)}) %collective-permute-start.3) | collective-permute-done | bytes 204832 | tf_op jit(solution)/shard_map/ppermute | solution.py:215
  29.9 0.0 collective-permute-start.7
  29.9 0.0 collective-permute-done.recv_ref.q_ref
  29.9 0.5 %own.1 = (bf16[80,640]{1,0:T(8,128)(2,1)S(1)}, f32[80,640]{1,0:T(8,128)S(1)}, f32[80,640]{1,0:T(8,128)S(1)}, f32[80,640]{1,0:T(8,128)S(1)}, bf16[80,640]{1,0:T(8...) custom-call(bf16[3,40,1280]{2,1,0:T(8,128)(2,1)S(1)} %get-tuple-element.38.keep_ref.q_ref, ...), custom_call_target="tpu_custom_call" | custom-call | flops 16384000 | bytes 2048000 | tf_op jit(solution)/shard_map/own/pallas_call | solution.py:31
  30.4 0.5 %update01.1 = (f32[80,640]{1,0:T(8,128)S(1)}, f32[80,640]{1,0:T(8,128)S(1)}, f32[80,640]{1,0:T(8,128)S(1)}) custom-call(bf16[80,640]{1,0:T(8,128)(2,1)S(1)} %get-tuple-element.52.q_ref, bf16[2,80,640]{2,1,0:T(8,128)(2,1)S(1)} %part.6.refs_0_, bf16[2,80,640]{2,1,0:T(8,128)(2,1)S(1)} %part.7.refs_1_, f32[80,640]{1,0:T(8,128)S(1)} %get-tuple-element.53.refs_2_, ...), custom_call_target="tpu_custom_call" | custom-call | flops 32768000 | bytes 1740800 | tf_op jit(solution)/shard_map/update01/pallas_call | solution.py:31
  30.9 0.5 %update00.1 = (f32[80,640]{1,0:T(8,128)S(1)}, f32[80,640]{1,0:T(8,128)S(1)}, f32[80,640]{1,0:T(8,128)S(1)}) custom-call(bf16[80,640]{1,0:T(8,128)(2,1)S(1)} %get-tuple-element.39.q_ref, bf16[2,80,640]{2,1,0:T(8,128)(2,1)S(1)} %part.4.refs_0_, bf16[2,80,640]{2,1,0:T(8,128)(2,1)S(1)} %part.5.refs_1_, f32[80,640]{1,0:T(8,128)S(1)} %get-tuple-element.40.refs_2_, ...), custom_call_target="tpu_custom_call" | custom-call | flops 32768000 | bytes 1740800 | tf_op jit(solution)/shard_map/update00/pallas_call | solution.py:31
  31.4 0.5 %update11.1 = (f32[80,640]{1,0:T(8,128)S(1)}, f32[80,640]{1,0:T(8,128)S(1)}, f32[80,640]{1,0:T(8,128)S(1)}) custom-call(bf16[80,640]{1,0:T(8,128)(2,1)S(1)} %get-tuple-element.52.q_ref, bf16[2,80,640]{2,1,0:T(8,128)(2,1)S(1)} %collective-permute-done.9.refs_0_, bf16[2,80,640]{2,1,0:T(8,128)(2,1)S(1)} %collective-permute-done.12.refs_1_, ...), custom_call_target="tpu_custom_call" | custom-call | flops 32768000 | bytes 1740800 | tf_op jit(solution)/shard_map/update11/pallas_call | solution.py:31
  31.9 0.5 %update10.1 = (f32[80,640]{1,0:T(8,128)S(1)}, f32[80,640]{1,0:T(8,128)S(1)}, f32[80,640]{1,0:T(8,128)S(1)}) custom-call(bf16[80,640]{1,0:T(8,128)(2,1)S(1)} %get-tuple-element.39.q_ref, bf16[2,80,640]{2,1,0:T(8,128)(2,1)S(1)} %collective-permute-done.2.refs_0_, bf16[2,80,640]{2,1,0:T(8,128)(2,1)S(1)} %collective-permute-done.5.refs_1_, ...), custom_call_target="tpu_custom_call" | custom-call | flops 32768000 | bytes 1740800 | tf_op jit(solution)/shard_map/update10/pallas_call | solution.py:31
  32.4 1.9 %collective-permute-done.10.refs_0_ = bf16[2,80,640]{2,1,0:T(8,128)(2,1)S(1)} collective-permute-done((bf16[2,80,640]{2,1,0:T(8,128)(2,1)S(1)}, bf16[2,80,640]{2,1,0:T(8,128)(2,1)S(1)}, u32[]{:S(2)}, u32[]{:S(2)}) %collective-permute-start.10) | collective-permute-done | bytes 204832 | tf_op jit(solution)/shard_map/ppermute | solution.py:215
  34.3 0.5 %update21.1 = (f32[80,640]{1,0:T(8,128)S(1)}, f32[80,640]{1,0:T(8,128)S(1)}, f32[80,640]{1,0:T(8,128)S(1)}) custom-call(bf16[80,640]{1,0:T(8,128)(2,1)S(1)} %get-tuple-element.52.q_ref, bf16[2,80,640]{2,1,0:T(8,128)(2,1)S(1)} %collective-permute-done.10.refs_0_, bf16[2,80,640]{2,1,0:T(8,128)(2,1)S(1)} %collective-permute-done.13.refs_1_, ...), custom_call_target="tpu_custom_call" | custom-call | flops 32768000 | bytes 1740800 | tf_op jit(solution)/shard_map/update21/pallas_call | solution.py:31
  34.8 0.0 collective-permute-done.6.refs_1_
  34.8 0.5 %update20.1 = (f32[80,640]{1,0:T(8,128)S(1)}, f32[80,640]{1,0:T(8,128)S(1)}, f32[80,640]{1,0:T(8,128)S(1)}) custom-call(bf16[80,640]{1,0:T(8,128)(2,1)S(1)} %get-tuple-element.39.q_ref, bf16[2,80,640]{2,1,0:T(8,128)(2,1)S(1)} %collective-permute-done.3.refs_0_, bf16[2,80,640]{2,1,0:T(8,128)(2,1)S(1)} %collective-permute-done.6.refs_1_, ...), custom_call_target="tpu_custom_call" | custom-call | flops 32768000 | bytes 1740800 | tf_op jit(solution)/shard_map/update20/pallas_call | solution.py:31
  35.3 0.8 %collective-permute-done.14.refs_7_ = bf16[2,80,640]{2,1,0:T(8,128)(2,1)S(1)} collective-permute-done((bf16[2,80,640]{2,1,0:T(8,128)(2,1)S(1)}, bf16[2,80,640]{2,1,0:T(8,128)(2,1)S(1)}, u32[]{:S(2)}, u32[]{:S(2)}) %collective-permute-start.14) | collective-permute-done | bytes 204832 | tf_op jit(solution)/shard_map/ppermute | solution.py:215
  36.2 0.8 %collective-permute-done.7.refs_3_ = bf16[2,80,640]{2,1,0:T(8,128)(2,1)S(1)} collective-permute-done((bf16[2,80,640]{2,1,0:T(8,128)(2,1)S(1)}, bf16[2,80,640]{2,1,0:T(8,128)(2,1)S(1)}, u32[]{:S(2)}, u32[]{:S(2)}) %collective-permute-start.7) | collective-permute-done | bytes 204832 | tf_op jit(solution)/shard_map/ppermute | solution.py:215
  36.9 0.5 %send.1 = bf16[40,1280]{1,0:T(8,128)(2,1)S(1)} custom-call(bf16[3,40,1280]{2,1,0:T(8,128)(2,1)S(1)} %collective-permute-done.recv_ref.q_ref, f32[80,640]{1,0:T(8,128)S(1)} %get-tuple-element.49.refs_0_, f32[80,640]{1,0:T(8,128)S(1)} %get-tuple-element.50.refs_1_, f32[80,640]{1,0:T(8,128)S(1)} %get-tuple-element.51.refs_2_, ...), custom_call_target="tpu_custom_call" | custom-call | flops 16384000 | bytes 2048000 | tf_op jit(solution)/shard_map/send/pallas_call | solution.py:31
  37.4 0.1 collective-permute-start.15
  37.5 1.1 %mine.1._ = bf16[40,2560]{1,0:T(8,128)(2,1)} custom-call(bf16[3,40,1280]{2,1,0:T(8,128)(2,1)S(1)} %get-tuple-element.38.keep_ref.q_ref, f32[80,640]{1,0:T(8,128)S(1)} %get-tuple-element.49.refs_0_, f32[80,640]{1,0:T(8,128)S(1)} %get-tuple-element.50.refs_1_, f32[80,640]{1,0:T(8,128)S(1)} %get-tuple-element.51.refs_2_, ...), custom_call_target="tpu_custom_call" | custom-call | flops 16384000 | bytes 2150400 | tf_op jit(solution)/shard_map/mine/pallas_call | solution.py:31
  38.6 0.1 collective-permute-done.15.recv_ref
  38.8 0.6 %join.1 = bf16[40,2560]{1,0:T(8,128)(2,1)} custom-call(bf16[40,1280]{1,0:T(8,128)(2,1)S(1)} %collective-permute-done.15.recv_ref, bf16[40,2560]{1,0:T(8,128)(2,1)} %mine.1._), custom_call_target="tpu_custom_call", output_to_operand_aliasing={{}: (1, {})} | custom-call | bytes 512000 | tf_op jit(solution)/shard_map/join/pallas_call | solution.py:31
  (2 shorter events, 0.0 us)
Async XLA Ops:
  1.1 9.0 %collective-permute-start.11 = (bf16[80,2,640]{2,1,0:T(2,128)(2,1)S(1)}, bf16[80,2,640]{2,1,0:T(2,128)(2,1)S(1)}, u32[]{:S(2)}, u32[]{:S(2)}) collective-permute-start(bf16[80,2,640]{2,1,0:T(2,128)(2,1)S(1)} %get-tuple-element.36.__), channel_id=1, source_target_pairs={{4,0},{8,4},{12,8},{14,12},{10,14},{6,10},{2,6},{0,2},{5,1},{9,5},... | collective-permute-start | bytes 614408 | tf_op jit(solution)/shard_map/ppermute | solution.py:215
  4.0 8.5 %collective-permute-start.1 = (bf16[80,2,640]{2,1,0:T(2,128)(2,1)S(1)}, bf16[80,2,640]{2,1,0:T(2,128)(2,1)S(1)}, u32[]{:S(2)}, u32[]{:S(2)}) collective-permute-start(bf16[80,2,640]{2,1,0:T(2,128)(2,1)S(1)} %get-tuple-element.35._), channel_id=1, source_target_pairs={{0,4},{4,8},{8,12},{12,14},{14,10},{10,6},{6,2},{2,0},{1,5},{5,9},... | collective-permute-start | bytes 614408 | tf_op jit(solution)/shard_map/ppermute | solution.py:215
  4.2 12.2 %collective-permute-start.8 = (bf16[80,2,640]{2,1,0:T(2,128)(2,1)S(1)}, bf16[80,2,640]{2,1,0:T(2,128)(2,1)S(1)}, u32[]{:S(2)}, u32[]{:S(2)}) collective-permute-start(bf16[80,2,640]{2,1,0:T(2,128)(2,1)S(1)} %get-tuple-element.36.__), channel_id=1, source_target_pairs={{0,4},{4,8},{8,12},{12,14},{14,10},{10,6},{6,2},{2,0},{1,5},{5,9},... | collective-permute-start | bytes 614408 | tf_op jit(solution)/shard_map/ppermute | solution.py:215
  6.2 11.0 %collective-permute-start.4 = (bf16[80,2,640]{2,1,0:T(2,128)(2,1)S(1)}, bf16[80,2,640]{2,1,0:T(2,128)(2,1)S(1)}, u32[]{:S(2)}, u32[]{:S(2)}) collective-permute-start(bf16[80,2,640]{2,1,0:T(2,128)(2,1)S(1)} %get-tuple-element.35._), channel_id=1, source_target_pairs={{4,0},{8,4},{12,8},{14,12},{10,14},{6,10},{2,6},{0,2},{5,1},{9,5},... | collective-permute-start | bytes 614408 | tf_op jit(solution)/shard_map/ppermute | solution.py:215
  10.5 11.1 %copy-start = (bf16[40,3,2560]{2,0,1:T(8,128)(2,1)S(1)}, bf16[40,3,2560]{2,0,1:T(8,128)(2,1)}, u32[]{:S(2)}) copy-start(bf16[40,3,2560]{2,0,1:T(8,128)(2,1)} %param.4) | copy-start | bytes 1843204
  10.5 9.1 %collective-permute-start.12 = (bf16[2,80,640]{2,1,0:T(8,128)(2,1)S(1)}, bf16[2,80,640]{2,1,0:T(8,128)(2,1)S(1)}, u32[]{:S(2)}, u32[]{:S(2)}) collective-permute-start(bf16[2,80,640]{2,1,0:T(8,128)(2,1)S(1)} %part.7.refs_1_), channel_id=1, source_target_pairs={{4,0},{8,4},{12,8},{14,12},{10,14},{6,10},{2,6},{0,2},{5,1},{9,5},... | collective-permute-start | bytes 614408 | tf_op jit(solution)/shard_map/ppermute | solution.py:215
  13.1 8.1 %collective-permute-start.2 = (bf16[2,80,640]{2,1,0:T(8,128)(2,1)S(1)}, bf16[2,80,640]{2,1,0:T(8,128)(2,1)S(1)}, u32[]{:S(2)}, u32[]{:S(2)}) collective-permute-start(bf16[2,80,640]{2,1,0:T(8,128)(2,1)S(1)} %part.4.refs_0_), channel_id=1, source_target_pairs={{0,4},{4,8},{8,12},{12,14},{14,10},{10,6},{6,2},{2,0},{1,5},{5,9},... | collective-permute-start | bytes 614408 | tf_op jit(solution)/shard_map/ppermute | solution.py:215
  16.9 4.7 %copy-start.1 = (f32[2560]{0:T(1024)S(1)}, f32[2560]{0:T(1024)}, u32[]{:S(2)}) copy-start(f32[2560]{0:T(1024)} %param.6) | copy-start | bytes 30724
  16.9 8.6 %collective-permute-start.9 = (bf16[2,80,640]{2,1,0:T(8,128)(2,1)S(1)}, bf16[2,80,640]{2,1,0:T(8,128)(2,1)S(1)}, u32[]{:S(2)}, u32[]{:S(2)}) collective-permute-start(bf16[2,80,640]{2,1,0:T(8,128)(2,1)S(1)} %part.6.refs_0_), channel_id=1, source_target_pairs={{0,4},{4,8},{8,12},{12,14},{14,10},{10,6},{6,2},{2,0},{1,5},{5,9},... | collective-permute-start | bytes 614408 | tf_op jit(solution)/shard_map/ppermute | solution.py:215
  17.6 4.0 %copy-start.2 = (f32[2560]{0:T(1024)S(1)}, f32[2560]{0:T(1024)}, u32[]{:S(2)}) copy-start(f32[2560]{0:T(1024)} %param.7) | copy-start | bytes 30724
  17.6 8.0 %collective-permute-start.5 = (bf16[2,80,640]{2,1,0:T(8,128)(2,1)S(1)}, bf16[2,80,640]{2,1,0:T(8,128)(2,1)S(1)}, u32[]{:S(2)}, u32[]{:S(2)}) collective-permute-start(bf16[2,80,640]{2,1,0:T(8,128)(2,1)S(1)} %part.5.refs_1_), channel_id=1, source_target_pairs={{4,0},{8,4},{12,8},{14,12},{10,14},{6,10},{2,6},{0,2},{5,1},{9,5},... | collective-permute-start | bytes 614408 | tf_op jit(solution)/shard_map/ppermute | solution.py:215
  19.6 8.0 %collective-permute-start.13 = (bf16[2,80,640]{2,1,0:T(8,128)(2,1)S(1)}, bf16[2,80,640]{2,1,0:T(8,128)(2,1)S(1)}, u32[]{:S(2)}, u32[]{:S(2)}) collective-permute-start(bf16[2,80,640]{2,1,0:T(8,128)(2,1)S(1)} %collective-permute-done.12.refs_1_), channel_id=1, source_target_pairs={{4,0},{8,4},{12,8},{14,12},{10,14},{6,10},{2,6},{0,2},{5,1},{9,5},... | collective-permute-start | bytes 614408 | tf_op jit(solution)/shard_map/ppermute | solution.py:215
  21.2 8.7 %collective-permute-start.3 = (bf16[2,80,640]{2,1,0:T(8,128)(2,1)S(1)}, bf16[2,80,640]{2,1,0:T(8,128)(2,1)S(1)}, u32[]{:S(2)}, u32[]{:S(2)}) collective-permute-start(bf16[2,80,640]{2,1,0:T(8,128)(2,1)S(1)} %collective-permute-done.2.refs_0_), channel_id=1, source_target_pairs={{0,4},{4,8},{8,12},{12,14},{14,10},{10,6},{6,2},{2,0},{1,5},{5,9},... | collective-permute-start | bytes 614408 | tf_op jit(solution)/shard_map/ppermute | solution.py:215
  22.9 7.1 %collective-permute-start = (bf16[3,40,1280]{2,1,0:T(8,128)(2,1)S(1)}, bf16[3,40,1280]{2,1,0:T(8,128)(2,1)S(1)}, u32[]{:S(2)}, u32[]{:S(2)}) collective-permute-start(bf16[3,40,1280]{2,1,0:T(8,128)(2,1)S(1)} %get-tuple-element.37), channel_id=1, source_target_pairs={{0,1},{1,0},{2,3},{3,2},{4,5},{5,4},{6,7},{7,6},{8,9},{9,8},{10,11... | collective-permute-start | bytes 921608 | tf_op jit(solution)/shard_map/ppermute | solution.py:241
  25.5 8.8 %collective-permute-start.10 = (bf16[2,80,640]{2,1,0:T(8,128)(2,1)S(1)}, bf16[2,80,640]{2,1,0:T(8,128)(2,1)S(1)}, u32[]{:S(2)}, u32[]{:S(2)}) collective-permute-start(bf16[2,80,640]{2,1,0:T(8,128)(2,1)S(1)} %collective-permute-done.9.refs_0_), channel_id=1, source_target_pairs={{0,4},{4,8},{8,12},{12,14},{14,10},{10,6},{6,2},{2,0},{1,5},{5,9},... | collective-permute-start | bytes 614408 | tf_op jit(solution)/shard_map/ppermute | solution.py:215
  25.6 9.2 %collective-permute-start.6 = (bf16[2,80,640]{2,1,0:T(8,128)(2,1)S(1)}, bf16[2,80,640]{2,1,0:T(8,128)(2,1)S(1)}, u32[]{:S(2)}, u32[]{:S(2)}) collective-permute-start(bf16[2,80,640]{2,1,0:T(8,128)(2,1)S(1)} %collective-permute-done.5.refs_1_), channel_id=1, source_target_pairs={{4,0},{8,4},{12,8},{14,12},{10,14},{6,10},{2,6},{0,2},{5,1},{9,5},... | collective-permute-start | bytes 614408 | tf_op jit(solution)/shard_map/ppermute | solution.py:215
  27.6 8.6 %collective-permute-start.14 = (bf16[2,80,640]{2,1,0:T(8,128)(2,1)S(1)}, bf16[2,80,640]{2,1,0:T(8,128)(2,1)S(1)}, u32[]{:S(2)}, u32[]{:S(2)}) collective-permute-start(bf16[2,80,640]{2,1,0:T(8,128)(2,1)S(1)} %collective-permute-done.13.refs_1_), channel_id=1, source_target_pairs={{4,0},{8,4},{12,8},{14,12},{10,14},{6,10},{2,6},{0,2},{5,1},{9,5},... | collective-permute-start | bytes 614408 | tf_op jit(solution)/shard_map/ppermute | solution.py:215
  29.9 7.0 %collective-permute-start.7 = (bf16[2,80,640]{2,1,0:T(8,128)(2,1)S(1)}, bf16[2,80,640]{2,1,0:T(8,128)(2,1)S(1)}, u32[]{:S(2)}, u32[]{:S(2)}) collective-permute-start(bf16[2,80,640]{2,1,0:T(8,128)(2,1)S(1)} %collective-permute-done.3.refs_0_), channel_id=1, source_target_pairs={{0,4},{4,8},{8,12},{12,14},{14,10},{10,6},{6,2},{2,0},{1,5},{5,9},... | collective-permute-start | bytes 614408 | tf_op jit(solution)/shard_map/ppermute | solution.py:215
  37.4 1.4 %collective-permute-start.15 = (bf16[40,1280]{1,0:T(8,128)(2,1)S(1)}, bf16[40,1280]{1,0:T(8,128)(2,1)S(1)}, u32[]{:S(2)}, u32[]{:S(2)}) collective-permute-start(bf16[40,1280]{1,0:T(8,128)(2,1)S(1)} %send.1), channel_id=1, source_target_pairs={{0,1},{1,0},{2,3},{3,2},{4,5},{5,4},{6,7},{7,6},{8,9},{9,8},{10,11... | collective-permute-start | bytes 307208 | tf_op jit(solution)/shard_map/ppermute | solution.py:259

commit v5 on v4

--- a/solution.py
+++ b/solution.py
@@ -21,7 +21,7 @@
 PREP = 1
 BYTES = 1
 GRANT = 55900000
-PIECES = 5
+PIECES = 2
 
 
 def call(name, body, outs, *args, flops=0, ins=None, to=None, aliases=None, scratch=(), grant=32 << 20):
@@ -44,18 +44,21 @@
 def load_kernel(x_hbm, *refs):
     outs, sem = refs[:2], refs[2]
     half = outs[0].shape[-1]
+    pieces = sem.shape[0]
+    rows = x_hbm.shape[0] // pieces
     copies = []
-    for side in range(2):
-        at = pl.ds(side * half, half)
-        copies.append(pltpu.make_async_copy(x_hbm.at[:, :, at], outs[side], sem.at[side]))
-        copies[side].start()
+    for side in (1, 0):
+        for i in range(pieces):
+            at = pl.ds(i * rows, rows)
+            from_ref = x_hbm.at[at, :, pl.ds(side * half, half)]
+            copies.append(pltpu.make_async_copy(from_ref, outs[side].at[at], sem.at[i, side]))
+            copies[-1].start()
     for copy in copies:
         copy.wait()
 
 
 def part_kernel(x_ref, out_ref):
-    for part in range(2):
-        out_ref[part] = x_ref[:, part]
+    out_ref[...] = jnp.swapaxes(x_ref[...], 0, 1)
 
 
 def prep_kernel(x_hbm, qg_ref, kg_ref, _, __, keep_ref, send_ref, buf, sem):
@@ -149,13 +152,14 @@
             ref[:, head * HD : (head + 1) * HD] = value
 
 
-def finish(begin, q_ref, sides, out_ref):
+def finish(begin, q_ref, sides, out_ref, skip=0):
     rows = q_ref.shape[1]
+    skip *= out_ref.shape[-1] // HD
     heads = []
     for *state, kv_refs in sides:
         for head in range(state[0].shape[-1] // HD):
             at = pl.ds(head * HD, HD)
-            query = q_ref[0, :, pl.ds(len(heads) * HD, HD)]
+            query = q_ref[0, :, pl.ds((skip + len(heads)) * HD, HD)]
             keys, values = ([kv[i, :, at] for kv in kv_refs] for i in range(2))
             old = [ref[begin : begin + rows, at] for ref in state]
             heads.append((query, keys, values, old))
@@ -167,26 +171,25 @@
     return [(*side[:3], side[3:]) for side in (refs[:cut], refs[cut:])]
 
 
-def send_kernel(begin, cut, q_ref, *refs):
+def send_kernel(begin, side, q_ref, *refs):
+    finish(begin, q_ref, [(*refs[:3], refs[3:-1])], refs[-1], side)
+
+
+def mine_kernel(begin, cut, q_ref, *refs):
     finish(begin, q_ref, two_sides(refs[:-1], cut), refs[-1])
 
 
-def mine_kernel(begin, cut, q_ref, *refs):
-    out_hbm, buf, sem = refs[-3:]
-    finish(begin, q_ref, two_sides(refs[:-3], cut), buf)
-    width = buf.shape[-1]
-    at = pl.ds(pl.multiple_of(lax.axis_index("uly") * width, HD), width)
-    copy = pltpu.make_async_copy(buf, out_hbm.at[:, at], sem)
-    copy.start()
-    copy.wait()
-
-
-def join_kernel(recv_ref, _, out_hbm, sem):
-    width = recv_ref.shape[-1]
-    at = pl.ds(pl.multiple_of((1 - lax.axis_index("uly")) * width, HD), width)
-    copy = pltpu.make_async_copy(recv_ref, out_hbm.at[:, at], sem)
-    copy.start()
-    copy.wait()
+def join_kernel(mine_ref, one_ref, two_ref, out_hbm, sem):
+    here = lax.axis_index("uly")
+    width, half = mine_ref.shape[-1], one_ref.shape[-1]
+    starts = [here * width, (1 - here) * width, (1 - here) * width + half]
+    copies = []
+    for i, (start, ref) in enumerate(zip(starts, (mine_ref, one_ref, two_ref))):
+        at = pl.ds(pl.multiple_of(start, HD), ref.shape[-1])
+        copies.append(pltpu.make_async_copy(ref, out_hbm.at[:, at], sem.at[i]))
+        copies[i].start()
+    for copy in copies:
+        copy.wait()
 
 
 def shards(n, fresh_qkv, stale_kv, q_gain, k_gain):
@@ -206,7 +209,7 @@
         [((patch_rows, 2, half), BF16)] * 2,
         stale_kv,
         ins=[ANY],
-        scratch=[dma((2,))],
+        scratch=[dma((PIECES, 2))],
         grant=GRANT,
     )
     forward, backward = list(sides), list(sides)
@@ -251,24 +254,32 @@
             states[side] = call(
                 f"update{hop}{side}", body, state, queries[side], *blocks, *states[side], flops=len(blocks) * (work if hop < len(arrived[0]) - 2 else LATE * work)
             )
+    incoming = [None, None]
+    for side in (1, 0):
+        (outgoing,) = call(
+            f"send{side}",
+            functools.partial(send_kernel, rows, side),
+            [((rows, half), BF16)],
+            recv,
+            *states[side],
+            *arrived[side][-1],
+            flops=work // 2,
+        )
+        incoming[side] = lax.ppermute(outgoing, "uly", swap)
     last = [*states[0], *arrived[0][-1], *states[1], *arrived[1][-1]]
     cut = len(states[0]) + len(arrived[0][-1])
-    (outgoing,) = call(
-        "send", functools.partial(send_kernel, rows, cut), [((rows, width), BF16)], recv, *last, flops=work
-    )
-    incoming = lax.ppermute(outgoing, "uly", swap)
-    result = [((rows, features), BF16)]
+    (mine,) = call(
+        "mine", functools.partial(mine_kernel, 0, cut), [((rows, width), BF16)], keep, *last, flops=work
+    )
     (out,) = call(
-        "mine",
-        functools.partial(mine_kernel, 0, cut),
-        result,
-        keep,
-        *last,
+        "join",
+        join_kernel,
+        [((rows, features), BF16)],
+        mine,
+        *incoming,
         to=[ANY],
-        scratch=[pltpu.VMEM((rows, width), BF16), dma],
-        flops=work,
-    )
-    (out,) = call("join", join_kernel, result, incoming, out, ins=[VMEM, ANY], to=[ANY], aliases={1: 0}, scratch=[dma])
+        scratch=[dma((3,))],
+    )
     return out
 
 

time: 39.6 us -> 39.5 us (level)
  Pallas kernels: 9.99 us -> 7.99 us
  waiting for transfers between devices: 14 us -> 15 us
  starting transfers between devices: 15.3 us -> 16.1 us
    pallas_call x16 -> x17, Pallas kernels: 9.99 us -> 7.99 us  [call(): pl.pallas_call(body, name=name, out_shape=[jax.ShapeDtypeStruct(s, t) for...]
    ppermute x14, starting transfers between devices: 15.1 us -> 15.9 us  [move(): block = lax.ppermute(block, 'patch', way)]
    ppermute x1 -> x2, waiting for transfers between devices: 0.14 us -> 0.71 us  [shards(): incoming[side] = lax.ppermute(outgoing, 'uly', swap)]
    ppermute x14, waiting for transfers between devices: 13.8 us -> 14.3 us  [move(): block = lax.ppermute(block, 'patch', way)]
  transfers between devices with their start and end apart: 16 -> 17, of which waited for: 8 -> 9; matrix products, arithmetic and copies ran while one was open for 0% -> 0% of each run, Pallas kernels for 20% -> 16%
where the time goes in v5:
time: 39.5 us; the launch traced here: 39.4 us
  starting transfers between devices  16.1 us (41%)
  waiting for transfers between devices  15 us (38%)
  Pallas kernels  7.99 us (20%)
    ppermute x14, starting transfers between devices, move(): block = lax.ppermute(block, 'patch', way)  15.9 us
    ppermute x14, waiting for transfers between devices, move(): block = lax.ppermute(block, 'patch', way)  14.3 us
    pallas_call x17, Pallas kernels, call(): pl.pallas_call(body, name=name, out_shape=[jax.ShapeDtypeStruct(s, t) for...  7.99 us
  transfers between devices with their start and end apart: 17, of which 9 were waited for; matrix products, arithmetic and copies ran while one was open for 0% of the time, Pallas kernels for 16%

profile of v5, /device:TPU:0, one launch (start us, length us, event | category | flops | bytes accessed | tf_op | source)
XLA Modules:
  0.0 39.4 jit_solution(14552717612434401944)
XLA Ops:
  0.0 1.1 %load.1 = (bf16[80,2,640]{2,1,0:T(2,128)(2,1)S(1)}, bf16[80,2,640]{2,1,0:T(2,128)(2,1)S(1)}) custom-call(bf16[80,2,1280]{2,1,0:T(2,128)(2,1)} %x_hbm.1), custom_call_target="tpu_custom_call" | custom-call | bytes 819200 | tf_op jit(solution)/shard_map/load/pallas_call | solution.py:31
  1.1 3.0 %collective-permute-start.11 = (bf16[80,2,640]{2,1,0:T(2,128)(2,1)S(1)}, bf16[80,2,640]{2,1,0:T(2,128)(2,1)S(1)}, u32[]{:S(2)}, u32[]{:S(2)}) collective-permute-start(bf16[80,2,640]{2,1,0:T(2,128)(2,1)S(1)} %get-tuple-element.36.__), channel_id=1, source_target_pairs={{4,0},{8,4},{12,8},{14,12},{10,14},{6,10},{2,6},{0,2},{5,1},{9,5},... | collective-permute-start | bytes 614408 | tf_op jit(solution)/shard_map/ppermute | solution.py:218
  4.1 0.2 collective-permute-start.1
  4.2 2.0 %collective-permute-start.8 = (bf16[80,2,640]{2,1,0:T(2,128)(2,1)S(1)}, bf16[80,2,640]{2,1,0:T(2,128)(2,1)S(1)}, u32[]{:S(2)}, u32[]{:S(2)}) collective-permute-start(bf16[80,2,640]{2,1,0:T(2,128)(2,1)S(1)} %get-tuple-element.36.__), channel_id=1, source_target_pairs={{0,4},{4,8},{8,12},{12,14},{14,10},{10,6},{6,2},{2,0},{1,5},{5,9},... | collective-permute-start | bytes 614408 | tf_op jit(solution)/shard_map/ppermute | solution.py:218
  6.2 0.1 collective-permute-start.4
  6.3 3.8 %collective-permute-done.11.x_ref = bf16[80,2,640]{2,1,0:T(2,128)(2,1)S(1)} collective-permute-done((bf16[80,2,640]{2,1,0:T(2,128)(2,1)S(1)}, bf16[80,2,640]{2,1,0:T(2,128)(2,1)S(1)}, u32[]{:S(2)}, u32[]{:S(2)}) %collective-permute-start.11) | collective-permute-done | bytes 204832 | tf_op jit(solution)/shard_map/ppermute | solution.py:218
  10.1 0.1 part.7.refs_1_
  10.1 0.0 copy-start
  10.1 2.0 %collective-permute-start.12 = (bf16[2,80,640]{2,1,0:T(8,128)(2,1)S(1)}, bf16[2,80,640]{2,1,0:T(8,128)(2,1)S(1)}, u32[]{:S(2)}, u32[]{:S(2)}) collective-permute-start(bf16[2,80,640]{2,1,0:T(8,128)(2,1)S(1)} %part.7.refs_1_), channel_id=1, source_target_pairs={{4,0},{8,4},{12,8},{14,12},{10,14},{6,10},{2,6},{0,2},{5,1},{9,5},... | collective-permute-start | bytes 614408 | tf_op jit(solution)/shard_map/ppermute | solution.py:218
  12.2 0.0 collective-permute-done.1.x_ref
  12.2 0.1 part.4.refs_0_
  12.2 0.2 collective-permute-start.2
  12.4 4.1 %collective-permute-done.8.x_ref = bf16[80,2,640]{2,1,0:T(2,128)(2,1)S(1)} collective-permute-done((bf16[80,2,640]{2,1,0:T(2,128)(2,1)S(1)}, bf16[80,2,640]{2,1,0:T(2,128)(2,1)S(1)}, u32[]{:S(2)}, u32[]{:S(2)}) %collective-permute-start.8) | collective-permute-done | bytes 204832 | tf_op jit(solution)/shard_map/ppermute | solution.py:218
  16.5 0.1 part.6.refs_0_
  16.5 0.0 copy-start.1
  16.5 0.2 collective-permute-start.9
  16.7 0.0 collective-permute-done.4.x_ref
  16.7 0.1 part.5.refs_1_
  16.8 0.0 copy-start.2
  16.8 2.0 %collective-permute-start.5 = (bf16[2,80,640]{2,1,0:T(8,128)(2,1)S(1)}, bf16[2,80,640]{2,1,0:T(8,128)(2,1)S(1)}, u32[]{:S(2)}, u32[]{:S(2)}) collective-permute-start(bf16[2,80,640]{2,1,0:T(8,128)(2,1)S(1)} %part.5.refs_1_), channel_id=1, source_target_pairs={{4,0},{8,4},{12,8},{14,12},{10,14},{6,10},{2,6},{0,2},{5,1},{9,5},... | collective-permute-start | bytes 614408 | tf_op jit(solution)/shard_map/ppermute | solution.py:218
  18.8 0.1 collective-permute-done.12.refs_1_
  18.8 2.0 %collective-permute-start.13 = (bf16[2,80,640]{2,1,0:T(8,128)(2,1)S(1)}, bf16[2,80,640]{2,1,0:T(8,128)(2,1)S(1)}, u32[]{:S(2)}, u32[]{:S(2)}) collective-permute-start(bf16[2,80,640]{2,1,0:T(8,128)(2,1)S(1)} %collective-permute-done.12.refs_1_), channel_id=1, source_target_pairs={{4,0},{8,4},{12,8},{14,12},{10,14},{6,10},{2,6},{0,2},{5,1},{9,5},... | collective-permute-start | bytes 614408 | tf_op jit(solution)/shard_map/ppermute | solution.py:218
  20.8 0.0 collective-permute-done.2.refs_0_
  20.9 0.1 collective-permute-start.3
  21.0 0.0 copy-done.1
  21.0 0.0 copy-done.2
  21.0 0.0 copy-done
  21.0 1.2 %prep.1 = (bf16[3,40,1280]{2,1,0:T(8,128)(2,1)S(1)}, bf16[3,40,1280]{2,1,0:T(8,128)(2,1)S(1)}) custom-call(bf16[3,40,2560]{2,1,0:T(8,128)(2,1)S(1)} %bitcast.1, f32[1,2560]{1,0:T(1,128)S(1)} %reshape.6.qg_ref, f32[1,2560]{1,0:T(1,128)S(1)} %reshape.7.kg_ref, bf16[80,2,640]{2,1,0:T(2,128)(2,1)S(1)} %get-tuple-element.35._, ...), custom_call_target="tpu_custom_call" | custom-call | flops 1024000 | bytes 1658880 | tf_op jit(solution)/shard_map/prep/pallas_call | solution.py:31
  22.2 0.1 collective-permute-start
  22.3 3.0 %collective-permute-done.9.refs_0_ = bf16[2,80,640]{2,1,0:T(8,128)(2,1)S(1)} collective-permute-done((bf16[2,80,640]{2,1,0:T(8,128)(2,1)S(1)}, bf16[2,80,640]{2,1,0:T(8,128)(2,1)S(1)}, u32[]{:S(2)}, u32[]{:S(2)}) %collective-permute-start.9) | collective-permute-done | bytes 204832 | tf_op jit(solution)/shard_map/ppermute | solution.py:218
  25.2 0.1 collective-permute-start.10
  25.4 0.0 collective-permute-done.5.refs_1_
  25.4 1.9 %collective-permute-start.6 = (bf16[2,80,640]{2,1,0:T(8,128)(2,1)S(1)}, bf16[2,80,640]{2,1,0:T(8,128)(2,1)S(1)}, u32[]{:S(2)}, u32[]{:S(2)}) collective-permute-start(bf16[2,80,640]{2,1,0:T(8,128)(2,1)S(1)} %collective-permute-done.5.refs_1_), channel_id=1, source_target_pairs={{4,0},{8,4},{12,8},{14,12},{10,14},{6,10},{2,6},{0,2},{5,1},{9,5},... | collective-permute-start | bytes 614408 | tf_op jit(solution)/shard_map/ppermute | solution.py:218
  27.3 0.0 collective-permute-done.13.refs_1_
  27.3 2.2 %collective-permute-start.14 = (bf16[2,80,640]{2,1,0:T(8,128)(2,1)S(1)}, bf16[2,80,640]{2,1,0:T(8,128)(2,1)S(1)}, u32[]{:S(2)}, u32[]{:S(2)}) collective-permute-start(bf16[2,80,640]{2,1,0:T(8,128)(2,1)S(1)} %collective-permute-done.13.refs_1_), channel_id=1, source_target_pairs={{4,0},{8,4},{12,8},{14,12},{10,14},{6,10},{2,6},{0,2},{5,1},{9,5},... | collective-permute-start | bytes 614408 | tf_op jit(solution)/shard_map/ppermute | solution.py:218
  29.5 0.2 collective-permute-done.3.refs_0_
  29.6 0.1 collective-permute-start.7
  29.7 0.0 collective-permute-done.recv_ref.q_ref
  29.7 0.5 %own.1 = (bf16[80,640]{1,0:T(8,128)(2,1)S(1)}, f32[80,640]{1,0:T(8,128)S(1)}, f32[80,640]{1,0:T(8,128)S(1)}, f32[80,640]{1,0:T(8,128)S(1)}, bf16[80,640]{1,0:T(8...) custom-call(bf16[3,40,1280]{2,1,0:T(8,128)(2,1)S(1)} %get-tuple-element.37.keep_ref.q_ref, ...), custom_call_target="tpu_custom_call" | custom-call | flops 16384000 | bytes 2048000 | tf_op jit(solution)/shard_map/own/pallas_call | solution.py:31
  30.2 0.5 %update01.1 = (f32[80,640]{1,0:T(8,128)S(1)}, f32[80,640]{1,0:T(8,128)S(1)}, f32[80,640]{1,0:T(8,128)S(1)}) custom-call(bf16[80,640]{1,0:T(8,128)(2,1)S(1)} %get-tuple-element.52.q_ref, bf16[2,80,640]{2,1,0:T(8,128)(2,1)S(1)} %part.6.refs_0_, bf16[2,80,640]{2,1,0:T(8,128)(2,1)S(1)} %part.7.refs_1_, f32[80,640]{1,0:T(8,128)S(1)} %get-tuple-element.53.refs_2_, ...), custom_call_target="tpu_custom_call" | custom-call | flops 32768000 | bytes 1740800 | tf_op jit(solution)/shard_map/update01/pallas_call | solution.py:31
  30.7 0.5 %update00.1 = (f32[80,640]{1,0:T(8,128)S(1)}, f32[80,640]{1,0:T(8,128)S(1)}, f32[80,640]{1,0:T(8,128)S(1)}) custom-call(bf16[80,640]{1,0:T(8,128)(2,1)S(1)} %get-tuple-element.39.q_ref, bf16[2,80,640]{2,1,0:T(8,128)(2,1)S(1)} %part.4.refs_0_, bf16[2,80,640]{2,1,0:T(8,128)(2,1)S(1)} %part.5.refs_1_, f32[80,640]{1,0:T(8,128)S(1)} %get-tuple-element.40.refs_2_, ...), custom_call_target="tpu_custom_call" | custom-call | flops 32768000 | bytes 1740800 | tf_op jit(solution)/shard_map/update00/pallas_call | solution.py:31
  31.3 0.5 %update11.1 = (f32[80,640]{1,0:T(8,128)S(1)}, f32[80,640]{1,0:T(8,128)S(1)}, f32[80,640]{1,0:T(8,128)S(1)}) custom-call(bf16[80,640]{1,0:T(8,128)(2,1)S(1)} %get-tuple-element.52.q_ref, bf16[2,80,640]{2,1,0:T(8,128)(2,1)S(1)} %collective-permute-done.9.refs_0_, bf16[2,80,640]{2,1,0:T(8,128)(2,1)S(1)} %collective-permute-done.12.refs_1_, ...), custom_call_target="tpu_custom_call" | custom-call | flops 32768000 | bytes 1740800 | tf_op jit(solution)/shard_map/update11/pallas_call | solution.py:31
  31.8 0.5 %update10.1 = (f32[80,640]{1,0:T(8,128)S(1)}, f32[80,640]{1,0:T(8,128)S(1)}, f32[80,640]{1,0:T(8,128)S(1)}) custom-call(bf16[80,640]{1,0:T(8,128)(2,1)S(1)} %get-tuple-element.39.q_ref, bf16[2,80,640]{2,1,0:T(8,128)(2,1)S(1)} %collective-permute-done.2.refs_0_, bf16[2,80,640]{2,1,0:T(8,128)(2,1)S(1)} %collective-permute-done.5.refs_1_, ...), custom_call_target="tpu_custom_call" | custom-call | flops 32768000 | bytes 1740800 | tf_op jit(solution)/shard_map/update10/pallas_call | solution.py:31
  32.3 1.8 %collective-permute-done.10.refs_0_ = bf16[2,80,640]{2,1,0:T(8,128)(2,1)S(1)} collective-permute-done((bf16[2,80,640]{2,1,0:T(8,128)(2,1)S(1)}, bf16[2,80,640]{2,1,0:T(8,128)(2,1)S(1)}, u32[]{:S(2)}, u32[]{:S(2)}) %collective-permute-start.10) | collective-permute-done | bytes 204832 | tf_op jit(solution)/shard_map/ppermute | solution.py:218
  34.0 0.5 %update21.1 = (f32[80,640]{1,0:T(8,128)S(1)}, f32[80,640]{1,0:T(8,128)S(1)}, f32[80,640]{1,0:T(8,128)S(1)}) custom-call(bf16[80,640]{1,0:T(8,128)(2,1)S(1)} %get-tuple-element.52.q_ref, bf16[2,80,640]{2,1,0:T(8,128)(2,1)S(1)} %collective-permute-done.10.refs_0_, bf16[2,80,640]{2,1,0:T(8,128)(2,1)S(1)} %collective-permute-done.13.refs_1_, ...), custom_call_target="tpu_custom_call" | custom-call | flops 32768000 | bytes 1740800 | tf_op jit(solution)/shard_map/update21/pallas_call | solution.py:31
  34.5 0.0 collective-permute-done.6.refs_1_
  34.5 0.5 %update20.1 = (f32[80,640]{1,0:T(8,128)S(1)}, f32[80,640]{1,0:T(8,128)S(1)}, f32[80,640]{1,0:T(8,128)S(1)}) custom-call(bf16[80,640]{1,0:T(8,128)(2,1)S(1)} %get-tuple-element.39.q_ref, bf16[2,80,640]{2,1,0:T(8,128)(2,1)S(1)} %collective-permute-done.3.refs_0_, bf16[2,80,640]{2,1,0:T(8,128)(2,1)S(1)} %collective-permute-done.6.refs_1_, ...), custom_call_target="tpu_custom_call" | custom-call | flops 32768000 | bytes 1740800 | tf_op jit(solution)/shard_map/update20/pallas_call | solution.py:31
  35.1 0.8 %collective-permute-done.14.refs_7_.refs_3_ = bf16[2,80,640]{2,1,0:T(8,128)(2,1)S(1)} collective-permute-done((bf16[2,80,640]{2,1,0:T(8,128)(2,1)S(1)}, bf16[2,80,640]{2,1,0:T(8,128)(2,1)S(1)}, u32[]{:S(2)}, u32[]{:S(2)}) %collective-permute-start.14) | collective-permute-done | bytes 204832 | tf_op jit(solution)/shard_map/ppermute | solution.py:218
  35.9 0.4 %send1.1 = bf16[40,640]{1,0:T(8,128)(2,1)S(1)} custom-call(bf16[3,40,1280]{2,1,0:T(8,128)(2,1)S(1)} %collective-permute-done.recv_ref.q_ref, f32[80,640]{1,0:T(8,128)S(1)} %get-tuple-element.62.refs_4_.refs_0_, f32[80,640]{1,0:T(8,128)S(1)} %get-tuple-element.63.refs_5_.refs_1_, f32[80,640]{1,0:T(8,128)S(1)} %get-tuple-element.64.refs_6_.refs_2_, ...), custom_call_target="tpu_custom_call" | custom-call | flops 8192000 | bytes 1177600 | tf_op jit(solution)/shard_map/send1/pallas_call | solution.py:31
  36.3 0.1 collective-permute-start.16
  36.4 0.6 %collective-permute-done.7.refs_3_ = bf16[2,80,640]{2,1,0:T(8,128)(2,1)S(1)} collective-permute-done((bf16[2,80,640]{2,1,0:T(8,128)(2,1)S(1)}, bf16[2,80,640]{2,1,0:T(8,128)(2,1)S(1)}, u32[]{:S(2)}, u32[]{:S(2)}) %collective-permute-start.7) | collective-permute-done | bytes 204832 | tf_op jit(solution)/shard_map/ppermute | solution.py:218
  36.9 0.4 %send0.1 = bf16[40,640]{1,0:T(8,128)(2,1)S(1)} custom-call(bf16[3,40,1280]{2,1,0:T(8,128)(2,1)S(1)} %collective-permute-done.recv_ref.q_ref, f32[80,640]{1,0:T(8,128)S(1)} %get-tuple-element.49.refs_0_, f32[80,640]{1,0:T(8,128)S(1)} %get-tuple-element.50.refs_1_, f32[80,640]{1,0:T(8,128)S(1)} %get-tuple-element.51.refs_2_, ...), custom_call_target="tpu_custom_call" | custom-call | flops 8192000 | bytes 1177600 | tf_op jit(solution)/shard_map/send0/pallas_call | solution.py:31
  37.4 0.1 collective-permute-start.15
  37.4 0.5 %mine.1.mine_ref = bf16[40,1280]{1,0:T(8,128)(2,1)S(1)} custom-call(bf16[3,40,1280]{2,1,0:T(8,128)(2,1)S(1)} %get-tuple-element.37.keep_ref.q_ref, f32[80,640]{1,0:T(8,128)S(1)} %get-tuple-element.49.refs_0_, f32[80,640]{1,0:T(8,128)S(1)} %get-tuple-element.50.refs_1_, f32[80,640]{1,0:T(8,128)S(1)} %get-tuple-element.51.refs_2_, ...), custom_call_target="tpu_custom_call" | custom-call | flops 16384000 | bytes 2048000 | tf_op jit(solution)/shard_map/mine/pallas_call | solution.py:31
  37.9 0.0 collective-permute-done.16.two_ref
  37.9 0.7 %collective-permute-done.15.one_ref = bf16[40,640]{1,0:T(8,128)(2,1)S(1)} collective-permute-done((bf16[40,640]{1,0:T(8,128)(2,1)S(1)}, bf16[40,640]{1,0:T(8,128)(2,1)S(1)}, u32[]{:S(2)}, u32[]{:S(2)}) %collective-permute-start.15) | collective-permute-done | bytes 51232 | tf_op jit(solution)/shard_map/ppermute | solution.py:268
  38.7 0.7 %join.1 = bf16[40,2560]{1,0:T(8,128)(2,1)} custom-call(bf16[40,1280]{1,0:T(8,128)(2,1)S(1)} %mine.1.mine_ref, bf16[40,640]{1,0:T(8,128)(2,1)S(1)} %collective-permute-done.15.one_ref, bf16[40,640]{1,0:T(8,128)(2,1)S(1)} %collective-permute-done.16.two_ref), custom_call_target="tpu_custom_call" | custom-call | bytes 409600 | tf_op jit(solution)/shard_map/join/pallas_call | solution.py:31
  (2 shorter events, 0.0 us)
Async XLA Ops:
  1.1 9.0 %collective-permute-start.11 = (bf16[80,2,640]{2,1,0:T(2,128)(2,1)S(1)}, bf16[80,2,640]{2,1,0:T(2,128)(2,1)S(1)}, u32[]{:S(2)}, u32[]{:S(2)}) collective-permute-start(bf16[80,2,640]{2,1,0:T(2,128)(2,1)S(1)} %get-tuple-element.36.__), channel_id=1, source_target_pairs={{4,0},{8,4},{12,8},{14,12},{10,14},{6,10},{2,6},{0,2},{5,1},{9,5},... | collective-permute-start | bytes 614408 | tf_op jit(solution)/shard_map/ppermute | solution.py:218
  4.1 8.1 %collective-permute-start.1 = (bf16[80,2,640]{2,1,0:T(2,128)(2,1)S(1)}, bf16[80,2,640]{2,1,0:T(2,128)(2,1)S(1)}, u32[]{:S(2)}, u32[]{:S(2)}) collective-permute-start(bf16[80,2,640]{2,1,0:T(2,128)(2,1)S(1)} %get-tuple-element.35._), channel_id=1, source_target_pairs={{0,4},{4,8},{8,12},{12,14},{14,10},{10,6},{6,2},{2,0},{1,5},{5,9},... | collective-permute-start | bytes 614408 | tf_op jit(solution)/shard_map/ppermute | solution.py:218
  4.2 12.2 %collective-permute-start.8 = (bf16[80,2,640]{2,1,0:T(2,128)(2,1)S(1)}, bf16[80,2,640]{2,1,0:T(2,128)(2,1)S(1)}, u32[]{:S(2)}, u32[]{:S(2)}) collective-permute-start(bf16[80,2,640]{2,1,0:T(2,128)(2,1)S(1)} %get-tuple-element.36.__), channel_id=1, source_target_pairs={{0,4},{4,8},{8,12},{12,14},{14,10},{10,6},{6,2},{2,0},{1,5},{5,9},... | collective-permute-start | bytes 614408 | tf_op jit(solution)/shard_map/ppermute | solution.py:218
  6.2 10.5 %collective-permute-start.4 = (bf16[80,2,640]{2,1,0:T(2,128)(2,1)S(1)}, bf16[80,2,640]{2,1,0:T(2,128)(2,1)S(1)}, u32[]{:S(2)}, u32[]{:S(2)}) collective-permute-start(bf16[80,2,640]{2,1,0:T(2,128)(2,1)S(1)} %get-tuple-element.35._), channel_id=1, source_target_pairs={{4,0},{8,4},{12,8},{14,12},{10,14},{6,10},{2,6},{0,2},{5,1},{9,5},... | collective-permute-start | bytes 614408 | tf_op jit(solution)/shard_map/ppermute | solution.py:218
  10.1 10.9 %copy-start = (bf16[40,3,2560]{2,0,1:T(8,128)(2,1)S(1)}, bf16[40,3,2560]{2,0,1:T(8,128)(2,1)}, u32[]{:S(2)}) copy-start(bf16[40,3,2560]{2,0,1:T(8,128)(2,1)} %param.4) | copy-start | bytes 1843204
  10.1 8.7 %collective-permute-start.12 = (bf16[2,80,640]{2,1,0:T(8,128)(2,1)S(1)}, bf16[2,80,640]{2,1,0:T(8,128)(2,1)S(1)}, u32[]{:S(2)}, u32[]{:S(2)}) collective-permute-start(bf16[2,80,640]{2,1,0:T(8,128)(2,1)S(1)} %part.7.refs_1_), channel_id=1, source_target_pairs={{4,0},{8,4},{12,8},{14,12},{10,14},{6,10},{2,6},{0,2},{5,1},{9,5},... | collective-permute-start | bytes 614408 | tf_op jit(solution)/shard_map/ppermute | solution.py:218
  12.2 8.6 %collective-permute-start.2 = (bf16[2,80,640]{2,1,0:T(8,128)(2,1)S(1)}, bf16[2,80,640]{2,1,0:T(8,128)(2,1)S(1)}, u32[]{:S(2)}, u32[]{:S(2)}) collective-permute-start(bf16[2,80,640]{2,1,0:T(8,128)(2,1)S(1)} %part.4.refs_0_), channel_id=1, source_target_pairs={{0,4},{4,8},{8,12},{12,14},{14,10},{10,6},{6,2},{2,0},{1,5},{5,9},... | collective-permute-start | bytes 614408 | tf_op jit(solution)/shard_map/ppermute | solution.py:218
  16.5 4.4 %copy-start.1 = (f32[2560]{0:T(1024)S(1)}, f32[2560]{0:T(1024)}, u32[]{:S(2)}) copy-start(f32[2560]{0:T(1024)} %param.6) | copy-start | bytes 30724
  16.5 8.7 %collective-permute-start.9 = (bf16[2,80,640]{2,1,0:T(8,128)(2,1)S(1)}, bf16[2,80,640]{2,1,0:T(8,128)(2,1)S(1)}, u32[]{:S(2)}, u32[]{:S(2)}) collective-permute-start(bf16[2,80,640]{2,1,0:T(8,128)(2,1)S(1)} %part.6.refs_0_), channel_id=1, source_target_pairs={{0,4},{4,8},{8,12},{12,14},{14,10},{10,6},{6,2},{2,0},{1,5},{5,9},... | collective-permute-start | bytes 614408 | tf_op jit(solution)/shard_map/ppermute | solution.py:218
  16.8 4.2 %copy-start.2 = (f32[2560]{0:T(1024)S(1)}, f32[2560]{0:T(1024)}, u32[]{:S(2)}) copy-start(f32[2560]{0:T(1024)} %param.7) | copy-start | bytes 30724
  16.8 8.6 %collective-permute-start.5 = (bf16[2,80,640]{2,1,0:T(8,128)(2,1)S(1)}, bf16[2,80,640]{2,1,0:T(8,128)(2,1)S(1)}, u32[]{:S(2)}, u32[]{:S(2)}) collective-permute-start(bf16[2,80,640]{2,1,0:T(8,128)(2,1)S(1)} %part.5.refs_1_), channel_id=1, source_target_pairs={{4,0},{8,4},{12,8},{14,12},{10,14},{6,10},{2,6},{0,2},{5,1},{9,5},... | collective-permute-start | bytes 614408 | tf_op jit(solution)/shard_map/ppermute | solution.py:218
  18.8 8.4 %collective-permute-start.13 = (bf16[2,80,640]{2,1,0:T(8,128)(2,1)S(1)}, bf16[2,80,640]{2,1,0:T(8,128)(2,1)S(1)}, u32[]{:S(2)}, u32[]{:S(2)}) collective-permute-start(bf16[2,80,640]{2,1,0:T(8,128)(2,1)S(1)} %collective-permute-done.12.refs_1_), channel_id=1, source_target_pairs={{4,0},{8,4},{12,8},{14,12},{10,14},{6,10},{2,6},{0,2},{5,1},{9,5},... | collective-permute-start | bytes 614408 | tf_op jit(solution)/shard_map/ppermute | solution.py:218
  20.9 8.8 %collective-permute-start.3 = (bf16[2,80,640]{2,1,0:T(8,128)(2,1)S(1)}, bf16[2,80,640]{2,1,0:T(8,128)(2,1)S(1)}, u32[]{:S(2)}, u32[]{:S(2)}) collective-permute-start(bf16[2,80,640]{2,1,0:T(8,128)(2,1)S(1)} %collective-permute-done.2.refs_0_), channel_id=1, source_target_pairs={{0,4},{4,8},{8,12},{12,14},{14,10},{10,6},{6,2},{2,0},{1,5},{5,9},... | collective-permute-start | bytes 614408 | tf_op jit(solution)/shard_map/ppermute | solution.py:218
  22.2 7.6 %collective-permute-start = (bf16[3,40,1280]{2,1,0:T(8,128)(2,1)S(1)}, bf16[3,40,1280]{2,1,0:T(8,128)(2,1)S(1)}, u32[]{:S(2)}, u32[]{:S(2)}) collective-permute-start(bf16[3,40,1280]{2,1,0:T(8,128)(2,1)S(1)} %get-tuple-element.38), channel_id=1, source_target_pairs={{0,1},{1,0},{2,3},{3,2},{4,5},{5,4},{6,7},{7,6},{8,9},{9,8},{10,11... | collective-permute-start | bytes 921608 | tf_op jit(solution)/shard_map/ppermute | solution.py:244
  25.2 8.8 %collective-permute-start.10 = (bf16[2,80,640]{2,1,0:T(8,128)(2,1)S(1)}, bf16[2,80,640]{2,1,0:T(8,128)(2,1)S(1)}, u32[]{:S(2)}, u32[]{:S(2)}) collective-permute-start(bf16[2,80,640]{2,1,0:T(8,128)(2,1)S(1)} %collective-permute-done.9.refs_0_), channel_id=1, source_target_pairs={{0,4},{4,8},{8,12},{12,14},{14,10},{10,6},{6,2},{2,0},{1,5},{5,9},... | collective-permute-start | bytes 614408 | tf_op jit(solution)/shard_map/ppermute | solution.py:218
  25.4 9.2 %collective-permute-start.6 = (bf16[2,80,640]{2,1,0:T(8,128)(2,1)S(1)}, bf16[2,80,640]{2,1,0:T(8,128)(2,1)S(1)}, u32[]{:S(2)}, u32[]{:S(2)}) collective-permute-start(bf16[2,80,640]{2,1,0:T(8,128)(2,1)S(1)} %collective-permute-done.5.refs_1_), channel_id=1, source_target_pairs={{4,0},{8,4},{12,8},{14,12},{10,14},{6,10},{2,6},{0,2},{5,1},{9,5},... | collective-permute-start | bytes 614408 | tf_op jit(solution)/shard_map/ppermute | solution.py:218
  27.3 8.6 %collective-permute-start.14 = (bf16[2,80,640]{2,1,0:T(8,128)(2,1)S(1)}, bf16[2,80,640]{2,1,0:T(8,128)(2,1)S(1)}, u32[]{:S(2)}, u32[]{:S(2)}) collective-permute-start(bf16[2,80,640]{2,1,0:T(8,128)(2,1)S(1)} %collective-permute-done.13.refs_1_), channel_id=1, source_target_pairs={{4,0},{8,4},{12,8},{14,12},{10,14},{6,10},{2,6},{0,2},{5,1},{9,5},... | collective-permute-start | bytes 614408 | tf_op jit(solution)/shard_map/ppermute | solution.py:218
  29.6 7.3 %collective-permute-start.7 = (bf16[2,80,640]{2,1,0:T(8,128)(2,1)S(1)}, bf16[2,80,640]{2,1,0:T(8,128)(2,1)S(1)}, u32[]{:S(2)}, u32[]{:S(2)}) collective-permute-start(bf16[2,80,640]{2,1,0:T(8,128)(2,1)S(1)} %collective-permute-done.3.refs_0_), channel_id=1, source_target_pairs={{0,4},{4,8},{8,12},{12,14},{14,10},{10,6},{6,2},{2,0},{1,5},{5,9},... | collective-permute-start | bytes 614408 | tf_op jit(solution)/shard_map/ppermute | solution.py:218
  36.3 1.7 %collective-permute-start.16 = (bf16[40,640]{1,0:T(8,128)(2,1)S(1)}, bf16[40,640]{1,0:T(8,128)(2,1)S(1)}, u32[]{:S(2)}, u32[]{:S(2)}) collective-permute-start(bf16[40,640]{1,0:T(8,128)(2,1)S(1)} %send1.1), channel_id=1, source_target_pairs={{0,1},{1,0},{2,3},{3,2},{4,5},{5,4},{6,7},{7,6},{8,9},{9,8},{10,11... | collective-permute-start | bytes 153608 | tf_op jit(solution)/shard_map/ppermute | solution.py:268
  37.4 1.3 %collective-permute-start.15 = (bf16[40,640]{1,0:T(8,128)(2,1)S(1)}, bf16[40,640]{1,0:T(8,128)(2,1)S(1)}, u32[]{:S(2)}, u32[]{:S(2)}) collective-permute-start(bf16[40,640]{1,0:T(8,128)(2,1)S(1)} %send0.1), channel_id=1, source_target_pairs={{0,1},{1,0},{2,3},{3,2},{4,5},{5,4},{6,7},{7,6},{8,9},{9,8},{10,11... | collective-permute-start | bytes 153608 | tf_op jit(solution)/shard_map/ppermute | solution.py:268

commit v6 on v4

--- a/solution.py
+++ b/solution.py
@@ -54,16 +54,12 @@
 
 
 def part_kernel(x_ref, out_ref):
-    for part in range(2):
-        out_ref[part] = x_ref[:, part]
-
-
-def prep_kernel(x_hbm, qg_ref, kg_ref, _, __, keep_ref, send_ref, buf, sem):
+    out_ref[...] = jnp.swapaxes(x_ref[...], 0, 1)
+
+
+def prep_kernel(x_ref, qg_ref, kg_ref, _, __, keep_ref, send_ref):
     width = keep_ref.shape[-1]
     first = lax.axis_index("uly") == 0
-    copies = [pltpu.make_async_copy(x_hbm.at[i], buf.at[i], sem.at[i]) for i in range(3)]
-    for copy in copies:
-        copy.start()
 
     def put(part, rows):
         low, high = rows[:, :width], rows[:, width:]
@@ -79,12 +75,10 @@
             send_ref[part] = low
 
     for part, gain in ((0, qg_ref), (1, kg_ref)):
-        copies[part].wait()
-        rows = buf[part].astype(F32)
+        rows = x_ref[part].astype(F32)
         inverse = lax.rsqrt(jnp.mean(rows * rows, axis=-1, keepdims=True) + EPSILON)
         put(part, (rows * inverse * gain[...]).astype(BF16))
-    copies[2].wait()
-    put(2, buf[2])
+    put(2, x_ref[2])
 
 
 def scores_of(query, key):
@@ -172,21 +166,19 @@
 
 
 def mine_kernel(begin, cut, q_ref, *refs):
-    out_hbm, buf, sem = refs[-3:]
-    finish(begin, q_ref, two_sides(refs[:-3], cut), buf)
-    width = buf.shape[-1]
-    at = pl.ds(pl.multiple_of(lax.axis_index("uly") * width, HD), width)
-    copy = pltpu.make_async_copy(buf, out_hbm.at[:, at], sem)
-    copy.start()
-    copy.wait()
-
-
-def join_kernel(recv_ref, _, out_hbm, sem):
-    width = recv_ref.shape[-1]
-    at = pl.ds(pl.multiple_of((1 - lax.axis_index("uly")) * width, HD), width)
-    copy = pltpu.make_async_copy(recv_ref, out_hbm.at[:, at], sem)
-    copy.start()
-    copy.wait()
+    finish(begin, q_ref, two_sides(refs[:-1], cut), refs[-1])
+
+
+def join_kernel(mine_ref, recv_ref, out_hbm, sem):
+    here = lax.axis_index("uly")
+    width = mine_ref.shape[-1]
+    copies = []
+    for i, (place, ref) in enumerate(((here, mine_ref), (1 - here, recv_ref))):
+        at = pl.ds(pl.multiple_of(place * width, HD), width)
+        copies.append(pltpu.make_async_copy(ref, out_hbm.at[:, at], sem.at[i]))
+        copies[i].start()
+    for copy in copies:
+        copy.wait()
 
 
 def shards(n, fresh_qkv, stale_kv, q_gain, k_gain):
@@ -196,6 +188,10 @@
     around = list(range(0, n, 2)) + list(range(1, n, 2))[::-1]
     right = [(around[i], around[(i + 1) % n]) for i in range(n)]
     left = [(b, a) for a, b in right]
+    ways = [
+        [(2 * a + core, 2 * b + core) for core, way in enumerate(pair) for a, b in way]
+        for pair in ((left, right), (right, left))
+    ]
     swap = [(0, 1), (1, 0)]
     far, near = n // 2, (n - 1) // 2
 
@@ -212,17 +208,17 @@
     forward, backward = list(sides), list(sides)
     arrived = [[], []]
     def move(block, hop, way):
-        block = lax.ppermute(block, "patch", way)
+        block = lax.ppermute(block, ("patch", "uly"), way)
         return call("part", part_kernel, [((2, patch_rows, half), BF16)], block)[0] if hop == 0 else block
 
     for hop in range(max(far, near)):
         for side in range(2):
             got = []
             if hop < (far if side == 0 else near):
-                forward[side] = move(forward[side], hop, right)
+                forward[side] = move(forward[side], hop, ways[0])
                 got.append(forward[side])
             if hop < (near if side == 0 else far):
-                backward[side] = move(backward[side], hop, left)
+                backward[side] = move(backward[side], hop, ways[1])
                 got.append(backward[side])
             arrived[side].append(got)
 
@@ -234,8 +230,7 @@
         q_gain.reshape(1, features),
         k_gain.reshape(1, features),
         *sides,
-        ins=[ANY, VMEM, VMEM, ANY, ANY],
-        scratch=[pltpu.VMEM((3, rows, features), BF16), dma((3,))],
+        ins=[VMEM, VMEM, VMEM, ANY, ANY],
         flops=PREP * patch_rows * patch_rows * width // 8,
     )
     recv = lax.ppermute(send, "uly", swap)
@@ -257,18 +252,18 @@
         "send", functools.partial(send_kernel, rows, cut), [((rows, width), BF16)], recv, *last, flops=work
     )
     incoming = lax.ppermute(outgoing, "uly", swap)
-    result = [((rows, features), BF16)]
+    (mine,) = call(
+        "mine", functools.partial(mine_kernel, 0, cut), [((rows, width), BF16)], keep, *last, flops=work
+    )
     (out,) = call(
-        "mine",
-        functools.partial(mine_kernel, 0, cut),
-        result,
-        keep,
-        *last,
+        "join",
+        join_kernel,
+        [((rows, features), BF16)],
+        mine,
+        incoming,
         to=[ANY],
-        scratch=[pltpu.VMEM((rows, width), BF16), dma],
-        flops=work,
-    )
-    (out,) = call("join", join_kernel, result, incoming, out, ins=[VMEM, ANY], to=[ANY], aliases={1: 0}, scratch=[dma])
+        scratch=[dma((2,))],
+    )
     return out
 
 

time: 39.6 us -> 39.1 us (0.987)
  Pallas kernels: 9.99 us -> 6.8 us
  waiting for transfers between devices: 14 us -> 15.4 us
  starting transfers between devices: 15.3 us -> 16.4 us
    pallas_call x16, Pallas kernels: 9.99 us -> 6.8 us  [call(): pl.pallas_call(body, name=name, out_shape=[jax.ShapeDtypeStruct(s, t) for...]
    ppermute x14, starting transfers between devices: 15.1 us -> 16.3 us  [move(): block = lax.ppermute(block, ('patch', 'uly'), way)]
    ppermute x14, waiting for transfers between devices: 13.8 us -> 14.7 us  [move(): block = lax.ppermute(block, ('patch', 'uly'), way)]
    ppermute x1, waiting for transfers between devices: 0.14 us -> 0.79 us  [shards(): incoming = lax.ppermute(outgoing, 'uly', swap)]
  transfers between devices with their start and end apart: 16 -> 16, of which waited for: 8 -> 6; matrix products, arithmetic and copies ran while one was open for 0% -> 0% of each run, Pallas kernels for 20% -> 12%
where the time goes in v6:
time: 39.1 us; the launch traced here: 38.9 us
  starting transfers between devices  16.4 us (42%)
  waiting for transfers between devices  15.4 us (39%)
  Pallas kernels  6.8 us (17%)
    ppermute x14, starting transfers between devices, move(): block = lax.ppermute(block, ('patch', 'uly'), way)  16.3 us
    ppermute x14, waiting for transfers between devices, move(): block = lax.ppermute(block, ('patch', 'uly'), way)  14.7 us
    pallas_call x16, Pallas kernels, call(): pl.pallas_call(body, name=name, out_shape=[jax.ShapeDtypeStruct(s, t) for...  6.8 us
    ppermute x1, waiting for transfers between devices, shards(): incoming = lax.ppermute(outgoing, 'uly', swap)  0.79 us
  transfers between devices with their start and end apart: 16, of which 6 were waited for; matrix products, arithmetic and copies ran while one was open for 0% of the time, Pallas kernels for 12%

profile of v6, /device:TPU:0, one launch (start us, length us, event | category | flops | bytes accessed | tf_op | source)
XLA Modules:
  0.0 38.9 jit_solution(18030693384264286404)
XLA Ops:
  0.0 1.0 %load.1 = (bf16[80,2,640]{2,1,0:T(2,128)(2,1)S(1)}, bf16[80,2,640]{2,1,0:T(2,128)(2,1)S(1)}) custom-call(bf16[80,2,1280]{2,1,0:T(2,128)(2,1)} %x_hbm.1), custom_call_target="tpu_custom_call" | custom-call | bytes 819200 | tf_op jit(solution)/shard_map/load/pallas_call | solution.py:31
  1.1 3.1 %collective-permute-start.11 = (bf16[80,2,640]{2,1,0:T(2,128)(2,1)S(1)}, bf16[80,2,640]{2,1,0:T(2,128)(2,1)S(1)}, u32[]{:S(2)}, u32[]{:S(2)}) collective-permute-start(bf16[80,2,640]{2,1,0:T(2,128)(2,1)S(1)} %get-tuple-element.36.__), channel_id=1, source_target_pairs={{0,4},{4,8},{8,12},{12,14},{14,10},{10,6},{6,2},{2,0},{5,1},{9,5},... | collective-permute-start | bytes 614408 | tf_op jit(solution)/shard_map/ppermute | solution.py:211
  4.1 0.0 collective-permute-start.1
  4.1 1.9 %collective-permute-start.8 = (bf16[80,2,640]{2,1,0:T(2,128)(2,1)S(1)}, bf16[80,2,640]{2,1,0:T(2,128)(2,1)S(1)}, u32[]{:S(2)}, u32[]{:S(2)}) collective-permute-start(bf16[80,2,640]{2,1,0:T(2,128)(2,1)S(1)} %get-tuple-element.36.__), channel_id=1, source_target_pairs={{4,0},{8,4},{12,8},{14,12},{10,14},{6,10},{2,6},{0,2},{1,5},{5,9},... | collective-permute-start | bytes 614408 | tf_op jit(solution)/shard_map/ppermute | solution.py:211
  6.1 0.1 collective-permute-start.4
  6.2 3.4 %collective-permute-done.11.x_ref = bf16[80,2,640]{2,1,0:T(2,128)(2,1)S(1)} collective-permute-done((bf16[80,2,640]{2,1,0:T(2,128)(2,1)S(1)}, bf16[80,2,640]{2,1,0:T(2,128)(2,1)S(1)}, u32[]{:S(2)}, u32[]{:S(2)}) %collective-permute-start.11) | collective-permute-done | bytes 204832 | tf_op jit(solution)/shard_map/ppermute | solution.py:211
  9.6 0.1 part.7.refs_1_
  9.7 0.0 copy-start
  9.7 2.5 %collective-permute-start.12 = (bf16[2,80,640]{2,1,0:T(8,128)(2,1)S(1)}, bf16[2,80,640]{2,1,0:T(8,128)(2,1)S(1)}, u32[]{:S(2)}, u32[]{:S(2)}) collective-permute-start(bf16[2,80,640]{2,1,0:T(8,128)(2,1)S(1)} %part.7.refs_1_), channel_id=1, source_target_pairs={{0,4},{4,8},{8,12},{12,14},{14,10},{10,6},{6,2},{2,0},{5,1},{9,5},... | collective-permute-start | bytes 614408 | tf_op jit(solution)/shard_map/ppermute | solution.py:211
  12.2 0.0 collective-permute-done.1.x_ref
  12.2 0.1 part.4.refs_0_
  12.3 0.1 collective-permute-start.2
  12.3 4.1 %collective-permute-done.8.x_ref = bf16[80,2,640]{2,1,0:T(2,128)(2,1)S(1)} collective-permute-done((bf16[80,2,640]{2,1,0:T(2,128)(2,1)S(1)}, bf16[80,2,640]{2,1,0:T(2,128)(2,1)S(1)}, u32[]{:S(2)}, u32[]{:S(2)}) %collective-permute-start.8) | collective-permute-done | bytes 204832 | tf_op jit(solution)/shard_map/ppermute | solution.py:211
  16.4 0.1 part.6.refs_0_
  16.5 0.0 copy-start.1
  16.5 0.1 collective-permute-start.9
  16.6 0.0 collective-permute-done.4.x_ref
  16.6 0.1 part.5.refs_1_
  16.7 0.0 copy-start.2
  16.7 2.0 %collective-permute-start.5 = (bf16[2,80,640]{2,1,0:T(8,128)(2,1)S(1)}, bf16[2,80,640]{2,1,0:T(8,128)(2,1)S(1)}, u32[]{:S(2)}, u32[]{:S(2)}) collective-permute-start(bf16[2,80,640]{2,1,0:T(8,128)(2,1)S(1)} %part.5.refs_1_), channel_id=1, source_target_pairs={{0,4},{4,8},{8,12},{12,14},{14,10},{10,6},{6,2},{2,0},{5,1},{9,5},... | collective-permute-start | bytes 614408 | tf_op jit(solution)/shard_map/ppermute | solution.py:211
  18.7 0.0 collective-permute-done.12.refs_1_
  18.7 2.1 %collective-permute-start.13 = (bf16[2,80,640]{2,1,0:T(8,128)(2,1)S(1)}, bf16[2,80,640]{2,1,0:T(8,128)(2,1)S(1)}, u32[]{:S(2)}, u32[]{:S(2)}) collective-permute-start(bf16[2,80,640]{2,1,0:T(8,128)(2,1)S(1)} %collective-permute-done.12.refs_1_), channel_id=1, source_target_pairs={{0,4},{4,8},{8,12},{12,14},{14,10},{10,6},{6,2},{2,0},{5,1},{9,5},... | collective-permute-start | bytes 614408 | tf_op jit(solution)/shard_map/ppermute | solution.py:211
  20.9 0.0 collective-permute-done.2.refs_0_
  20.9 0.0 collective-permute-start.3
  20.9 0.0 copy-done.1
  20.9 0.0 copy-done.2
  20.9 0.0 copy-done
  20.9 0.3 prep.1
  21.3 0.1 collective-permute-start
  21.4 3.2 %collective-permute-done.9.refs_0_ = bf16[2,80,640]{2,1,0:T(8,128)(2,1)S(1)} collective-permute-done((bf16[2,80,640]{2,1,0:T(8,128)(2,1)S(1)}, bf16[2,80,640]{2,1,0:T(8,128)(2,1)S(1)}, u32[]{:S(2)}, u32[]{:S(2)}) %collective-permute-start.9) | collective-permute-done | bytes 204832 | tf_op jit(solution)/shard_map/ppermute | solution.py:211
  24.6 0.0 collective-permute-start.10
  24.6 0.0 collective-permute-done.5.refs_1_
  24.6 2.0 %collective-permute-start.6 = (bf16[2,80,640]{2,1,0:T(8,128)(2,1)S(1)}, bf16[2,80,640]{2,1,0:T(8,128)(2,1)S(1)}, u32[]{:S(2)}, u32[]{:S(2)}) collective-permute-start(bf16[2,80,640]{2,1,0:T(8,128)(2,1)S(1)} %collective-permute-done.5.refs_1_), channel_id=1, source_target_pairs={{0,4},{4,8},{8,12},{12,14},{14,10},{10,6},{6,2},{2,0},{5,1},{9,5},... | collective-permute-start | bytes 614408 | tf_op jit(solution)/shard_map/ppermute | solution.py:211
  26.6 2.3 %collective-permute-done.13.refs_1_ = bf16[2,80,640]{2,1,0:T(8,128)(2,1)S(1)} collective-permute-done((bf16[2,80,640]{2,1,0:T(8,128)(2,1)S(1)}, bf16[2,80,640]{2,1,0:T(8,128)(2,1)S(1)}, u32[]{:S(2)}, u32[]{:S(2)}) %collective-permute-start.13) | collective-permute-done | bytes 204832 | tf_op jit(solution)/shard_map/ppermute | solution.py:211
  28.9 1.7 %collective-permute-start.14 = (bf16[2,80,640]{2,1,0:T(8,128)(2,1)S(1)}, bf16[2,80,640]{2,1,0:T(8,128)(2,1)S(1)}, u32[]{:S(2)}, u32[]{:S(2)}) collective-permute-start(bf16[2,80,640]{2,1,0:T(8,128)(2,1)S(1)} %collective-permute-done.13.refs_1_), channel_id=1, source_target_pairs={{0,4},{4,8},{8,12},{12,14},{14,10},{10,6},{6,2},{2,0},{5,1},{9,5},... | collective-permute-start | bytes 614408 | tf_op jit(solution)/shard_map/ppermute | solution.py:211
  30.6 0.0 collective-permute-done.3.refs_0_
  30.6 0.5 %collective-permute-start.7 = (bf16[2,80,640]{2,1,0:T(8,128)(2,1)S(1)}, bf16[2,80,640]{2,1,0:T(8,128)(2,1)S(1)}, u32[]{:S(2)}, u32[]{:S(2)}) collective-permute-start(bf16[2,80,640]{2,1,0:T(8,128)(2,1)S(1)} %collective-permute-done.3.refs_0_), channel_id=1, source_target_pairs={{4,0},{8,4},{12,8},{14,12},{10,14},{6,10},{2,6},{0,2},{1,5},{5,9},... | collective-permute-start | bytes 614408 | tf_op jit(solution)/shard_map/ppermute | solution.py:211
  31.2 0.0 collective-permute-done.recv_ref.q_ref
  31.2 0.5 %own.1 = (bf16[80,640]{1,0:T(8,128)(2,1)S(1)}, f32[80,640]{1,0:T(8,128)S(1)}, f32[80,640]{1,0:T(8,128)S(1)}, f32[80,640]{1,0:T(8,128)S(1)}, bf16[80,640]{1,0:T(8...) custom-call(bf16[3,40,1280]{2,1,0:T(8,128)(2,1)S(1)} %get-tuple-element.37.keep_ref.q_ref, ...), custom_call_target="tpu_custom_call" | custom-call | flops 16384000 | bytes 2048000 | tf_op jit(solution)/shard_map/own/pallas_call | solution.py:31
  31.6 0.5 %update01.1 = (f32[80,640]{1,0:T(8,128)S(1)}, f32[80,640]{1,0:T(8,128)S(1)}, f32[80,640]{1,0:T(8,128)S(1)}) custom-call(bf16[80,640]{1,0:T(8,128)(2,1)S(1)} %get-tuple-element.52.q_ref, bf16[2,80,640]{2,1,0:T(8,128)(2,1)S(1)} %part.6.refs_0_, bf16[2,80,640]{2,1,0:T(8,128)(2,1)S(1)} %part.7.refs_1_, f32[80,640]{1,0:T(8,128)S(1)} %get-tuple-element.53.refs_2_, ...), custom_call_target="tpu_custom_call" | custom-call | flops 32768000 | bytes 1740800 | tf_op jit(solution)/shard_map/update01/pallas_call | solution.py:31
  32.2 0.5 %update00.1 = (f32[80,640]{1,0:T(8,128)S(1)}, f32[80,640]{1,0:T(8,128)S(1)}, f32[80,640]{1,0:T(8,128)S(1)}) custom-call(bf16[80,640]{1,0:T(8,128)(2,1)S(1)} %get-tuple-element.39.q_ref, bf16[2,80,640]{2,1,0:T(8,128)(2,1)S(1)} %part.4.refs_0_, bf16[2,80,640]{2,1,0:T(8,128)(2,1)S(1)} %part.5.refs_1_, f32[80,640]{1,0:T(8,128)S(1)} %get-tuple-element.40.refs_2_, ...), custom_call_target="tpu_custom_call" | custom-call | flops 32768000 | bytes 1740800 | tf_op jit(solution)/shard_map/update00/pallas_call | solution.py:31
  32.7 0.5 %update11.1 = (f32[80,640]{1,0:T(8,128)S(1)}, f32[80,640]{1,0:T(8,128)S(1)}, f32[80,640]{1,0:T(8,128)S(1)}) custom-call(bf16[80,640]{1,0:T(8,128)(2,1)S(1)} %get-tuple-element.52.q_ref, bf16[2,80,640]{2,1,0:T(8,128)(2,1)S(1)} %collective-permute-done.9.refs_0_, bf16[2,80,640]{2,1,0:T(8,128)(2,1)S(1)} %collective-permute-done.12.refs_1_, ...), custom_call_target="tpu_custom_call" | custom-call | flops 32768000 | bytes 1740800 | tf_op jit(solution)/shard_map/update11/pallas_call | solution.py:31
  33.2 0.5 %update10.1 = (f32[80,640]{1,0:T(8,128)S(1)}, f32[80,640]{1,0:T(8,128)S(1)}, f32[80,640]{1,0:T(8,128)S(1)}) custom-call(bf16[80,640]{1,0:T(8,128)(2,1)S(1)} %get-tuple-element.39.q_ref, bf16[2,80,640]{2,1,0:T(8,128)(2,1)S(1)} %collective-permute-done.2.refs_0_, bf16[2,80,640]{2,1,0:T(8,128)(2,1)S(1)} %collective-permute-done.5.refs_1_, ...), custom_call_target="tpu_custom_call" | custom-call | flops 32768000 | bytes 1740800 | tf_op jit(solution)/shard_map/update10/pallas_call | solution.py:31
  33.7 0.0 collective-permute-done.10.refs_0_
  33.7 0.5 %update21.1 = (f32[80,640]{1,0:T(8,128)S(1)}, f32[80,640]{1,0:T(8,128)S(1)}, f32[80,640]{1,0:T(8,128)S(1)}) custom-call(bf16[80,640]{1,0:T(8,128)(2,1)S(1)} %get-tuple-element.52.q_ref, bf16[2,80,640]{2,1,0:T(8,128)(2,1)S(1)} %collective-permute-done.10.refs_0_, bf16[2,80,640]{2,1,0:T(8,128)(2,1)S(1)} %collective-permute-done.13.refs_1_, ...), custom_call_target="tpu_custom_call" | custom-call | flops 32768000 | bytes 1740800 | tf_op jit(solution)/shard_map/update21/pallas_call | solution.py:31
  34.2 0.0 collective-permute-done.6.refs_1_
  34.2 0.5 %update20.1 = (f32[80,640]{1,0:T(8,128)S(1)}, f32[80,640]{1,0:T(8,128)S(1)}, f32[80,640]{1,0:T(8,128)S(1)}) custom-call(bf16[80,640]{1,0:T(8,128)(2,1)S(1)} %get-tuple-element.39.q_ref, bf16[2,80,640]{2,1,0:T(8,128)(2,1)S(1)} %collective-permute-done.3.refs_0_, bf16[2,80,640]{2,1,0:T(8,128)(2,1)S(1)} %collective-permute-done.6.refs_1_, ...), custom_call_target="tpu_custom_call" | custom-call | flops 32768000 | bytes 1740800 | tf_op jit(solution)/shard_map/update20/pallas_call | solution.py:31
  34.7 1.6 %collective-permute-done.14.refs_7_ = bf16[2,80,640]{2,1,0:T(8,128)(2,1)S(1)} collective-permute-done((bf16[2,80,640]{2,1,0:T(8,128)(2,1)S(1)}, bf16[2,80,640]{2,1,0:T(8,128)(2,1)S(1)}, u32[]{:S(2)}, u32[]{:S(2)}) %collective-permute-start.14) | collective-permute-done | bytes 204832 | tf_op jit(solution)/shard_map/ppermute | solution.py:211
  36.3 0.1 collective-permute-done.7.refs_3_
  36.4 0.5 %send.1 = bf16[40,1280]{1,0:T(8,128)(2,1)S(1)} custom-call(bf16[3,40,1280]{2,1,0:T(8,128)(2,1)S(1)} %collective-permute-done.recv_ref.q_ref, f32[80,640]{1,0:T(8,128)S(1)} %get-tuple-element.49.refs_0_, f32[80,640]{1,0:T(8,128)S(1)} %get-tuple-element.50.refs_1_, f32[80,640]{1,0:T(8,128)S(1)} %get-tuple-element.51.refs_2_, ...), custom_call_target="tpu_custom_call" | custom-call | flops 16384000 | bytes 2048000 | tf_op jit(solution)/shard_map/send/pallas_call | solution.py:31
  36.9 0.1 collective-permute-start.15
  36.9 0.5 %mine.1.mine_ref = bf16[40,1280]{1,0:T(8,128)(2,1)S(1)} custom-call(bf16[3,40,1280]{2,1,0:T(8,128)(2,1)S(1)} %get-tuple-element.37.keep_ref.q_ref, f32[80,640]{1,0:T(8,128)S(1)} %get-tuple-element.49.refs_0_, f32[80,640]{1,0:T(8,128)S(1)} %get-tuple-element.50.refs_1_, f32[80,640]{1,0:T(8,128)S(1)} %get-tuple-element.51.refs_2_, ...), custom_call_target="tpu_custom_call" | custom-call | flops 16384000 | bytes 2048000 | tf_op jit(solution)/shard_map/mine/pallas_call | solution.py:31
  37.4 0.8 %collective-permute-done.15.recv_ref = bf16[40,1280]{1,0:T(8,128)(2,1)S(1)} collective-permute-done((bf16[40,1280]{1,0:T(8,128)(2,1)S(1)}, bf16[40,1280]{1,0:T(8,128)(2,1)S(1)}, u32[]{:S(2)}, u32[]{:S(2)}) %collective-permute-start.15) | collective-permute-done | bytes 102432 | tf_op jit(solution)/shard_map/ppermute | solution.py:254
  38.2 0.7 %join.1 = bf16[40,2560]{1,0:T(8,128)(2,1)} custom-call(bf16[40,1280]{1,0:T(8,128)(2,1)S(1)} %mine.1.mine_ref, bf16[40,1280]{1,0:T(8,128)(2,1)S(1)} %collective-permute-done.15.recv_ref), custom_call_target="tpu_custom_call" | custom-call | bytes 409600 | tf_op jit(solution)/shard_map/join/pallas_call | solution.py:31
  (2 shorter events, 0.0 us)
Async XLA Ops:
  1.1 8.5 %collective-permute-start.11 = (bf16[80,2,640]{2,1,0:T(2,128)(2,1)S(1)}, bf16[80,2,640]{2,1,0:T(2,128)(2,1)S(1)}, u32[]{:S(2)}, u32[]{:S(2)}) collective-permute-start(bf16[80,2,640]{2,1,0:T(2,128)(2,1)S(1)} %get-tuple-element.36.__), channel_id=1, source_target_pairs={{0,4},{4,8},{8,12},{12,14},{14,10},{10,6},{6,2},{2,0},{5,1},{9,5},... | collective-permute-start | bytes 614408 | tf_op jit(solution)/shard_map/ppermute | solution.py:211
  4.1 8.1 %collective-permute-start.1 = (bf16[80,2,640]{2,1,0:T(2,128)(2,1)S(1)}, bf16[80,2,640]{2,1,0:T(2,128)(2,1)S(1)}, u32[]{:S(2)}, u32[]{:S(2)}) collective-permute-start(bf16[80,2,640]{2,1,0:T(2,128)(2,1)S(1)} %get-tuple-element.35._), channel_id=1, source_target_pairs={{4,0},{8,4},{12,8},{14,12},{10,14},{6,10},{2,6},{0,2},{1,5},{5,9},... | collective-permute-start | bytes 614408 | tf_op jit(solution)/shard_map/ppermute | solution.py:211
  4.1 12.3 %collective-permute-start.8 = (bf16[80,2,640]{2,1,0:T(2,128)(2,1)S(1)}, bf16[80,2,640]{2,1,0:T(2,128)(2,1)S(1)}, u32[]{:S(2)}, u32[]{:S(2)}) collective-permute-start(bf16[80,2,640]{2,1,0:T(2,128)(2,1)S(1)} %get-tuple-element.36.__), channel_id=1, source_target_pairs={{4,0},{8,4},{12,8},{14,12},{10,14},{6,10},{2,6},{0,2},{1,5},{5,9},... | collective-permute-start | bytes 614408 | tf_op jit(solution)/shard_map/ppermute | solution.py:211
  6.1 10.6 %collective-permute-start.4 = (bf16[80,2,640]{2,1,0:T(2,128)(2,1)S(1)}, bf16[80,2,640]{2,1,0:T(2,128)(2,1)S(1)}, u32[]{:S(2)}, u32[]{:S(2)}) collective-permute-start(bf16[80,2,640]{2,1,0:T(2,128)(2,1)S(1)} %get-tuple-element.35._), channel_id=1, source_target_pairs={{0,4},{4,8},{8,12},{12,14},{14,10},{10,6},{6,2},{2,0},{5,1},{9,5},... | collective-permute-start | bytes 614408 | tf_op jit(solution)/shard_map/ppermute | solution.py:211
  9.7 11.3 %copy-start = (bf16[40,3,2560]{2,0,1:T(8,128)(2,1)S(1)}, bf16[40,3,2560]{2,0,1:T(8,128)(2,1)}, u32[]{:S(2)}) copy-start(bf16[40,3,2560]{2,0,1:T(8,128)(2,1)} %param.4) | copy-start | bytes 1843204
  9.7 9.0 %collective-permute-start.12 = (bf16[2,80,640]{2,1,0:T(8,128)(2,1)S(1)}, bf16[2,80,640]{2,1,0:T(8,128)(2,1)S(1)}, u32[]{:S(2)}, u32[]{:S(2)}) collective-permute-start(bf16[2,80,640]{2,1,0:T(8,128)(2,1)S(1)} %part.7.refs_1_), channel_id=1, source_target_pairs={{0,4},{4,8},{8,12},{12,14},{14,10},{10,6},{6,2},{2,0},{5,1},{9,5},... | collective-permute-start | bytes 614408 | tf_op jit(solution)/shard_map/ppermute | solution.py:211
  12.3 8.6 %collective-permute-start.2 = (bf16[2,80,640]{2,1,0:T(8,128)(2,1)S(1)}, bf16[2,80,640]{2,1,0:T(8,128)(2,1)S(1)}, u32[]{:S(2)}, u32[]{:S(2)}) collective-permute-start(bf16[2,80,640]{2,1,0:T(8,128)(2,1)S(1)} %part.4.refs_0_), channel_id=1, source_target_pairs={{4,0},{8,4},{12,8},{14,12},{10,14},{6,10},{2,6},{0,2},{1,5},{5,9},... | collective-permute-start | bytes 614408 | tf_op jit(solution)/shard_map/ppermute | solution.py:211
  16.5 4.4 %copy-start.1 = (f32[2560]{0:T(1024)S(1)}, f32[2560]{0:T(1024)}, u32[]{:S(2)}) copy-start(f32[2560]{0:T(1024)} %param.6) | copy-start | bytes 30724
  16.5 8.1 %collective-permute-start.9 = (bf16[2,80,640]{2,1,0:T(8,128)(2,1)S(1)}, bf16[2,80,640]{2,1,0:T(8,128)(2,1)S(1)}, u32[]{:S(2)}, u32[]{:S(2)}) collective-permute-start(bf16[2,80,640]{2,1,0:T(8,128)(2,1)S(1)} %part.6.refs_0_), channel_id=1, source_target_pairs={{4,0},{8,4},{12,8},{14,12},{10,14},{6,10},{2,6},{0,2},{1,5},{5,9},... | collective-permute-start | bytes 614408 | tf_op jit(solution)/shard_map/ppermute | solution.py:211
  16.7 4.2 %copy-start.2 = (f32[2560]{0:T(1024)S(1)}, f32[2560]{0:T(1024)}, u32[]{:S(2)}) copy-start(f32[2560]{0:T(1024)} %param.7) | copy-start | bytes 30724
  16.7 7.9 %collective-permute-start.5 = (bf16[2,80,640]{2,1,0:T(8,128)(2,1)S(1)}, bf16[2,80,640]{2,1,0:T(8,128)(2,1)S(1)}, u32[]{:S(2)}, u32[]{:S(2)}) collective-permute-start(bf16[2,80,640]{2,1,0:T(8,128)(2,1)S(1)} %part.5.refs_1_), channel_id=1, source_target_pairs={{0,4},{4,8},{8,12},{12,14},{14,10},{10,6},{6,2},{2,0},{5,1},{9,5},... | collective-permute-start | bytes 614408 | tf_op jit(solution)/shard_map/ppermute | solution.py:211
  18.7 10.2 %collective-permute-start.13 = (bf16[2,80,640]{2,1,0:T(8,128)(2,1)S(1)}, bf16[2,80,640]{2,1,0:T(8,128)(2,1)S(1)}, u32[]{:S(2)}, u32[]{:S(2)}) collective-permute-start(bf16[2,80,640]{2,1,0:T(8,128)(2,1)S(1)} %collective-permute-done.12.refs_1_), channel_id=1, source_target_pairs={{0,4},{4,8},{8,12},{12,14},{14,10},{10,6},{6,2},{2,0},{5,1},{9,5},... | collective-permute-start | bytes 614408 | tf_op jit(solution)/shard_map/ppermute | solution.py:211
  20.9 9.7 %collective-permute-start.3 = (bf16[2,80,640]{2,1,0:T(8,128)(2,1)S(1)}, bf16[2,80,640]{2,1,0:T(8,128)(2,1)S(1)}, u32[]{:S(2)}, u32[]{:S(2)}) collective-permute-start(bf16[2,80,640]{2,1,0:T(8,128)(2,1)S(1)} %collective-permute-done.2.refs_0_), channel_id=1, source_target_pairs={{4,0},{8,4},{12,8},{14,12},{10,14},{6,10},{2,6},{0,2},{1,5},{5,9},... | collective-permute-start | bytes 614408 | tf_op jit(solution)/shard_map/ppermute | solution.py:211
  21.3 9.9 %collective-permute-start = (bf16[3,40,1280]{2,1,0:T(8,128)(2,1)S(1)}, bf16[3,40,1280]{2,1,0:T(8,128)(2,1)S(1)}, u32[]{:S(2)}, u32[]{:S(2)}) collective-permute-start(bf16[3,40,1280]{2,1,0:T(8,128)(2,1)S(1)} %get-tuple-element.38), channel_id=1, source_target_pairs={{0,1},{1,0},{2,3},{3,2},{4,5},{5,4},{6,7},{7,6},{8,9},{9,8},{10,11... | collective-permute-start | bytes 921608 | tf_op jit(solution)/shard_map/ppermute | solution.py:236
  24.6 9.1 %collective-permute-start.10 = (bf16[2,80,640]{2,1,0:T(8,128)(2,1)S(1)}, bf16[2,80,640]{2,1,0:T(8,128)(2,1)S(1)}, u32[]{:S(2)}, u32[]{:S(2)}) collective-permute-start(bf16[2,80,640]{2,1,0:T(8,128)(2,1)S(1)} %collective-permute-done.9.refs_0_), channel_id=1, source_target_pairs={{4,0},{8,4},{12,8},{14,12},{10,14},{6,10},{2,6},{0,2},{1,5},{5,9},... | collective-permute-start | bytes 614408 | tf_op jit(solution)/shard_map/ppermute | solution.py:211
  24.6 9.6 %collective-permute-start.6 = (bf16[2,80,640]{2,1,0:T(8,128)(2,1)S(1)}, bf16[2,80,640]{2,1,0:T(8,128)(2,1)S(1)}, u32[]{:S(2)}, u32[]{:S(2)}) collective-permute-start(bf16[2,80,640]{2,1,0:T(8,128)(2,1)S(1)} %collective-permute-done.5.refs_1_), channel_id=1, source_target_pairs={{0,4},{4,8},{8,12},{12,14},{14,10},{10,6},{6,2},{2,0},{5,1},{9,5},... | collective-permute-start | bytes 614408 | tf_op jit(solution)/shard_map/ppermute | solution.py:211
  28.9 7.4 %collective-permute-start.14 = (bf16[2,80,640]{2,1,0:T(8,128)(2,1)S(1)}, bf16[2,80,640]{2,1,0:T(8,128)(2,1)S(1)}, u32[]{:S(2)}, u32[]{:S(2)}) collective-permute-start(bf16[2,80,640]{2,1,0:T(8,128)(2,1)S(1)} %collective-permute-done.13.refs_1_), channel_id=1, source_target_pairs={{0,4},{4,8},{8,12},{12,14},{14,10},{10,6},{6,2},{2,0},{5,1},{9,5},... | collective-permute-start | bytes 614408 | tf_op jit(solution)/shard_map/ppermute | solution.py:211
  30.6 5.8 %collective-permute-start.7 = (bf16[2,80,640]{2,1,0:T(8,128)(2,1)S(1)}, bf16[2,80,640]{2,1,0:T(8,128)(2,1)S(1)}, u32[]{:S(2)}, u32[]{:S(2)}) collective-permute-start(bf16[2,80,640]{2,1,0:T(8,128)(2,1)S(1)} %collective-permute-done.3.refs_0_), channel_id=1, source_target_pairs={{4,0},{8,4},{12,8},{14,12},{10,14},{6,10},{2,6},{0,2},{1,5},{5,9},... | collective-permute-start | bytes 614408 | tf_op jit(solution)/shard_map/ppermute | solution.py:211
  36.9 1.4 %collective-permute-start.15 = (bf16[40,1280]{1,0:T(8,128)(2,1)S(1)}, bf16[40,1280]{1,0:T(8,128)(2,1)S(1)}, u32[]{:S(2)}, u32[]{:S(2)}) collective-permute-start(bf16[40,1280]{1,0:T(8,128)(2,1)S(1)} %send.1), channel_id=1, source_target_pairs={{0,1},{1,0},{2,3},{3,2},{4,5},{5,4},{6,7},{7,6},{8,9},{9,8},{10,11... | collective-permute-start | bytes 307208 | tf_op jit(solution)/shard_map/ppermute | solution.py:254

commit v7 on v6

--- a/solution.py
+++ b/solution.py
@@ -190,7 +190,7 @@
     left = [(b, a) for a, b in right]
     ways = [
         [(2 * a + core, 2 * b + core) for core, way in enumerate(pair) for a, b in way]
-        for pair in ((left, right), (right, left))
+        for pair in ((right, left), (left, right))
     ]
     swap = [(0, 1), (1, 0)]
     far, near = n // 2, (n - 1) // 2

time: 39.1 us -> 39.1 us (level)
  no operation moved by 1% of the time
where the time goes in v7:
time: 39.1 us; the launch traced here: 39 us
  starting transfers between devices  16.5 us (42%)
  waiting for transfers between devices  15.4 us (39%)
  Pallas kernels  6.82 us (17%)
    ppermute x14, starting transfers between devices, move(): block = lax.ppermute(block, ('patch', 'uly'), way)  16.4 us
    ppermute x14, waiting for transfers between devices, move(): block = lax.ppermute(block, ('patch', 'uly'), way)  14.6 us
    pallas_call x16, Pallas kernels, call(): pl.pallas_call(body, name=name, out_shape=[jax.ShapeDtypeStruct(s, t) for...  6.82 us
    ppermute x1, waiting for transfers between devices, shards(): incoming = lax.ppermute(outgoing, 'uly', swap)  0.79 us
  transfers between devices with their start and end apart: 16, of which 6 were waited for; matrix products, arithmetic and copies ran while one was open for 0% of the time, Pallas kernels for 12%

profile of v7, /device:TPU:0, one launch (start us, length us, event | category | flops | bytes accessed | tf_op | source)
XLA Modules:
  0.0 39.0 jit_solution(8131959528166160458)
XLA Ops:
  0.0 1.0 %load.1 = (bf16[80,2,640]{2,1,0:T(2,128)(2,1)S(1)}, bf16[80,2,640]{2,1,0:T(2,128)(2,1)S(1)}) custom-call(bf16[80,2,1280]{2,1,0:T(2,128)(2,1)} %x_hbm.1), custom_call_target="tpu_custom_call" | custom-call | bytes 819200 | tf_op jit(solution)/shard_map/load/pallas_call | solution.py:31
  1.1 3.0 %collective-permute-start.11 = (bf16[80,2,640]{2,1,0:T(2,128)(2,1)S(1)}, bf16[80,2,640]{2,1,0:T(2,128)(2,1)S(1)}, u32[]{:S(2)}, u32[]{:S(2)}) collective-permute-start(bf16[80,2,640]{2,1,0:T(2,128)(2,1)S(1)} %get-tuple-element.36.__), channel_id=1, source_target_pairs={{4,0},{8,4},{12,8},{14,12},{10,14},{6,10},{2,6},{0,2},{1,5},{5,9},... | collective-permute-start | bytes 614408 | tf_op jit(solution)/shard_map/ppermute | solution.py:211
  4.0 0.2 collective-permute-start.1
  4.2 2.0 %collective-permute-start.8 = (bf16[80,2,640]{2,1,0:T(2,128)(2,1)S(1)}, bf16[80,2,640]{2,1,0:T(2,128)(2,1)S(1)}, u32[]{:S(2)}, u32[]{:S(2)}) collective-permute-start(bf16[80,2,640]{2,1,0:T(2,128)(2,1)S(1)} %get-tuple-element.36.__), channel_id=1, source_target_pairs={{0,4},{4,8},{8,12},{12,14},{14,10},{10,6},{6,2},{2,0},{5,1},{9,5},... | collective-permute-start | bytes 614408 | tf_op jit(solution)/shard_map/ppermute | solution.py:211
  6.2 0.1 collective-permute-start.4
  6.2 3.3 %collective-permute-done.11.x_ref = bf16[80,2,640]{2,1,0:T(2,128)(2,1)S(1)} collective-permute-done((bf16[80,2,640]{2,1,0:T(2,128)(2,1)S(1)}, bf16[80,2,640]{2,1,0:T(2,128)(2,1)S(1)}, u32[]{:S(2)}, u32[]{:S(2)}) %collective-permute-start.11) | collective-permute-done | bytes 204832 | tf_op jit(solution)/shard_map/ppermute | solution.py:211
  9.5 0.1 part.7.refs_1_
  9.6 0.0 copy-start
  9.6 2.5 %collective-permute-start.12 = (bf16[2,80,640]{2,1,0:T(8,128)(2,1)S(1)}, bf16[2,80,640]{2,1,0:T(8,128)(2,1)S(1)}, u32[]{:S(2)}, u32[]{:S(2)}) collective-permute-start(bf16[2,80,640]{2,1,0:T(8,128)(2,1)S(1)} %part.7.refs_1_), channel_id=1, source_target_pairs={{4,0},{8,4},{12,8},{14,12},{10,14},{6,10},{2,6},{0,2},{1,5},{5,9},... | collective-permute-start | bytes 614408 | tf_op jit(solution)/shard_map/ppermute | solution.py:211
  12.1 0.0 collective-permute-done.1.x_ref
  12.1 0.1 part.4.refs_0_
  12.2 0.1 collective-permute-start.2
  12.3 4.0 %collective-permute-done.8.x_ref = bf16[80,2,640]{2,1,0:T(2,128)(2,1)S(1)} collective-permute-done((bf16[80,2,640]{2,1,0:T(2,128)(2,1)S(1)}, bf16[80,2,640]{2,1,0:T(2,128)(2,1)S(1)}, u32[]{:S(2)}, u32[]{:S(2)}) %collective-permute-start.8) | collective-permute-done | bytes 204832 | tf_op jit(solution)/shard_map/ppermute | solution.py:211
  16.3 0.1 part.6.refs_0_
  16.4 0.0 copy-start.1
  16.4 0.3 collective-permute-start.9
  16.7 0.0 collective-permute-done.4.x_ref
  16.7 0.1 part.5.refs_1_
  16.8 0.0 copy-start.2
  16.8 1.9 %collective-permute-start.5 = (bf16[2,80,640]{2,1,0:T(8,128)(2,1)S(1)}, bf16[2,80,640]{2,1,0:T(8,128)(2,1)S(1)}, u32[]{:S(2)}, u32[]{:S(2)}) collective-permute-start(bf16[2,80,640]{2,1,0:T(8,128)(2,1)S(1)} %part.5.refs_1_), channel_id=1, source_target_pairs={{4,0},{8,4},{12,8},{14,12},{10,14},{6,10},{2,6},{0,2},{1,5},{5,9},... | collective-permute-start | bytes 614408 | tf_op jit(solution)/shard_map/ppermute | solution.py:211
  18.6 0.0 collective-permute-done.12.refs_1_
  18.6 2.1 %collective-permute-start.13 = (bf16[2,80,640]{2,1,0:T(8,128)(2,1)S(1)}, bf16[2,80,640]{2,1,0:T(8,128)(2,1)S(1)}, u32[]{:S(2)}, u32[]{:S(2)}) collective-permute-start(bf16[2,80,640]{2,1,0:T(8,128)(2,1)S(1)} %collective-permute-done.12.refs_1_), channel_id=1, source_target_pairs={{4,0},{8,4},{12,8},{14,12},{10,14},{6,10},{2,6},{0,2},{1,5},{5,9},... | collective-permute-start | bytes 614408 | tf_op jit(solution)/shard_map/ppermute | solution.py:211
  20.8 0.0 collective-permute-done.2.refs_0_
  20.8 0.0 collective-permute-start.3
  20.8 0.0 copy-done.1
  20.8 0.0 copy-done.2
  20.8 0.0 copy-done
  20.8 0.3 prep.1
  21.2 0.1 collective-permute-start
  21.3 3.2 %collective-permute-done.9.refs_0_ = bf16[2,80,640]{2,1,0:T(8,128)(2,1)S(1)} collective-permute-done((bf16[2,80,640]{2,1,0:T(8,128)(2,1)S(1)}, bf16[2,80,640]{2,1,0:T(8,128)(2,1)S(1)}, u32[]{:S(2)}, u32[]{:S(2)}) %collective-permute-start.9) | collective-permute-done | bytes 204832 | tf_op jit(solution)/shard_map/ppermute | solution.py:211
  24.5 0.1 collective-permute-start.10
  24.6 0.0 collective-permute-done.5.refs_1_
  24.6 1.9 %collective-permute-start.6 = (bf16[2,80,640]{2,1,0:T(8,128)(2,1)S(1)}, bf16[2,80,640]{2,1,0:T(8,128)(2,1)S(1)}, u32[]{:S(2)}, u32[]{:S(2)}) collective-permute-start(bf16[2,80,640]{2,1,0:T(8,128)(2,1)S(1)} %collective-permute-done.5.refs_1_), channel_id=1, source_target_pairs={{4,0},{8,4},{12,8},{14,12},{10,14},{6,10},{2,6},{0,2},{1,5},{5,9},... | collective-permute-start | bytes 614408 | tf_op jit(solution)/shard_map/ppermute | solution.py:211
  26.5 2.4 %collective-permute-done.13.refs_1_ = bf16[2,80,640]{2,1,0:T(8,128)(2,1)S(1)} collective-permute-done((bf16[2,80,640]{2,1,0:T(8,128)(2,1)S(1)}, bf16[2,80,640]{2,1,0:T(8,128)(2,1)S(1)}, u32[]{:S(2)}, u32[]{:S(2)}) %collective-permute-start.13) | collective-permute-done | bytes 204832 | tf_op jit(solution)/shard_map/ppermute | solution.py:211
  29.0 1.6 %collective-permute-start.14 = (bf16[2,80,640]{2,1,0:T(8,128)(2,1)S(1)}, bf16[2,80,640]{2,1,0:T(8,128)(2,1)S(1)}, u32[]{:S(2)}, u32[]{:S(2)}) collective-permute-start(bf16[2,80,640]{2,1,0:T(8,128)(2,1)S(1)} %collective-permute-done.13.refs_1_), channel_id=1, source_target_pairs={{4,0},{8,4},{12,8},{14,12},{10,14},{6,10},{2,6},{0,2},{1,5},{5,9},... | collective-permute-start | bytes 614408 | tf_op jit(solution)/shard_map/ppermute | solution.py:211
  30.6 0.0 collective-permute-done.3.refs_0_
  30.6 0.7 %collective-permute-start.7 = (bf16[2,80,640]{2,1,0:T(8,128)(2,1)S(1)}, bf16[2,80,640]{2,1,0:T(8,128)(2,1)S(1)}, u32[]{:S(2)}, u32[]{:S(2)}) collective-permute-start(bf16[2,80,640]{2,1,0:T(8,128)(2,1)S(1)} %collective-permute-done.3.refs_0_), channel_id=1, source_target_pairs={{0,4},{4,8},{8,12},{12,14},{14,10},{10,6},{6,2},{2,0},{5,1},{9,5},... | collective-permute-start | bytes 614408 | tf_op jit(solution)/shard_map/ppermute | solution.py:211
  31.2 0.0 collective-permute-done.recv_ref.q_ref
  31.2 0.5 %own.1 = (bf16[80,640]{1,0:T(8,128)(2,1)S(1)}, f32[80,640]{1,0:T(8,128)S(1)}, f32[80,640]{1,0:T(8,128)S(1)}, f32[80,640]{1,0:T(8,128)S(1)}, bf16[80,640]{1,0:T(8...) custom-call(bf16[3,40,1280]{2,1,0:T(8,128)(2,1)S(1)} %get-tuple-element.37.keep_ref.q_ref, ...), custom_call_target="tpu_custom_call" | custom-call | flops 16384000 | bytes 2048000 | tf_op jit(solution)/shard_map/own/pallas_call | solution.py:31
  31.7 0.5 %update01.1 = (f32[80,640]{1,0:T(8,128)S(1)}, f32[80,640]{1,0:T(8,128)S(1)}, f32[80,640]{1,0:T(8,128)S(1)}) custom-call(bf16[80,640]{1,0:T(8,128)(2,1)S(1)} %get-tuple-element.52.q_ref, bf16[2,80,640]{2,1,0:T(8,128)(2,1)S(1)} %part.6.refs_0_, bf16[2,80,640]{2,1,0:T(8,128)(2,1)S(1)} %part.7.refs_1_, f32[80,640]{1,0:T(8,128)S(1)} %get-tuple-element.53.refs_2_, ...), custom_call_target="tpu_custom_call" | custom-call | flops 32768000 | bytes 1740800 | tf_op jit(solution)/shard_map/update01/pallas_call | solution.py:31
  32.2 0.5 %update00.1 = (f32[80,640]{1,0:T(8,128)S(1)}, f32[80,640]{1,0:T(8,128)S(1)}, f32[80,640]{1,0:T(8,128)S(1)}) custom-call(bf16[80,640]{1,0:T(8,128)(2,1)S(1)} %get-tuple-element.39.q_ref, bf16[2,80,640]{2,1,0:T(8,128)(2,1)S(1)} %part.4.refs_0_, bf16[2,80,640]{2,1,0:T(8,128)(2,1)S(1)} %part.5.refs_1_, f32[80,640]{1,0:T(8,128)S(1)} %get-tuple-element.40.refs_2_, ...), custom_call_target="tpu_custom_call" | custom-call | flops 32768000 | bytes 1740800 | tf_op jit(solution)/shard_map/update00/pallas_call | solution.py:31
  32.7 0.5 %update11.1 = (f32[80,640]{1,0:T(8,128)S(1)}, f32[80,640]{1,0:T(8,128)S(1)}, f32[80,640]{1,0:T(8,128)S(1)}) custom-call(bf16[80,640]{1,0:T(8,128)(2,1)S(1)} %get-tuple-element.52.q_ref, bf16[2,80,640]{2,1,0:T(8,128)(2,1)S(1)} %collective-permute-done.9.refs_0_, bf16[2,80,640]{2,1,0:T(8,128)(2,1)S(1)} %collective-permute-done.12.refs_1_, ...), custom_call_target="tpu_custom_call" | custom-call | flops 32768000 | bytes 1740800 | tf_op jit(solution)/shard_map/update11/pallas_call | solution.py:31
  33.2 0.5 %update10.1 = (f32[80,640]{1,0:T(8,128)S(1)}, f32[80,640]{1,0:T(8,128)S(1)}, f32[80,640]{1,0:T(8,128)S(1)}) custom-call(bf16[80,640]{1,0:T(8,128)(2,1)S(1)} %get-tuple-element.39.q_ref, bf16[2,80,640]{2,1,0:T(8,128)(2,1)S(1)} %collective-permute-done.2.refs_0_, bf16[2,80,640]{2,1,0:T(8,128)(2,1)S(1)} %collective-permute-done.5.refs_1_, ...), custom_call_target="tpu_custom_call" | custom-call | flops 32768000 | bytes 1740800 | tf_op jit(solution)/shard_map/update10/pallas_call | solution.py:31
  33.8 0.0 collective-permute-done.10.refs_0_
  33.8 0.5 %update21.1 = (f32[80,640]{1,0:T(8,128)S(1)}, f32[80,640]{1,0:T(8,128)S(1)}, f32[80,640]{1,0:T(8,128)S(1)}) custom-call(bf16[80,640]{1,0:T(8,128)(2,1)S(1)} %get-tuple-element.52.q_ref, bf16[2,80,640]{2,1,0:T(8,128)(2,1)S(1)} %collective-permute-done.10.refs_0_, bf16[2,80,640]{2,1,0:T(8,128)(2,1)S(1)} %collective-permute-done.13.refs_1_, ...), custom_call_target="tpu_custom_call" | custom-call | flops 32768000 | bytes 1740800 | tf_op jit(solution)/shard_map/update21/pallas_call | solution.py:31
  34.3 0.0 collective-permute-done.6.refs_1_
  34.3 0.5 %update20.1 = (f32[80,640]{1,0:T(8,128)S(1)}, f32[80,640]{1,0:T(8,128)S(1)}, f32[80,640]{1,0:T(8,128)S(1)}) custom-call(bf16[80,640]{1,0:T(8,128)(2,1)S(1)} %get-tuple-element.39.q_ref, bf16[2,80,640]{2,1,0:T(8,128)(2,1)S(1)} %collective-permute-done.3.refs_0_, bf16[2,80,640]{2,1,0:T(8,128)(2,1)S(1)} %collective-permute-done.6.refs_1_, ...), custom_call_target="tpu_custom_call" | custom-call | flops 32768000 | bytes 1740800 | tf_op jit(solution)/shard_map/update20/pallas_call | solution.py:31
  34.8 1.6 %collective-permute-done.14.refs_7_ = bf16[2,80,640]{2,1,0:T(8,128)(2,1)S(1)} collective-permute-done((bf16[2,80,640]{2,1,0:T(8,128)(2,1)S(1)}, bf16[2,80,640]{2,1,0:T(8,128)(2,1)S(1)}, u32[]{:S(2)}, u32[]{:S(2)}) %collective-permute-start.14) | collective-permute-done | bytes 204832 | tf_op jit(solution)/shard_map/ppermute | solution.py:211
  36.4 0.0 collective-permute-done.7.refs_3_
  36.4 0.5 %send.1 = bf16[40,1280]{1,0:T(8,128)(2,1)S(1)} custom-call(bf16[3,40,1280]{2,1,0:T(8,128)(2,1)S(1)} %collective-permute-done.recv_ref.q_ref, f32[80,640]{1,0:T(8,128)S(1)} %get-tuple-element.49.refs_0_, f32[80,640]{1,0:T(8,128)S(1)} %get-tuple-element.50.refs_1_, f32[80,640]{1,0:T(8,128)S(1)} %get-tuple-element.51.refs_2_, ...), custom_call_target="tpu_custom_call" | custom-call | flops 16384000 | bytes 2048000 | tf_op jit(solution)/shard_map/send/pallas_call | solution.py:31
  36.9 0.1 collective-permute-start.15
  37.0 0.5 %mine.1.mine_ref = bf16[40,1280]{1,0:T(8,128)(2,1)S(1)} custom-call(bf16[3,40,1280]{2,1,0:T(8,128)(2,1)S(1)} %get-tuple-element.37.keep_ref.q_ref, f32[80,640]{1,0:T(8,128)S(1)} %get-tuple-element.49.refs_0_, f32[80,640]{1,0:T(8,128)S(1)} %get-tuple-element.50.refs_1_, f32[80,640]{1,0:T(8,128)S(1)} %get-tuple-element.51.refs_2_, ...), custom_call_target="tpu_custom_call" | custom-call | flops 16384000 | bytes 2048000 | tf_op jit(solution)/shard_map/mine/pallas_call | solution.py:31
  37.5 0.8 %collective-permute-done.15.recv_ref = bf16[40,1280]{1,0:T(8,128)(2,1)S(1)} collective-permute-done((bf16[40,1280]{1,0:T(8,128)(2,1)S(1)}, bf16[40,1280]{1,0:T(8,128)(2,1)S(1)}, u32[]{:S(2)}, u32[]{:S(2)}) %collective-permute-start.15) | collective-permute-done | bytes 102432 | tf_op jit(solution)/shard_map/ppermute | solution.py:254
  38.3 0.7 %join.1 = bf16[40,2560]{1,0:T(8,128)(2,1)} custom-call(bf16[40,1280]{1,0:T(8,128)(2,1)S(1)} %mine.1.mine_ref, bf16[40,1280]{1,0:T(8,128)(2,1)S(1)} %collective-permute-done.15.recv_ref), custom_call_target="tpu_custom_call" | custom-call | bytes 409600 | tf_op jit(solution)/shard_map/join/pallas_call | solution.py:31
  (2 shorter events, 0.0 us)
Async XLA Ops:
  1.1 8.5 %collective-permute-start.11 = (bf16[80,2,640]{2,1,0:T(2,128)(2,1)S(1)}, bf16[80,2,640]{2,1,0:T(2,128)(2,1)S(1)}, u32[]{:S(2)}, u32[]{:S(2)}) collective-permute-start(bf16[80,2,640]{2,1,0:T(2,128)(2,1)S(1)} %get-tuple-element.36.__), channel_id=1, source_target_pairs={{4,0},{8,4},{12,8},{14,12},{10,14},{6,10},{2,6},{0,2},{1,5},{5,9},... | collective-permute-start | bytes 614408 | tf_op jit(solution)/shard_map/ppermute | solution.py:211
  4.0 8.1 %collective-permute-start.1 = (bf16[80,2,640]{2,1,0:T(2,128)(2,1)S(1)}, bf16[80,2,640]{2,1,0:T(2,128)(2,1)S(1)}, u32[]{:S(2)}, u32[]{:S(2)}) collective-permute-start(bf16[80,2,640]{2,1,0:T(2,128)(2,1)S(1)} %get-tuple-element.35._), channel_id=1, source_target_pairs={{0,4},{4,8},{8,12},{12,14},{14,10},{10,6},{6,2},{2,0},{5,1},{9,5},... | collective-permute-start | bytes 614408 | tf_op jit(solution)/shard_map/ppermute | solution.py:211
  4.2 12.1 %collective-permute-start.8 = (bf16[80,2,640]{2,1,0:T(2,128)(2,1)S(1)}, bf16[80,2,640]{2,1,0:T(2,128)(2,1)S(1)}, u32[]{:S(2)}, u32[]{:S(2)}) collective-permute-start(bf16[80,2,640]{2,1,0:T(2,128)(2,1)S(1)} %get-tuple-element.36.__), channel_id=1, source_target_pairs={{0,4},{4,8},{8,12},{12,14},{14,10},{10,6},{6,2},{2,0},{5,1},{9,5},... | collective-permute-start | bytes 614408 | tf_op jit(solution)/shard_map/ppermute | solution.py:211
  6.2 10.5 %collective-permute-start.4 = (bf16[80,2,640]{2,1,0:T(2,128)(2,1)S(1)}, bf16[80,2,640]{2,1,0:T(2,128)(2,1)S(1)}, u32[]{:S(2)}, u32[]{:S(2)}) collective-permute-start(bf16[80,2,640]{2,1,0:T(2,128)(2,1)S(1)} %get-tuple-element.35._), channel_id=1, source_target_pairs={{4,0},{8,4},{12,8},{14,12},{10,14},{6,10},{2,6},{0,2},{1,5},{5,9},... | collective-permute-start | bytes 614408 | tf_op jit(solution)/shard_map/ppermute | solution.py:211
  9.6 11.3 %copy-start = (bf16[40,3,2560]{2,0,1:T(8,128)(2,1)S(1)}, bf16[40,3,2560]{2,0,1:T(8,128)(2,1)}, u32[]{:S(2)}) copy-start(bf16[40,3,2560]{2,0,1:T(8,128)(2,1)} %param.4) | copy-start | bytes 1843204
  9.6 9.0 %collective-permute-start.12 = (bf16[2,80,640]{2,1,0:T(8,128)(2,1)S(1)}, bf16[2,80,640]{2,1,0:T(8,128)(2,1)S(1)}, u32[]{:S(2)}, u32[]{:S(2)}) collective-permute-start(bf16[2,80,640]{2,1,0:T(8,128)(2,1)S(1)} %part.7.refs_1_), channel_id=1, source_target_pairs={{4,0},{8,4},{12,8},{14,12},{10,14},{6,10},{2,6},{0,2},{1,5},{5,9},... | collective-permute-start | bytes 614408 | tf_op jit(solution)/shard_map/ppermute | solution.py:211
  12.2 8.6 %collective-permute-start.2 = (bf16[2,80,640]{2,1,0:T(8,128)(2,1)S(1)}, bf16[2,80,640]{2,1,0:T(8,128)(2,1)S(1)}, u32[]{:S(2)}, u32[]{:S(2)}) collective-permute-start(bf16[2,80,640]{2,1,0:T(8,128)(2,1)S(1)} %part.4.refs_0_), channel_id=1, source_target_pairs={{0,4},{4,8},{8,12},{12,14},{14,10},{10,6},{6,2},{2,0},{5,1},{9,5},... | collective-permute-start | bytes 614408 | tf_op jit(solution)/shard_map/ppermute | solution.py:211
  16.4 4.4 %copy-start.1 = (f32[2560]{0:T(1024)S(1)}, f32[2560]{0:T(1024)}, u32[]{:S(2)}) copy-start(f32[2560]{0:T(1024)} %param.6) | copy-start | bytes 30724
  16.4 8.1 %collective-permute-start.9 = (bf16[2,80,640]{2,1,0:T(8,128)(2,1)S(1)}, bf16[2,80,640]{2,1,0:T(8,128)(2,1)S(1)}, u32[]{:S(2)}, u32[]{:S(2)}) collective-permute-start(bf16[2,80,640]{2,1,0:T(8,128)(2,1)S(1)} %part.6.refs_0_), channel_id=1, source_target_pairs={{0,4},{4,8},{8,12},{12,14},{14,10},{10,6},{6,2},{2,0},{5,1},{9,5},... | collective-permute-start | bytes 614408 | tf_op jit(solution)/shard_map/ppermute | solution.py:211
  16.8 4.0 %copy-start.2 = (f32[2560]{0:T(1024)S(1)}, f32[2560]{0:T(1024)}, u32[]{:S(2)}) copy-start(f32[2560]{0:T(1024)} %param.7) | copy-start | bytes 30724
  16.8 7.8 %collective-permute-start.5 = (bf16[2,80,640]{2,1,0:T(8,128)(2,1)S(1)}, bf16[2,80,640]{2,1,0:T(8,128)(2,1)S(1)}, u32[]{:S(2)}, u32[]{:S(2)}) collective-permute-start(bf16[2,80,640]{2,1,0:T(8,128)(2,1)S(1)} %part.5.refs_1_), channel_id=1, source_target_pairs={{4,0},{8,4},{12,8},{14,12},{10,14},{6,10},{2,6},{0,2},{1,5},{5,9},... | collective-permute-start | bytes 614408 | tf_op jit(solution)/shard_map/ppermute | solution.py:211
  18.6 10.3 %collective-permute-start.13 = (bf16[2,80,640]{2,1,0:T(8,128)(2,1)S(1)}, bf16[2,80,640]{2,1,0:T(8,128)(2,1)S(1)}, u32[]{:S(2)}, u32[]{:S(2)}) collective-permute-start(bf16[2,80,640]{2,1,0:T(8,128)(2,1)S(1)} %collective-permute-done.12.refs_1_), channel_id=1, source_target_pairs={{4,0},{8,4},{12,8},{14,12},{10,14},{6,10},{2,6},{0,2},{1,5},{5,9},... | collective-permute-start | bytes 614408 | tf_op jit(solution)/shard_map/ppermute | solution.py:211
  20.8 9.8 %collective-permute-start.3 = (bf16[2,80,640]{2,1,0:T(8,128)(2,1)S(1)}, bf16[2,80,640]{2,1,0:T(8,128)(2,1)S(1)}, u32[]{:S(2)}, u32[]{:S(2)}) collective-permute-start(bf16[2,80,640]{2,1,0:T(8,128)(2,1)S(1)} %collective-permute-done.2.refs_0_), channel_id=1, source_target_pairs={{0,4},{4,8},{8,12},{12,14},{14,10},{10,6},{6,2},{2,0},{5,1},{9,5},... | collective-permute-start | bytes 614408 | tf_op jit(solution)/shard_map/ppermute | solution.py:211
  21.2 10.0 %collective-permute-start = (bf16[3,40,1280]{2,1,0:T(8,128)(2,1)S(1)}, bf16[3,40,1280]{2,1,0:T(8,128)(2,1)S(1)}, u32[]{:S(2)}, u32[]{:S(2)}) collective-permute-start(bf16[3,40,1280]{2,1,0:T(8,128)(2,1)S(1)} %get-tuple-element.38), channel_id=1, source_target_pairs={{0,1},{1,0},{2,3},{3,2},{4,5},{5,4},{6,7},{7,6},{8,9},{9,8},{10,11... | collective-permute-start | bytes 921608 | tf_op jit(solution)/shard_map/ppermute | solution.py:236
  24.5 9.3 %collective-permute-start.10 = (bf16[2,80,640]{2,1,0:T(8,128)(2,1)S(1)}, bf16[2,80,640]{2,1,0:T(8,128)(2,1)S(1)}, u32[]{:S(2)}, u32[]{:S(2)}) collective-permute-start(bf16[2,80,640]{2,1,0:T(8,128)(2,1)S(1)} %collective-permute-done.9.refs_0_), channel_id=1, source_target_pairs={{0,4},{4,8},{8,12},{12,14},{14,10},{10,6},{6,2},{2,0},{5,1},{9,5},... | collective-permute-start | bytes 614408 | tf_op jit(solution)/shard_map/ppermute | solution.py:211
  24.6 9.7 %collective-permute-start.6 = (bf16[2,80,640]{2,1,0:T(8,128)(2,1)S(1)}, bf16[2,80,640]{2,1,0:T(8,128)(2,1)S(1)}, u32[]{:S(2)}, u32[]{:S(2)}) collective-permute-start(bf16[2,80,640]{2,1,0:T(8,128)(2,1)S(1)} %collective-permute-done.5.refs_1_), channel_id=1, source_target_pairs={{4,0},{8,4},{12,8},{14,12},{10,14},{6,10},{2,6},{0,2},{1,5},{5,9},... | collective-permute-start | bytes 614408 | tf_op jit(solution)/shard_map/ppermute | solution.py:211
  29.0 7.4 %collective-permute-start.14 = (bf16[2,80,640]{2,1,0:T(8,128)(2,1)S(1)}, bf16[2,80,640]{2,1,0:T(8,128)(2,1)S(1)}, u32[]{:S(2)}, u32[]{:S(2)}) collective-permute-start(bf16[2,80,640]{2,1,0:T(8,128)(2,1)S(1)} %collective-permute-done.13.refs_1_), channel_id=1, source_target_pairs={{4,0},{8,4},{12,8},{14,12},{10,14},{6,10},{2,6},{0,2},{1,5},{5,9},... | collective-permute-start | bytes 614408 | tf_op jit(solution)/shard_map/ppermute | solution.py:211
  30.6 5.8 %collective-permute-start.7 = (bf16[2,80,640]{2,1,0:T(8,128)(2,1)S(1)}, bf16[2,80,640]{2,1,0:T(8,128)(2,1)S(1)}, u32[]{:S(2)}, u32[]{:S(2)}) collective-permute-start(bf16[2,80,640]{2,1,0:T(8,128)(2,1)S(1)} %collective-permute-done.3.refs_0_), channel_id=1, source_target_pairs={{0,4},{4,8},{8,12},{12,14},{14,10},{10,6},{6,2},{2,0},{5,1},{9,5},... | collective-permute-start | bytes 614408 | tf_op jit(solution)/shard_map/ppermute | solution.py:211
  36.9 1.4 %collective-permute-start.15 = (bf16[40,1280]{1,0:T(8,128)(2,1)S(1)}, bf16[40,1280]{1,0:T(8,128)(2,1)S(1)}, u32[]{:S(2)}, u32[]{:S(2)}) collective-permute-start(bf16[40,1280]{1,0:T(8,128)(2,1)S(1)} %send.1), channel_id=1, source_target_pairs={{0,1},{1,0},{2,3},{3,2},{4,5},{5,4},{6,7},{7,6},{8,9},{9,8},{10,11... | collective-permute-start | bytes 307208 | tf_op jit(solution)/shard_map/ppermute | solution.py:254
